TPU v7x, 32 devices: a whole 2x2x4 slice. The times are simulated.
32 devices in a mesh: cfg: 2 (over y), group: 4 (over x, core), mp: 4 (over z).
Axes of the slice: x: 2, y: 2, z: 4, core: 2. Of those that a mesh axis runs over, the one named last changes fastest.
Arguments:
- latents: float32 [4096, 64], P(('group', 'mp')), may hold values from -0.6 to 0.6
- text_hidden: bfloat16 [2, 2048, 3072], P('cfg', ('group', 'mp')), may hold values from -6 to 6
- w_img_in: bfloat16 [64, 3072], replicated, may hold values from -0.75 to 0.75
- w_img_qkv: bfloat16 [3072, 4608], P(None, 'mp'), may hold values from -1 to 1
- w_txt_kv: bfloat16 [3072, 3072], P(None, 'mp'), may hold values from -0.109375 to 0.109375
- q_gain: float32 [128], replicated, may hold values from 0.25 to 1.75
- k_gain: float32 [128], replicated, may hold values from 0.25 to 1.75
- w_out: bfloat16 [1536, 3072], replicated, may hold values from -1 to 1
- w_final: bfloat16 [3072, 64], replicated, may hold values from -0.109375 to 0.109375
- mod_img: float32 [8, 3, 3072], replicated, may hold values from -3 to 3
- mod_txt: float32 [8, 2, 3072], replicated, may hold values from -3 to 3
- mod_final: float32 [8, 2, 3072], replicated, may hold values from -3 to 3
- guide: float32 [4], replicated, may hold values from 1.5 to 5
- step_size: float32 [8], replicated, may hold values from 0.02 to 0.3
- img_len: int32 [4], replicated, may hold values from 1 to 1024, as said below
- txt_len: int32 [4], replicated, may hold values from 1 to 512, as said below
- split_flag: int32 [2, 4], replicated, may hold values from 0 to 1, as said below
- tstep: int32 [4], replicated, may hold values from 0 to 7
Outputs:
- velocity: float32 [2, 2048, 64], P('cfg', ('group', 'mp'))
- next_latents: float32 [2, 2048, 64], P('cfg', ('group', 'mp'))
Inputs may be any that keep to these rules, and one draw needn't show every extreme that they name: `img_len`: some group has exactly 1024 live image tokens. `txt_len`: some group has exactly 512 live text tokens. `split_flag`: entries [c, 2j] and [c, 2j + 1] are equal; at least one such pair carries 1 and at least one carries 0.
All inputs are finite; a program needn't handle non-finite values.
Results may differ from a plain program's by a relative error of at most 0.035.
Values may be sent and summed in bfloat16 or wider, within the bound.
No kernel may reach another device: no remote copies, remote signals or barrier semaphores. Data moves between devices by JAX's collectives and lax.ppermute only.
A program may use at most 192 MiB of HBM per device.

v0:
```python
import jax
import jax.numpy as jnp
from jax import lax
from jax.sharding import PartitionSpec as P

HD = 128


def partner(value, axis, bit):
    mask = 2**bit
    pairs = [(source, source ^ mask) for source in range(lax.axis_size(axis))]
    return lax.ppermute(value, axis, pairs)


def layer_norm(values):
    center = values - jnp.mean(values, -1, keepdims=True)
    spread = jnp.mean(center * center, -1, keepdims=True)
    return center * lax.rsqrt(spread + 1e-06)


def head_norm(values, gain):
    return values * lax.rsqrt(jnp.mean(values * values, -1, keepdims=True) + 1e-06) * gain


def pick_entry(table, index):
    return lax.dynamic_index_in_dim(table, index, 0, keepdims=False)


def local(
    latents,
    text_hidden,
    w_img_in,
    w_img_qkv,
    w_txt_kv,
    q_gain,
    k_gain,
    w_out,
    w_final,
    mod_img,
    mod_txt,
    mod_final,
    guide,
    step_size,
    img_len,
    txt_len,
    split_flag,
    tstep,
):
    group_index = lax.axis_index("group")
    mp_index = lax.axis_index("mp")
    cfg_index = lax.axis_index("cfg")
    mp_count = lax.axis_size("mp")
    mate_index = jnp.bitwise_xor(group_index, 1)
    step_index = pick_entry(tstep, group_index)
    mod_rows = pick_entry(mod_img, step_index)
    text_rows = pick_entry(mod_txt, step_index)
    final_rows = pick_entry(mod_final, step_index)
    shard_rows = latents.shape[0]
    half_rows = shard_rows // 2
    full_img = shard_rows * mp_count
    full_txt = text_hidden.shape[1] * mp_count
    local_heads = w_img_qkv.shape[1] // (3 * HD)
    x_img = jnp.dot(latents.astype(jnp.bfloat16), w_img_in, preferred_element_type=jnp.float32)
    img_mod = (layer_norm(x_img) * (1.0 + mod_rows[1]) + mod_rows[0]).astype(jnp.bfloat16)
    txt_mod = (
        layer_norm(text_hidden[0].astype(jnp.float32)) * (1.0 + text_rows[1]) + text_rows[0]
    ).astype(jnp.bfloat16)
    img_full, txt_full = (
        lax.all_gather(img_mod, "mp", axis=0, tiled=True),
        lax.all_gather(txt_mod, "mp", axis=0, tiled=True),
    )
    qkv = jnp.dot(img_full, w_img_qkv, preferred_element_type=jnp.float32).reshape(
        full_img, local_heads, 3, HD
    )
    query = head_norm(qkv[:, :, 0], q_gain).astype(jnp.bfloat16)
    key_img = head_norm(qkv[:, :, 1], k_gain).astype(jnp.bfloat16)
    value_img = qkv[:, :, 2].astype(jnp.bfloat16)
    text_kv = jnp.dot(txt_full, w_txt_kv, preferred_element_type=jnp.float32).reshape(
        full_txt, local_heads, 2, HD
    )
    key_txt = head_norm(text_kv[:, :, 0], k_gain).astype(jnp.bfloat16)
    value_txt = text_kv[:, :, 1].astype(jnp.bfloat16)
    key_rows = jnp.concatenate([key_txt, key_img], axis=0)
    value_rows = jnp.concatenate([value_txt, value_img], axis=0)
    mate_keys, mate_values = partner((key_rows, value_rows), "group", 0)
    spots_txt = jnp.arange(full_txt, dtype=jnp.int32)
    spots_img = jnp.arange(full_img, dtype=jnp.int32)

    def live_rows(index):
        return jnp.concatenate(
            [spots_txt < pick_entry(txt_len, index), spots_img < pick_entry(img_len, index)]
        )

    flagged = pick_entry(pick_entry(split_flag, cfg_index), group_index) == 1
    live = jnp.concatenate([live_rows(group_index), live_rows(mate_index) & flagged])
    all_keys = jnp.concatenate([key_rows, mate_keys], axis=0)
    all_values = jnp.concatenate([value_rows, mate_values], axis=0)
    scores = jnp.einsum(
        "qhe,khe->hqk", query, all_keys, preferred_element_type=jnp.float32
    ) * HD ** (-0.5)
    scores = jnp.where(live[None, None, :], scores, -1e30)
    weights = jnp.exp(scores - jnp.max(scores, -1, keepdims=True))
    probs = (weights / jnp.sum(weights, -1, keepdims=True)).astype(jnp.bfloat16)
    mixed = jnp.einsum(
        "hqk,khe->qhe", probs, all_values, preferred_element_type=jnp.float32
    ).astype(jnp.bfloat16)
    mixed = mixed.reshape(full_img, local_heads * HD)
    w_local = lax.dynamic_slice_in_dim(w_out, mp_index * local_heads * HD, local_heads * HD, 0)
    attended = lax.psum_scatter(
        jnp.dot(mixed, w_local, preferred_element_type=jnp.float32),
        "mp",
        scatter_dimension=0,
        tiled=True,
    )
    hidden = x_img + mod_rows[2] * attended
    final = (layer_norm(hidden) * (1.0 + final_rows[1]) + final_rows[0]).astype(jnp.bfloat16)
    own_velocity = jnp.dot(final, w_final, preferred_element_type=jnp.float32)
    scale = pick_entry(guide, group_index)
    other_velocity = partner(own_velocity.astype(jnp.bfloat16), "cfg", 0).astype(own_velocity.dtype)
    is_cond = cfg_index == 0
    cond_part = jnp.where(is_cond, own_velocity, other_velocity)
    uncond_part = jnp.where(is_cond, other_velocity, own_velocity)
    guided_all = uncond_part + scale * (cond_part - uncond_part)
    guided = lax.dynamic_slice_in_dim(guided_all, cfg_index * half_rows, half_rows, 0)
    row_place = (
        mp_index * shard_rows + cfg_index * half_rows + jnp.arange(half_rows, dtype=jnp.int32)
    )
    row_live = row_place < pick_entry(img_len, group_index)
    guided = jnp.where(row_live[:, None], guided, 0.0)
    start_rows = lax.dynamic_slice_in_dim(latents, cfg_index * half_rows, half_rows, 0)
    moved = start_rows - pick_entry(step_size, step_index) * guided
    return (guided[None], moved[None])


def solution(mesh):
    placed = (
        P(("group", "mp"), None),
        P("cfg", ("group", "mp"), None),
        P(),
        P(None, "mp"),
        P(None, "mp"),
        P(),
        P(),
        P(),
        P(),
        P(),
        P(),
        P(),
        P(),
        P(),
        P(),
        P(),
        P(),
        P(),
    )
    return jax.shard_map(
        local,
        mesh=mesh,
        in_specs=placed,
        out_specs=(P("cfg", ("group", "mp"), None), P("cfg", ("group", "mp"), None)),
        check_vma=False,
    )
```

profile of v0, /device:TPU:0, one launch (start us, length us, event | category | flops | bytes accessed | tf_op | source)
XLA Modules:
  0.0 507.8 jit_solution(14190769731366580914)
XLA Ops:
  7.2 1.3 dynamic_slice.51
  9.8 1.3 convert_reduce_fusion
  11.1 1.5 fusion.18
  14.3 2.4 fusion.21
  16.8 1.5 fusion.50
  18.8 1.6 constant_dynamic-slice_fusion
  20.3 1.8 add_convert_fusion.1
  25.1 58.0 %all-gather.3.cloned.1.call-done = bf16[512,3072]{1,0:T(8,128)(2,1)} async-done(((bf16[128,3072]{1,0:T(8,128)(2,1)}), bf16[512,3072]{1,0:T(8,128)(2,1)}) %all-gather.3.cloned.1.call-update) | async-done | bytes 3145744 | tf_op jit(solution)/shard_map/all_gather | solution.py:70
  83.1 7.0 %fusion.53 = f32[512,768]{1,0:T(8,128)} fusion(bf16[512,3072]{1,0:T(8,128)(2,1)} %all-gather.3.cloned.1.call-done, bf16[3072,768]{1,0:T(8,128)(2,1)} %param.22), kind=kOutput, calls=%fused_computation.97 | convolution fusion | flops 2415919104 | bytes 9437184 | tf_op jit(solution)/shard_map/dot_general | solution.py:78
  90.1 3.1 reshape.125
  93.2 2.1 slice.60
  95.9 102.8 %all-gather.5.cloned.1.call-done = bf16[1024,3072]{1,0:T(8,128)(2,1)} async-done(((bf16[256,3072]{1,0:T(8,128)(2,1)}), bf16[1024,3072]{1,0:T(8,128)(2,1)}) %all-gather.5.cloned.1.call-update) | async-done | bytes 6291472 | tf_op jit(solution)/shard_map/all_gather | solution.py:69
  198.7 11.3 %fusion.54 = f32[1024,1152]{0,1:T(8,128)S(1)} fusion(bf16[1024,3072]{1,0:T(8,128)(2,1)} %all-gather.5.cloned.1.call-done, bf16[3072,1152]{1,0:T(8,128)(2,1)} %param.21), kind=kOutput, calls=%fused_computation.98 | convolution fusion | flops 7247757312 | bytes 18087936 | tf_op jit(solution)/shard_map/dot_general | solution.py:72
  210.0 2.1 copy-done.2
  212.1 1.3 slice.61
  213.4 3.0 copy.40
  216.4 1.9 fusion.22
  218.3 1.9 fusion.24
  222.9 1.3 dynamic_slice.57
  225.5 3.1 slice.57
  228.6 2.9 copy.41
  231.5 1.5 fusion.30
  233.9 2.1 pad_maximum_fusion.1
  236.4 1.6 multiply_reduce_fusion.2
  238.0 19.8 %fusion.51 = (f32[3,1024]{1,0:T(4,128)}, f32[3,1024,3072]{2,1,0:T(8,128)}) fusion(pred[3072]{0:T(1024)(128)(4,1)} %pad_add_fusion, bf16[1536,3,128]{2,0,1:T(8,128)(2,1)} %collective-permute-done.1, bf16[1024,3,128]{2,0,1:T(8,128)(2,1)} %copy-done.4, bf16[512,3,128]{2,0,1:T(8,128)(2,1)S(1)} %multiply_convert_fusion.1, f32[1024,3,3,128]{0,3,2,1:T(8,128)} %bitcast.91, ...), kind=kOutput, calls=%fused_computation.95 | convolution fusion | flops 2461928448 | bytes 41709056 | tf_op jit(solution)/shard_map/sub | solution.py:102
  257.9 15.0 %fusion.26 = bf16[3,128,1024]{2,1,0:T(8,128)(2,1)S(1)} fusion(f32[3,1024,3072]{2,1,0:T(8,128)} %get-tuple-element.19, f32[3,1024]{1,0:T(4,128)} %get-tuple-element.18, bf16[1536,3,128]{0,2,1:T(8,128)(2,1)} %collective-permute-done, bf16[1024,3,128]{0,2,1:T(8,128)(2,1)} %copy-done.3, bf16[512,3,128]{0,2,1:T(8,128)(2,1)} %bitcast.93), kind=kOutput, calls=%fused_computation.42 | convolution fusion | flops 2442264576 | bytes 40906752 | tf_op jit(solution)/shard_map/hqk,khe->qhe/dot_general | solution.py:104
  272.9 8.1 %fusion.13 = f32[1024,3072]{1,0:T(8,128)} fusion(bf16[1024,384]{0,1:T(8,128)(2,1)S(1)} %bitcast.94, bf16[1536,3072]{1,0:T(8,128)(2,1)} %param.25, s32[]{:T(128)S(6)} %select_n.66), kind=kOutput, calls=%fused_computation.21 | convolution fusion | flops 2415919104 | bytes 15728644 | tf_op jit(solution)/shard_map/dot_general | solution.py:110
  281.0 1.4 dynamic-slice_add_fusion
  282.5 208.8 %reduce-scatter.2.cloned.1.call-done = f32[256,3072]{1,0:T(8,128)} async-done(((f32[1024,3072]{1,0:T(8,128)}), f32[256,3072]{1,0:T(8,128)}) %reduce-scatter.2.cloned.1.call-update) | async-done | bytes 3145744 | tf_op jit(solution)/shard_map/reduce_scatter | solution.py:109
  491.2 2.3 fusion.47
  495.4 1.5 collective-permute-start.2
  499.4 1.9 subtract_bitcast_fusion
  (64 shorter events, 13.9 us)
Async XLA Ops:
  7.2 9.6 %copy-start = (bf16[64,3072]{1,0:T(8,128)(2,1)S(1)}, bf16[64,3072]{1,0:T(8,128)(2,1)}, u32[]{:S(2)}) copy-start(bf16[64,3072]{1,0:T(8,128)(2,1)} %param.20) | copy-start | bytes 1179652
  7.2 75.9 %all-gather.3.cloned.1.call-start = ((), (), s32[]{:S(2)}) async-start(), calls=%async_computation.1 | async-start | bytes 3932160 | tf_op jit(solution)/shard_map/all_gather | solution.py:70
  16.7 182.0 %all-gather.5.cloned.1.call-start = ((), (), s32[]{:S(2)}) async-start(), calls=%async_computation.2 | async-start | bytes 7864320 | tf_op jit(solution)/shard_map/all_gather | solution.py:69
  20.3 2.1 copy-start.8
  20.3 2.1 copy-start.9
  22.2 469.0 %reduce-scatter.2.cloned.1.call-start = ((), (), s32[]{:S(2)}) async-start(), calls=%async_computation.3 | async-start | bytes 15728640 | tf_op jit(solution)/shard_map/reduce_scatter | solution.py:109
  90.1 5.5 %copy-start.10 = (f32[128]{0:T(128)S(1)}, f32[128]{0:T(128)}, u32[]{:S(2)}) copy-start(f32[128]{0:T(128)} %param.24) | copy-start | bytes 1540
  210.0 2.2 copy-start.2
  220.2 0.9 copy-start.4
  222.2 15.8 %collective-permute-start.1 = (bf16[1536,3,128]{2,0,1:T(8,128)(2,1)}, bf16[1536,3,128]{2,0,1:T(8,128)(2,1)}, u32[]{:S(2)}, u32[]{:S(2)}) collective-permute-start(bf16[1536,3,128]{2,0,1:T(8,128)(2,1)} %pad_maximum_fusion.2), channel_id=1, source_target_pairs={{0,4},{4,0},{8,12},{12,8},{1,5},{5,1},{9,13},{13,9},{2,6},{6,2},{1... | collective-permute-start | bytes 3538952 | tf_op jit(solution)/shard_map/ppermute | solution.py:12
  233.0 0.9 copy-start.3
  236.0 21.9 %collective-permute-start = (bf16[1536,3,128]{0,2,1:T(8,128)(2,1)}, bf16[1536,3,128]{0,2,1:T(8,128)(2,1)}, u32[]{:S(2)}, u32[]{:S(2)}) collective-permute-start(bf16[1536,3,128]{0,2,1:T(8,128)(2,1)} %pad_maximum_fusion.1), channel_id=1, source_target_pairs={{0,4},{4,0},{8,12},{12,8},{1,5},{5,1},{9,13},{13,9},{2,6},{6,2},{1... | collective-permute-start | bytes 3538952 | tf_op jit(solution)/shard_map/ppermute | solution.py:12
  281.0 210.3 %copy-start.6 = (f32[1,1,3072]{2,0,1:T(1,128)S(1)}, f32[1,1,3072]{2,0,1:T(1,128)}, u32[]{:S(2)}) copy-start(f32[1,1,3072]{2,0,1:T(1,128)} %get-tuple-element.4) | copy-start | bytes 36868
  493.6 0.7 copy-start.7
  493.6 1.1 copy-start.11
  493.6 7.7 %copy-start.1 = (bf16[64,3072]{1,0:T(8,128)(2,1)S(1)}, bf16[64,3072]{1,0:T(8,128)(2,1)}, u32[]{:S(2)}) copy-start(bf16[64,3072]{1,0:T(8,128)(2,1)} %param.20) | copy-start | bytes 1179652
  493.6 4.0 copy-start.12
  493.6 4.7 copy-start.13
  493.6 5.8 %copy-start.5 = (f32[256,64]{0,1:T(8,128)S(1)}, f32[256,64]{0,1:T(8,128)}, u32[]{:S(2)}) copy-start(f32[256,64]{0,1:T(8,128)} %param.18) | copy-start | bytes 196612
  495.4 4.0 collective-permute-start.2
Sparse Core Ops, SparseCore 0:
  16.8 66.1 all-gather.2
  84.6 113.9 all-gather.4
  281.1 210.0 reduce-scatter.1
where the time goes:
time: 509 us; the launch traced here: 508 us
  waiting for transfers between devices  370 us (73%)
  matrix products  63.5 us (12%)
  other arithmetic  27.7 us (5%)
  local copies, waits for them, and re-layouts  27.5 us (5%)
  between operations  16.7 us (3%)
    reduce_scatter x1, waiting for transfers between devices, local(): lax.psum_scatter(jnp.dot(mixed, w_local, preferred_element_type=jnp.float...  209 us
    all_gather x1, waiting for transfers between devices, local(): lax.all_gather(img_mod, 'mp', axis=0, tiled=True)  103 us
    all_gather x1, waiting for transfers between devices, local(): lax.all_gather(txt_mod, 'mp', axis=0, tiled=True)  58 us
    sub x1, matrix products, local(): weights = jnp.exp(scores - jnp.max(scores, -1, keepdims=True))  19.8 us
    dot_general x1, matrix products, local(): jnp.einsum('hqk,khe->qhe', probs, all_values, preferred_element_type=jnp....  15 us
    dot_general x1, matrix products, local(): jnp.dot(img_full, w_img_qkv, preferred_element_type=jnp.float32)  11.3 us
    unnamed x30, local copies, waits for them, and re-layouts  10.4 us
  transfers between devices with their start and end apart: 6, of which 4 were waited for; matrix products, arithmetic and copies ran while one was open for 11% of the time, Pallas kernels for 0%

commit v1 on v0

v1 whole, which is shorter than its diff:
```python
import functools

import jax
import jax.numpy as jnp
import numpy as np
from jax import lax
from jax.experimental import pallas as pl
from jax.experimental.pallas import tpu as pltpu
from jax.sharding import PartitionSpec as P

HD = 128
EPS = 1e-6
BF = jnp.bfloat16
F32 = jnp.float32
QSCALE = float(HD**-0.5 / np.log(2.0))
VLIM = 32 * 2**20


def ring(value, step):
    n = lax.axis_size("mp")
    return lax.ppermute(value, "mp", [(i, (i + step) % n) for i in range(n)])


def partner(value, axis):
    n = lax.axis_size(axis)
    return lax.ppermute(value, axis, [(i, i ^ 1) for i in range(n)])


def split2(value):
    high = value.astype(BF)
    return high, (value - high.astype(F32)).astype(BF)


def dot(a, b):
    return jnp.dot(a, b, preferred_element_type=F32)


def dot_t(a, b):
    return lax.dot_general(a, b, (((1,), (1,)), ((), ())), preferred_element_type=F32)


def call(body, name, scalars, grid, in_specs, out_specs, out_shape, scratch, args, flops, nbytes):
    return pl.pallas_call(
        body,
        name=name,
        grid_spec=pltpu.PrefetchScalarGridSpec(
            num_scalar_prefetch=len(scalars),
            grid=grid,
            in_specs=in_specs,
            out_specs=out_specs,
            scratch_shapes=scratch,
        ),
        out_shape=out_shape,
        compiler_params=pltpu.CompilerParams(vmem_limit_bytes=VLIM),
        cost_estimate=pl.CostEstimate(flops=flops, bytes_accessed=nbytes, transcendentals=0),
    )(*scalars, *args)


def whole(shape):
    return pl.BlockSpec(shape, lambda *_: (0,) * len(shape))


def prep_body(*refs):
    *lat_refs, win_ref, out_ref = refs
    for i, ref in enumerate(lat_refs):
        rows = ref[...].T.astype(BF)
        n = rows.shape[0]
        x = dot(rows, win_ref[...])
        center = x - jnp.mean(x, -1, keepdims=True)
        rstd = lax.rsqrt(jnp.mean(center * center, -1, keepdims=True) + EPS)
        high, low = split2(rows.astype(F32) * rstd)
        out_ref[i * n : (i + 1) * n, :] = jnp.concatenate([high, low], axis=1)


def fold_body(ids, tstep, win_ref, mod_ref, w_ref, mats_ref, shift_ref, rows_ref):
    ch, d = win_ref.shape

    @pl.when(pl.program_id(0) == 0)
    def _():
        values = win_ref[...].astype(F32)
        center = values - jnp.mean(values, -1, keepdims=True)
        spot = lax.broadcasted_iota(jnp.int32, (16, d), 0)
        tail = jnp.zeros((16, d), F32)
        for i in range(2):
            at = pl.ds(tstep[ids[1] ^ i], 1)
            high, low = split2(center * (1.0 + mod_ref[1, at, :]))
            rows_ref[2 * i * ch : (2 * i + 1) * ch, :] = high
            rows_ref[(2 * i + 1) * ch : (2 * i + 2) * ch, :] = low
            high, low = split2(mod_ref[0, at, :])
            tail = jnp.where(spot == 2 * i, high.astype(F32), tail)
            tail = jnp.where(spot == 2 * i + 1, low.astype(F32), tail)
        rows_ref[4 * ch :, :] = tail.astype(BF)

    out = dot(rows_ref[...], w_ref[...])
    for i in range(2):
        high, low = split2(out[2 * i * ch : (2 * i + 1) * ch] + out[(2 * i + 1) * ch : (2 * i + 2) * ch])
        mats_ref[i] = jnp.concatenate([high, high, low], axis=0)
        base = 4 * ch + 2 * i
        shift_ref[i] = jnp.broadcast_to(out[base : base + 1] + out[base + 1 : base + 2], shift_ref.shape[1:])


def live_mask(first, rows, length):
    return (lax.broadcasted_iota(jnp.int32, (rows, HD), 0) + first) < length


def fill_ones(ref):
    head = [lax.broadcasted_iota(jnp.int32, ref.shape, i) // HD for i in range(2)]
    ref[...] = (head[0] == head[1]).astype(BF)


def head_norm(values, ones, gain):
    square = dot((values * values).astype(BF), ones)
    return values * lax.rsqrt(square * (1.0 / HD) + EPS) * gain


def image_body(kb, n_mp, ids, img_len, flags, own_ref, mate_ref, mats_ref, shift_ref, qg_ref, kg_ref,
               q_ref, acc_ref, k_ref, v_ref, x_ref, ones_ref):
    group = ids[1]
    n_rows = own_ref.shape[0]
    shard = n_rows // n_mp
    half = HD // 2
    length = img_len[group]
    mate_length = jnp.where(flags[ids[0], group] == 1, img_len[group ^ 1], 0)

    @pl.when(pl.program_id(0) == 0)
    def _():
        fill_ones(ones_ref)
        for base, ref, most in ((0, own_ref, length), (n_rows, mate_ref, mate_length)):
            for s in range(n_mp):
                start = pl.multiple_of(lax.rem(ids[2] + n_mp - s, n_mp) * shard, shard)
                lat = ref[s * shard : (s + 1) * shard, :]
                x_ref[pl.ds(base + start, shard), :] = jnp.concatenate(
                    [lat, lat[:, :half], jnp.zeros((shard, half), BF)], axis=1
                )
            v_ref[base : base + n_rows, HD:] = live_mask(0, n_rows, most).astype(BF)

    zeros = jnp.zeros((half, 3 * HD), BF)
    own_mat = jnp.concatenate([mats_ref[0], zeros], axis=0)
    block = dot(x_ref[:n_rows, :], own_mat) + shift_ref[0, 0:1, :]
    gains = jnp.concatenate([qg_ref[...] * QSCALE, kg_ref[...]], axis=1)
    normed = head_norm(block[:, : 2 * HD], ones_ref[...], gains).astype(BF)
    q_ref[0] = normed[:, :HD]
    k_ref[:n_rows, :] = normed[:, HD:]
    v_ref[:n_rows, :HD] = jnp.where(live_mask(0, n_rows, length), block[:, 2 * HD :], 0.0).astype(BF)

    @pl.when(mate_length > 0)
    def _():
        mate_mat = jnp.concatenate([mats_ref[1], zeros], axis=0)[:, HD:]
        block = dot(x_ref[n_rows:, :], mate_mat) + shift_ref[1, 0:1, HD:]
        k_ref[n_rows:, :] = head_norm(block[:, :HD], ones_ref[:HD, :HD], kg_ref[...]).astype(BF)
        v_ref[n_rows:, :HD] = jnp.where(
            live_mask(0, n_rows, mate_length), block[:, HD:], 0.0
        ).astype(BF)

    def attend(start):
        spot = pl.ds(start, kb)
        p = jnp.exp2(dot_t(q_ref[0], k_ref[spot, :])).astype(BF)
        return dot(p, v_ref[spot, :])

    acc_ref[0] = attend(0)
    for start in range(kb, 2 * n_rows, kb):
        seen = length > start if start < n_rows else mate_length > start - n_rows

        @pl.when(seen)
        def _():
            acc_ref[0] += attend(start)


def text_body(n_in, ids, tstep, *refs):
    rows_refs, (mod_ref, w_ref, kg_ref, out_ref, ones_ref) = refs[:n_in], refs[n_in:]
    fill_ones(ones_ref)
    first = 0
    for ref in rows_refs:
        n = ref.shape[0]
        x = ref[...].astype(F32)
        center = x - jnp.mean(x, -1, keepdims=True)
        rstd = lax.rsqrt(jnp.mean(center * center, -1, keepdims=True) + EPS)
        y = (center * rstd * (1.0 + mod_ref[0, 1:2, :]) + mod_ref[0, 0:1, :]).astype(BF)
        for h in range(out_ref.shape[0]):
            kv = dot(y, w_ref[:, 2 * HD * h : 2 * HD * (h + 1)])
            out_ref[h, first : first + n, :HD] = head_norm(kv[:, :HD], ones_ref[...], kg_ref[...]).astype(BF)
            out_ref[h, first : first + n, HD:] = kv[:, HD:].astype(BF)
        first += n


def text_attend(offsets, shard, n_mp, ids, txt_len, flags, q, acc, own, mate):
    side, group, m = ids[0], ids[1], ids[2]
    length = txt_len[group]
    mate_length = jnp.where(flags[side, group] == 1, txt_len[group ^ 1], 0)
    keys, values = [], []
    for kv, most in ((own, length), (mate, mate_length)):
        keys.append(kv[:, :HD])
        for i, off in enumerate(offsets):
            live = live_mask(lax.rem(m + off, n_mp) * shard, shard, most)
            v = kv[i * shard : (i + 1) * shard, HD:]
            values.append(
                jnp.concatenate([jnp.where(live, v, jnp.zeros_like(v)), live.astype(BF)], axis=1)
            )
    p = jnp.exp2(dot_t(q, jnp.concatenate(keys, axis=0))).astype(BF)
    return acc + dot(p, jnp.concatenate(values, axis=0))


def near_body(offsets, shard, n_mp, ids, txt_len, flags, q_ref, acc_ref, own0, mate0, own1, mate1, out_ref):
    own = jnp.concatenate([own0[0], own1[0]], axis=0)
    mate = jnp.concatenate([mate0[0], mate1[0]], axis=0)
    out_ref[0] = text_attend(offsets, shard, n_mp, ids, txt_len, flags, q_ref[0], acc_ref[0], own, mate)


def last_body(offsets, shard, n_mp, ids, txt_len, flags, q_ref, acc_ref, own_ref, mate_ref, *out_refs):
    step = pl.program_id(0)
    half = q_ref.shape[1] // 2
    is_cond = ids[0] == 0
    parts = []
    for h in range(q_ref.shape[0]):
        acc = text_attend(
            offsets, shard, n_mp, ids, txt_len, flags, q_ref[h], acc_ref[h], own_ref[h], mate_ref[h]
        )
        parts.append((acc[:, :HD] / acc[:, HD:]).astype(BF))
    mixed = jnp.concatenate(parts, axis=1)
    low, high = mixed[:half], mixed[half:]
    for i in range(n_mp):

        @pl.when(step == i)
        def _():
            out_refs[2 * i][...] = jnp.where(is_cond, low, high)
            out_refs[2 * i + 1][...] = jnp.where(is_cond, high, low)


def stage_body(n_mp, ids, w_ref, lat_ref, win_ref, rest_ref, x_ref):
    rest_ref[0] = w_ref[0]

    @pl.when(pl.program_id(0) == 0)
    def _():
        half = x_ref.shape[0]
        lat = jnp.where(ids[0] == 0, lat_ref[:, :half], lat_ref[:, half:])
        x_ref[...] = dot(lat.T.astype(BF), win_ref[...])


def project_sides(pieces, weights):
    total = None
    for i, w in enumerate(weights):
        rows = jnp.concatenate([pieces[2 * i][...], pieces[2 * i + 1][...]], axis=0)
        term = dot(rows, w)
        total = term if total is None else total + term
    return total


def early_body(*refs):
    n = (len(refs) - 1) // 3
    refs[-1][...] = project_sides(refs[: 2 * n], [ref[0] for ref in refs[2 * n : -1]])


def out_body(ids, tstep, img_len, guide, step_size, *refs):
    pieces, refs = refs[:2], refs[2:]
    wout_ref, total_ref, x_ref, lat_ref, mod_ref, final_ref, wf_ref, vel_ref, next_ref = refs
    side, group, m = ids[0], ids[1], ids[2]
    step = tstep[group]
    total = total_ref[...] + project_sides(pieces, [wout_ref[0]])
    x = x_ref[...]
    hidden = jnp.concatenate([x, x], axis=0) + mod_ref[2, pl.ds(step, 1), :] * total
    center = hidden - jnp.mean(hidden, -1, keepdims=True)
    rstd = lax.rsqrt(jnp.mean(center * center, -1, keepdims=True) + EPS)
    final = (center * rstd * (1.0 + final_ref[0, 1:2, :]) + final_ref[0, 0:1, :]).astype(BF)
    vel = dot_t(wf_ref[...], final)
    half = x.shape[0]
    own, other = vel[:, :half], vel[:, half:]
    is_cond = side == 0
    cond = jnp.where(is_cond, own, other)
    uncond = jnp.where(is_cond, other, own)
    guided = uncond + guide[group] * (cond - uncond)
    place = lax.broadcasted_iota(jnp.int32, guided.shape, 1) + (2 * m + side) * half
    guided = jnp.where(place < img_len[group], guided, 0.0)
    vel_ref[0] = guided
    start = jnp.where(is_cond, lat_ref[:, :half], lat_ref[:, half:])
    next_ref[0] = start - step_size[step] * guided


def local(
    latents, text_hidden, w_img_in, w_img_qkv, w_txt_kv, q_gain, k_gain, w_out, w_final,
    mod_img, mod_txt, mod_final, guide, step_size, img_len, txt_len, split_flag, tstep,
):
    n_mp = lax.axis_size("mp")
    ids = jnp.stack([lax.axis_index("cfg"), lax.axis_index("group"), lax.axis_index("mp")]).astype(jnp.int32)
    rows, ch = latents.shape
    full = rows * n_mp
    d = w_img_in.shape[1]
    cols = w_img_qkv.shape[1]
    heads = cols // (3 * HD)
    shard = text_hidden.shape[1]
    qg, kg = q_gain.reshape(1, HD), k_gain.reshape(1, HD)

    lat_t = latents.T

    shards = [lat_t] + [ring(lat_t, s) for s in range(1, n_mp)]
    text, *shards = lax.optimization_barrier((text_hidden.reshape(shard, d), *shards))
    text_left = ring(text, 1)
    text_right = ring(text, n_mp - 1)
    own_lat = call(
        prep_body, "prep", (), (1,), [whole((ch, rows))] * n_mp + [whole((ch, d))],
        whole((full, 2 * ch)), jax.ShapeDtypeStruct((full, 2 * ch), BF), [],
        (*shards, w_img_in), 2 * full * ch * d, 2 * ch * d,
    )
    mate_lat = partner(own_lat, "group")

    mod_rows = jnp.transpose(mod_img, (1, 0, 2))
    at_step = pl.BlockSpec((1, 2, d), lambda s, ids, ts, *_: (ts[ids[1]], 0, 0))
    mats, shift = call(
        fold_body, "fold", (ids, tstep), (heads,),
        [whole((ch, d)), whole(mod_rows.shape), pl.BlockSpec((d, 3 * HD), lambda h, *_: (0, h))],
        [pl.BlockSpec((2, 3 * ch, 3 * HD), lambda h, *_: (0, 0, h)),
         pl.BlockSpec((2, 8, 3 * HD), lambda h, *_: (0, 0, h))],
        [jax.ShapeDtypeStruct((2, 3 * ch, cols), BF), jax.ShapeDtypeStruct((2, 8, cols), F32)],
        [pltpu.VMEM((4 * ch + 16, d), BF)],
        (w_img_in, mod_rows, w_img_qkv), 2 * 272 * d * cols, 2 * d * cols,
    )

    by_head = lambda *shape: pl.BlockSpec((1,) + shape, lambda h, *_: (h, 0, 0))
    q, acc = call(
        functools.partial(image_body, full, n_mp), "image_attention", (ids, img_len, split_flag), (heads,),
        [whole((full, 2 * ch)), whole((full, 2 * ch)),
         pl.BlockSpec((2, 3 * ch, 3 * HD), lambda h, *_: (0, 0, h)),
         pl.BlockSpec((2, 8, 3 * HD), lambda h, *_: (0, 0, h)), whole((1, HD)), whole((1, HD))],
        [by_head(full, HD), by_head(full, 2 * HD)],
        [jax.ShapeDtypeStruct((heads, full, HD), BF), jax.ShapeDtypeStruct((heads, full, 2 * HD), F32)],
        [pltpu.VMEM((2 * full, HD), BF), pltpu.VMEM((2 * full, 2 * HD), BF),
         pltpu.VMEM((2 * full, 2 * HD), BF), pltpu.VMEM((2 * HD, 2 * HD), BF)],
        (own_lat, mate_lat, mats, shift, qg, kg), 2 * heads * full * full * 4 * HD * 2, 2**22,
    )

    def text_kv(name, *pieces):
        n = sum(p.shape[0] for p in pieces)
        return call(
            functools.partial(text_body, len(pieces)), name, (ids, tstep), (1,),
            [whole(p.shape) for p in pieces] + [at_step, whole(w_txt_kv.shape), whole((1, HD))],
            whole((heads, n, 2 * HD)), jax.ShapeDtypeStruct((heads, n, 2 * HD), BF),
            [pltpu.VMEM((HD, HD), BF)],
            pieces + (mod_txt, w_txt_kv, kg), 2 * n * d * heads * 2 * HD, 2 * d * heads * 2 * HD,
        )

    kv_own = text_kv("text_kv_own", text)
    mate_own = partner(kv_own, "group")
    text_left, acc = lax.optimization_barrier((text_left, acc))
    text_far = ring(text_left, 1)
    kv_near = text_kv("text_kv_near", text_left, text_right)
    mate_near = partner(kv_near, "group")

    scalars = (ids, txt_len, split_flag)
    acc = call(
        functools.partial(near_body, (0, n_mp - 1, 1), shard, n_mp), "text_attention_near", scalars, (heads,),
        [by_head(full, HD), by_head(full, 2 * HD)] + [by_head(v.shape[1], 2 * HD) for v in (kv_own, mate_own, kv_near, mate_near)],
        by_head(full, 2 * HD), jax.ShapeDtypeStruct(acc.shape, F32), [],
        (q, acc, kv_own, mate_own, kv_near, mate_near), 2 * heads * full * 6 * shard * 3 * HD, 2**23,
    )
    text_far, acc = lax.optimization_barrier((text_far, acc))
    kv_far = text_kv("text_kv_far", text_far)
    mate_far = partner(kv_far, "group")
    block = lambda width: pl.BlockSpec(
        (heads, rows, width), lambda s, ids, *_: (0, lax.rem(ids[2] + s, n_mp), 0)
    )
    depth = heads * HD
    half = rows // 2
    mixed = call(
        functools.partial(last_body, (n_mp - 2,), shard, n_mp), "text_attention_far", scalars, (n_mp,),
        [block(HD), block(2 * HD), whole(kv_far.shape), whole(kv_far.shape)],
        [whole((half, depth))] * (2 * n_mp),
        [jax.ShapeDtypeStruct((half, depth), BF)] * (2 * n_mp), [],
        (q, acc, kv_far, mate_far), 2 * heads * full * 2 * shard * 3 * HD, 2**22,
    )

    n_cfg = lax.axis_size("cfg")

    def send(s, flip):
        if s == 0 and flip == 0:
            return mixed[0]
        pairs = [
            (c * n_mp + i, (c ^ flip) * n_mp + (i + s) % n_mp) for c in range(n_cfg) for i in range(n_mp)
        ]
        return lax.ppermute(mixed[2 * s + flip], ("cfg", "mp"), pairs)

    order = [2, 1, 0, 3]
    pieces = [send(s, flip) for s in order for flip in range(2)]
    w_late, _ = lax.optimization_barrier((w_out, mixed[0]))
    rest, x_kept = call(
        functools.partial(stage_body, n_mp), "out_weights", (ids,), (n_mp,),
        [pl.BlockSpec((1, depth, d), lambda s, ids: (lax.rem(ids[2] + n_mp - s, n_mp), 0, 0)),
         whole((ch, rows)), whole((ch, d))],
        [pl.BlockSpec((1, depth, d), lambda s, ids: (s, 0, 0)), whole((half, d))],
        [jax.ShapeDtypeStruct((n_mp, depth, d), BF), jax.ShapeDtypeStruct((half, d), F32)], [],
        (w_late.reshape(n_mp, depth, d), lat_t, w_img_in), 2 * half * ch * d, 4 * n_mp * depth * d,
    )
    at_weight = lambda s: pl.BlockSpec((1, depth, d), lambda *_: (s, 0, 0))
    total = call(
        early_body, "out_early", (), (1,),
        [whole((half, depth))] * (2 * (n_mp - 1)) + [at_weight(s) for s in order[:-1]],
        whole((rows, d)), jax.ShapeDtypeStruct((rows, d), F32), [],
        (*pieces[:-2], *[rest] * (n_mp - 1)), 2 * rows * (n_mp - 1) * depth * d, 2 * (n_mp - 1) * depth * d,
    )
    vel, moved = call(
        out_body, "out_late", (ids, tstep, img_len, guide, step_size), (1,),
        [whole((half, depth))] * 2
        + [at_weight(order[-1]), whole((rows, d)), whole((half, d)), whole((ch, rows)),
           whole(mod_rows.shape), at_step, whole((ch, d))],
        [whole((1, ch, half))] * 2, [jax.ShapeDtypeStruct((1, ch, half), F32)] * 2, [],
        (*pieces[-2:], rest, total, x_kept, lat_t, mod_rows, mod_final, w_final.T),
        2 * rows * depth * d, 2 * depth * d,
    )
    return jnp.swapaxes(vel, 1, 2), jnp.swapaxes(moved, 1, 2)


def solution(mesh):
    placed = (
        P(("group", "mp"), None),
        P("cfg", ("group", "mp"), None),
        P(),
        P(None, "mp"),
        P(None, "mp"),
    ) + (P(),) * 13
    return jax.shard_map(
        local,
        mesh=mesh,
        in_specs=placed,
        out_specs=(P("cfg", ("group", "mp"), None), P("cfg", ("group", "mp"), None)),
        check_vma=False,
    )
```

time: 509 us -> 107 us (0.21)
  waiting for transfers between devices: 370 us -> 20.5 us
  matrix products: 63.5 us -> 0 us
  Pallas kernels: 0 us -> 44.9 us
  other arithmetic: 27.7 us -> 0.08 us
  starting transfers between devices: 2.35 us -> 29.1 us
  local copies, waits for them, and re-layouts: 27.5 us -> 11.2 us
  between operations: 16.7 us -> 0.99 us
    reduce_scatter x1 -> x0, waiting for transfers between devices: 209 us -> none  [local(): lax.psum_scatter(jnp.dot(mixed, w_local, preferred_element_type=jnp.float...]
    all_gather x2 -> x0, waiting for transfers between devices: 161 us -> none  [the longest x1 103 us: local(): lax.all_gather(img_mod, 'mp', axis=0, tiled=True)]
    pallas_call x0 -> x11, Pallas kernels: none -> 44.9 us  [call(): pl.pallas_call(body, name=name, grid_spec=pltpu.PrefetchScalarGridSpec(nu...]
    dot_general x6 -> x0, matrix products: 43.7 us -> none  [the longest x1 15 us: local(): jnp.einsum('hqk,khe->qhe', probs, all_values, preferred_element_type=jnp....]
    ppermute x3 -> x17, starting transfers between devices: 2.05 us -> 29.1 us  [the longest x6 19.6 us: ring(): return lax.ppermute(value, 'mp', [(i, (i + step) % n) for i in range(n)])]
    ppermute x3 -> x17, waiting for transfers between devices: 0.48 us -> 20.5 us  [the longest x6 12.4 us: ring(): return lax.ppermute(value, 'mp', [(i, (i + step) % n) for i in range(n)])]
    sub x1 -> x0, matrix products: 19.8 us -> none  [local(): weights = jnp.exp(scores - jnp.max(scores, -1, keepdims=True))]
    reduce_sum x8 -> x0, other arithmetic: 9.8 us -> none  [the longest x3 3.74 us: head_norm(): jnp.mean(values * values, -1, keepdims=True) + 1e-06]
  transfers between devices with their start and end apart: 6 -> 17, of which waited for: 4 -> 9; matrix products, arithmetic and copies ran while one was open for 11% -> 0% of each run, Pallas kernels for 0% -> 30%
where the time goes in v1:
time: 107 us
  Pallas kernels  44.9 us (42%)
  starting transfers between devices  29.1 us (27%)
  waiting for transfers between devices  20.5 us (19%)
  local copies, waits for them, and re-layouts  11.2 us (10%)
    pallas_call x11, Pallas kernels, call(): pl.pallas_call(body, name=name, grid_spec=pltpu.PrefetchScalarGridSpec(nu...  44.9 us
    ppermute x6, starting transfers between devices, ring(): return lax.ppermute(value, 'mp', [(i, (i + step) % n) for i in range(n)])  19.6 us
    ppermute x6, waiting for transfers between devices, ring(): return lax.ppermute(value, 'mp', [(i, (i + step) % n) for i in range(n)])  12.4 us
    unnamed x48, local copies, waits for them, and re-layouts  11.2 us
    ppermute x7, starting transfers between devices, send(): return lax.ppermute(mixed[2 * s + flip], ('cfg', 'mp'), pairs)  8.74 us
    ppermute x7, waiting for transfers between devices, send(): return lax.ppermute(mixed[2 * s + flip], ('cfg', 'mp'), pairs)  5.56 us
    ppermute x4, waiting for transfers between devices, partner(): return lax.ppermute(value, axis, [(i, i ^ 1) for i in range(n)])  2.5 us
  transfers between devices with their start and end apart: 17, of which 9 were waited for; matrix products, arithmetic and copies ran while one was open for 0% of the time, Pallas kernels for 30%

profile of v1, /device:TPU:0, one launch (start us, length us, event | category | flops | bytes accessed | tf_op | source)
XLA Modules:
  0.0 106.8 jit_solution(6291426458458310558)
XLA Ops:
  0.7 5.1 %collective-permute-start.2 = (f32[64,256]{1,0:T(8,128)}, f32[64,256]{1,0:T(8,128)S(1)}, u32[]{:S(2)}, u32[]{:S(2)}) collective-permute-start(f32[64,256]{1,0:T(8,128)} %bitcast.21), channel_id=1, source_target_pairs={{0,3},{1,0},{2,1},{3,2},{4,7},{5,4},{6,5},{7,6},{8,11},{9,8},{10,9... | collective-permute-start | bytes 196616 | tf_op jit(solution)/shard_map/ppermute | solution.py:21
  5.8 1.0 collective-permute-start
  6.8 1.8 %collective-permute-done.2.refs_3_ = f32[64,256]{1,0:T(8,128)S(1)} collective-permute-done((f32[64,256]{1,0:T(8,128)}, f32[64,256]{1,0:T(8,128)S(1)}, u32[]{:S(2)}, u32[]{:S(2)}) %collective-permute-start.2) | collective-permute-done | bytes 65568 | tf_op jit(solution)/shard_map/ppermute | solution.py:21
  8.6 3.9 %collective-permute-done.1.refs_2_ = f32[64,256]{1,0:T(8,128)S(1)} collective-permute-done((f32[64,256]{1,0:T(8,128)}, f32[64,256]{1,0:T(8,128)S(1)}, u32[]{:S(2)}, u32[]{:S(2)}) %collective-permute-start.1) | collective-permute-done | bytes 65568 | tf_op jit(solution)/shard_map/ppermute | solution.py:21
  12.5 1.0 copy-done.3
  13.5 0.8 copy-done.10
  14.3 3.5 %prep.1.own_ref = bf16[1024,128]{1,0:T(8,128)(2,1)S(1)} custom-call(f32[64,256]{1,0:T(8,128)S(1)} %bitcast.24, f32[64,256]{1,0:T(8,128)S(1)} %collective-permute-done.refs_1_, f32[64,256]{1,0:T(8,128)S(1)} %collective-permute-done.1.refs_2_, f32[64,256]{1,0:T(8,128)S(1)} %collective-permute-done.2.refs_3_, bf16[64,3072]{1,0:T(8,128)(2,1)S(1)} %copy-done.3), custom_call_target="tpu_custom_call" | custom-call | flops 402653184 | bytes 393216 | tf_op jit(solution)/shard_map/prep/pallas_call | solution.py:43
  18.1 3.7 %collective-permute-start.7 = (bf16[128,3072]{1,0:T(8,128)(2,1)}, bf16[128,3072]{1,0:T(8,128)(2,1)S(1)}, u32[]{:S(2)}, u32[]{:S(2)}) collective-permute-start(bf16[128,3072]{1,0:T(8,128)(2,1)} %bitcast.18), channel_id=1, source_target_pairs={{0,3},{1,0},{2,1},{3,2},{4,7},{5,4},{6,5},{7,6},{8,11},{9,8},{10,9... | collective-permute-start | bytes 2359304 | tf_op jit(solution)/shard_map/ppermute | solution.py:21
  21.8 3.0 %copy-done.1 = bf16[3072,1152]{1,0:T(8,128)(2,1)S(1)} copy-done((bf16[3072,1152]{1,0:T(8,128)(2,1)S(1)}, bf16[3072,1152]{1,0:T(8,128)(2,1)}, u32[]{:S(2)}) %copy-start.1) | copy-done | bytes 7077912
  24.8 1.0 copy-done.4
  25.8 1.0 copy-done.6
  27.4 5.2 %fold.1 = (bf16[2,192,1152]{2,1,0:T(8,128)(2,1)S(1)}, f32[2,8,1152]{2,1,0:T(8,128)S(1)}) custom-call(s32[3]{0:T(128)S(1)} %pad_add_fusion.ids, s32[4]{0:T(128)S(1)} %copy-done.13, bf16[64,3072]{1,0:T(8,128)(2,1)S(1)} %copy-done.4, f32[3,8,3072]{2,1,0:T(8,128)S(1)} %bitcast.15, bf16[3072,1152]{1,0:T(8,128)(2,1)S(1)} %copy-done.1), custom_call_target="tpu_custom_call" | custom-call | flops 1925185536 | bytes 7077888 | tf_op jit(solution)/shard_map/fold/pallas_call | solution.py:43
  32.7 12.4 %image_attention.1 = (bf16[3,1024,128]{2,1,0:T(8,128)(2,1)S(1)}, f32[3,1024,256]{2,1,0:T(8,128)S(1)}) custom-call(s32[3]{0:T(128)S(1)} %pad_add_fusion.ids, s32[4]{0:T(128)S(1)} %copy-done.18, s32[2,4]{1,0:T(2,128)S(1)} %copy-done.16, bf16[1024,128]{1,0:T(8,128)(2,1)S(1)} %prep.1.own_ref, bf16[1024,128]{1,0:T(8,128)(2,1)S(1)} %collective-permute-done.3.mate_ref, ...), custom_call_target="tpu_custom_call" | custom-call | flops 6442450944 | bytes 4194304 | tf_op jit(solution)/shard_map/image_attention/pallas_call | solution.py:43
  45.2 9.7 %collective-permute-start.5 = (bf16[128,3072]{1,0:T(8,128)(2,1)S(1)}, bf16[128,3072]{1,0:T(8,128)(2,1)S(1)}, u32[]{:S(2)}, u32[]{:S(2)}) collective-permute-start(bf16[128,3072]{1,0:T(8,128)(2,1)S(1)} %collective-permute-done.4.refs_0_), channel_id=1, source_target_pairs={{0,1},{1,2},{2,3},{3,0},{4,5},{5,6},{6,7},{7,4},{8,9},{9,10},{10,1... | collective-permute-start | bytes 2359304 | tf_op jit(solution)/shard_map/ppermute | solution.py:21
  55.3 4.2 %text_kv_near.1.own1 = bf16[3,256,256]{2,1,0:T(8,128)(2,1)S(1)} custom-call(s32[3]{0:T(128)S(1)} %pad_add_fusion.ids, s32[4]{0:T(128)S(1)} %copy-done.14, bf16[128,3072]{1,0:T(8,128)(2,1)S(1)} %collective-permute-done.4.refs_0_, bf16[128,3072]{1,0:T(8,128)(2,1)S(1)} %collective-permute-done.7.refs_1_, f32[8,2,3072]{2,1,0:T(2,128)S(1)} %copy-done.2, ...), custom_call_target="tpu_custom_call" | custom-call | flops 1207959552 | bytes 4718592 | tf_op jit(solution)/shard_map/text_kv_near/pallas_call | solution.py:43
  59.6 2.0 %text_kv_own.1.own0 = bf16[3,128,256]{2,1,0:T(8,128)(2,1)S(1)} custom-call(s32[3]{0:T(128)S(1)} %pad_add_fusion.ids, s32[4]{0:T(128)S(1)} %copy-done.14, bf16[128,3072]{1,0:T(8,128)(2,1)S(1)} %bitcast.19, f32[8,2,3072]{2,1,0:T(2,128)S(1)} %copy-done.2, bf16[3072,768]{1,0:T(8,128)(2,1)S(1)} %bitcast.13, f32[1,128]{1,0:T(1,128)S(1)} %bitcast.29), custom_call_target="tpu_custom_call" | custom-call | flops 603979776 | bytes 4718592 | tf_op jit(solution)/shard_map/text_kv_own/pallas_call | solution.py:43
  62.2 1.1 %collective-permute-done.6.mate0 = bf16[3,128,256]{2,1,0:T(8,128)(2,1)S(1)} collective-permute-done((bf16[3,128,256]{2,1,0:T(8,128)(2,1)S(1)}, bf16[3,128,256]{2,1,0:T(8,128)(2,1)S(1)}, u32[]{:S(2)}, u32[]{:S(2)}) %collective-permute-start.6) | collective-permute-done | bytes 196640 | tf_op jit(solution)/shard_map/ppermute | solution.py:26
  63.3 3.9 %text_attention_near.1.acc_ref = f32[3,1024,256]{2,1,0:T(8,128)S(1)} custom-call(s32[3]{0:T(128)S(1)} %pad_add_fusion.ids, s32[4]{0:T(128)S(1)} %copy-done.17, s32[2,4]{1,0:T(2,128)S(1)} %copy-done.16, bf16[3,1024,128]{2,1,0:T(8,128)(2,1)S(1)} %get-tuple-element.34.q_ref, f32[3,1024,256]{2,1,0:T(8,128)S(1)} %get-tuple-element.38.acc_ref, ...), custom_call_target="tpu_custom_call" | custom-call | flops 1811939328 | bytes 8388608 | tf_op jit(solution)/shard_map/text_attention_near/pallas_call | solution.py:43
  67.2 6.4 %collective-permute-done.5.refs_0_ = bf16[128,3072]{1,0:T(8,128)(2,1)S(1)} collective-permute-done((bf16[128,3072]{1,0:T(8,128)(2,1)S(1)}, bf16[128,3072]{1,0:T(8,128)(2,1)S(1)}, u32[]{:S(2)}, u32[]{:S(2)}) %collective-permute-start.5) | collective-permute-done | bytes 786464 | tf_op jit(solution)/shard_map/ppermute | solution.py:21
  73.5 2.0 %text_kv_far.1.own_ref = bf16[3,128,256]{2,1,0:T(8,128)(2,1)S(1)} custom-call(s32[3]{0:T(128)S(1)} %pad_add_fusion.ids, s32[4]{0:T(128)S(1)} %copy-done.14, bf16[128,3072]{1,0:T(8,128)(2,1)S(1)} %collective-permute-done.5.refs_0_, f32[8,2,3072]{2,1,0:T(2,128)S(1)} %copy-done.2, bf16[3072,768]{1,0:T(8,128)(2,1)S(1)} %bitcast.13, f32[1,128]{1,0:T(1,128)S(1)} %bitcast.30), custom_call_target="tpu_custom_call" | custom-call | flops 603979776 | bytes 4718592 | tf_op jit(solution)/shard_map/text_kv_far/pallas_call | solution.py:43
  75.7 1.4 %collective-permute-done.9.mate_ref = bf16[3,128,256]{2,1,0:T(8,128)(2,1)S(1)} collective-permute-done((bf16[3,128,256]{2,1,0:T(8,128)(2,1)S(1)}, bf16[3,128,256]{2,1,0:T(8,128)(2,1)S(1)}, u32[]{:S(2)}, u32[]{:S(2)}) %collective-permute-start.9) | collective-permute-done | bytes 196640 | tf_op jit(solution)/shard_map/ppermute | solution.py:26
  77.1 3.1 %text_attention_far.1 = (bf16[128,384]{1,0:T(8,128)(2,1)S(1)}, bf16[128,384]{1,0:T(8,128)(2,1)S(1)}, bf16[128,384]{1,0:T(8,128)(2,1)S(1)}, bf16[128,384]{1,0:T(8...) custom-call(s32[3]{0:T(128)S(1)} %pad_add_fusion.ids, ...), custom_call_target="tpu_custom_call" | custom-call | flops 603979776 | bytes 4194304 | tf_op jit(solution)/shard_map/text_attention_far/pallas_call | solution.py:43
  80.2 2.0 %collective-permute-start.12 = (bf16[128,384]{1,0:T(8,128)(2,1)S(1)}, bf16[128,384]{1,0:T(8,128)(2,1)S(1)}, u32[]{:S(2)}, u32[]{:S(2)}) collective-permute-start(bf16[128,384]{1,0:T(8,128)(2,1)S(1)} %get-tuple-element.46), channel_id=1, source_target_pairs={{0,2},{1,3},{2,0},{3,1},{16,18},{17,19},{18,16},{19,17},{4,6},{5,7... | collective-permute-start | bytes 294920 | tf_op jit(solution)/shard_map/ppermute | solution.py:378
  82.2 1.9 %collective-permute-start.13 = (bf16[128,384]{1,0:T(8,128)(2,1)S(1)}, bf16[128,384]{1,0:T(8,128)(2,1)S(1)}, u32[]{:S(2)}, u32[]{:S(2)}) collective-permute-start(bf16[128,384]{1,0:T(8,128)(2,1)S(1)} %get-tuple-element.47), channel_id=1, source_target_pairs={{0,18},{1,19},{2,16},{3,17},{16,2},{17,3},{18,0},{19,1},{4,22},{5,... | collective-permute-start | bytes 294920 | tf_op jit(solution)/shard_map/ppermute | solution.py:378
  84.1 2.4 %collective-permute-start.15 = (bf16[128,384]{1,0:T(8,128)(2,1)S(1)}, bf16[128,384]{1,0:T(8,128)(2,1)S(1)}, u32[]{:S(2)}, u32[]{:S(2)}) collective-permute-start(bf16[128,384]{1,0:T(8,128)(2,1)S(1)} %get-tuple-element.49), channel_id=1, source_target_pairs={{0,17},{1,18},{2,19},{3,16},{16,1},{17,2},{18,3},{19,0},{4,21},{5,... | collective-permute-start | bytes 294920 | tf_op jit(solution)/shard_map/ppermute | solution.py:378
  86.6 1.5 %collective-permute-start.16 = (bf16[128,384]{1,0:T(8,128)(2,1)S(1)}, bf16[128,384]{1,0:T(8,128)(2,1)S(1)}, u32[]{:S(2)}, u32[]{:S(2)}) collective-permute-start(bf16[128,384]{1,0:T(8,128)(2,1)S(1)} %get-tuple-element.50), channel_id=1, source_target_pairs={{0,16},{1,17},{2,18},{3,19},{16,0},{17,1},{18,2},{19,3},{4,20},{5,... | collective-permute-start | bytes 294920 | tf_op jit(solution)/shard_map/ppermute | solution.py:378
  88.1 3.7 %copy-done = bf16[1536,3072]{1,0:T(8,128)(2,1)S(1)} copy-done((bf16[1536,3072]{1,0:T(8,128)(2,1)S(1)}, bf16[1536,3072]{1,0:T(8,128)(2,1)}, u32[]{:S(2)}) %copy-start) | copy-done | bytes 9437208
  91.8 1.6 %out_weights.1 = (bf16[4,384,3072]{2,1,0:T(8,128)(2,1)S(1)}, f32[128,3072]{1,0:T(8,128)S(1)}) custom-call(s32[3]{0:T(128)S(1)} %pad_add_fusion.ids, bf16[4,384,3072]{2,1,0:T(8,128)(2,1)S(1)} %bitcast.14, f32[64,256]{1,0:T(8,128)S(1)} %bitcast.25, bf16[64,3072]{1,0:T(8,128)(2,1)S(1)} %copy-done.5), custom_call_target="tpu_custom_call" | custom-call | flops 50331648 | bytes 18874368 | tf_op jit(solution)/shard_map/out_weights/pallas_call | solution.py:43
  94.8 2.2 %collective-permute-done.13.refs_1_ = bf16[128,384]{1,0:T(8,128)(2,1)S(1)} collective-permute-done((bf16[128,384]{1,0:T(8,128)(2,1)S(1)}, bf16[128,384]{1,0:T(8,128)(2,1)S(1)}, u32[]{:S(2)}, u32[]{:S(2)}) %collective-permute-start.13) | collective-permute-done | bytes 98336 | tf_op jit(solution)/shard_map/ppermute | solution.py:378
  97.1 2.6 %out_early.1.refs_3_ = f32[256,3072]{1,0:T(8,128)S(1)} custom-call(bf16[128,384]{1,0:T(8,128)(2,1)S(1)} %collective-permute-done.12.refs_0_, bf16[128,384]{1,0:T(8,128)(2,1)S(1)} %collective-permute-done.13.refs_1_, bf16[128,384]{1,0:T(8,128)(2,1)S(1)} %collective-permute-done.14.refs_2_, bf16[128,384]{1,0:T(8,128)(2,1)S(1)} %collective-permute-done.15.refs_3_, ...), custom_call_target="tpu_custom_call" | custom-call | flops 1811939328 | bytes 7077888 | tf_op jit(solution)/shard_map/out_early/pallas_call | solution.py:43
  99.7 2.8 %collective-permute-done.11.refs_1_ = bf16[128,384]{1,0:T(8,128)(2,1)S(1)} collective-permute-done((bf16[128,384]{1,0:T(8,128)(2,1)S(1)}, bf16[128,384]{1,0:T(8,128)(2,1)S(1)}, u32[]{:S(2)}, u32[]{:S(2)}) %collective-permute-start.11) | collective-permute-done | bytes 98336 | tf_op jit(solution)/shard_map/ppermute | solution.py:378
  102.6 4.2 %out_late.1 = (f32[1,64,128]{2,1,0:T(8,128)}, f32[1,64,128]{2,1,0:T(8,128)}) custom-call(s32[3]{0:T(128)S(1)} %pad_add_fusion.ids, s32[4]{0:T(128)S(1)} %copy-done.14, s32[4]{0:T(128)S(1)} %copy-done.18, f32[4]{0:T(128)S(1)} %copy-done.19, f32[8]{0:T(128)S(1)} %copy-done.20, bf16[128,384]{1,0:T(8,128)(2,1)S(1)} %collective-permute-done.10.refs_0_, ...), custom_call_target="tpu_custom_call" | custom-call | flops 603979776 | bytes 2359296 | tf_op jit(solution)/shard_map/out_late/pallas_call | solution.py:43
  (63 shorter events, 3.6 us)
Async XLA Ops:
  0.6 32.0 %copy-start.16 = (s32[2,4]{1,0:T(2,128)S(1)}, s32[2,4]{1,0:T(2,128)}, u32[]{:S(2)}) copy-start(s32[2,4]{1,0:T(2,128)} %flags.5) | copy-start | bytes 100
  0.6 32.0 %copy-start.18 = (s32[4]{0:T(128)S(1)}, s32[4]{0:T(128)}, u32[]{:S(2)}) copy-start(s32[4]{0:T(128)} %img_len.3) | copy-start | bytes 52
  0.7 32.0 %copy-start.15 = (f32[128]{0:T(128)S(1)}, f32[128]{0:T(128)}, u32[]{:S(2)}) copy-start(f32[128]{0:T(128)} %param.24) | copy-start | bytes 1540
  0.7 32.0 %copy-start.21 = (f32[128]{0:T(128)S(1)}, f32[128]{0:T(128)}, u32[]{:S(2)}) copy-start(f32[128]{0:T(128)} %param.23) | copy-start | bytes 1540
  0.7 7.9 %collective-permute-start.2 = (f32[64,256]{1,0:T(8,128)}, f32[64,256]{1,0:T(8,128)S(1)}, u32[]{:S(2)}, u32[]{:S(2)}) collective-permute-start(f32[64,256]{1,0:T(8,128)} %bitcast.21), channel_id=1, source_target_pairs={{0,3},{1,0},{2,1},{3,2},{4,7},{5,4},{6,5},{7,6},{8,11},{9,8},{10,9... | collective-permute-start | bytes 196616 | tf_op jit(solution)/shard_map/ppermute | solution.py:21
  5.8 6.7 %collective-permute-start.1 = (f32[64,256]{1,0:T(8,128)}, f32[64,256]{1,0:T(8,128)S(1)}, u32[]{:S(2)}, u32[]{:S(2)}) collective-permute-start(f32[64,256]{1,0:T(8,128)} %bitcast.22), channel_id=1, source_target_pairs={{0,2},{1,3},{2,0},{3,1},{4,6},{5,7},{6,4},{7,5},{8,10},{9,11},{10,... | collective-permute-start | bytes 196616 | tf_op jit(solution)/shard_map/ppermute | solution.py:21
  5.8 6.7 %collective-permute-start = (f32[64,256]{1,0:T(8,128)}, f32[64,256]{1,0:T(8,128)S(1)}, u32[]{:S(2)}, u32[]{:S(2)}) collective-permute-start(f32[64,256]{1,0:T(8,128)} %bitcast.23), channel_id=1, source_target_pairs={{0,1},{1,2},{2,3},{3,0},{4,5},{5,6},{6,7},{7,4},{8,9},{9,10},{10,1... | collective-permute-start | bytes 196616 | tf_op jit(solution)/shard_map/ppermute | solution.py:21
  17.8 14.8 %collective-permute-start.3 = (bf16[1024,128]{1,0:T(8,128)(2,1)S(1)}, bf16[1024,128]{1,0:T(8,128)(2,1)S(1)}, u32[]{:S(2)}, u32[]{:S(2)}) collective-permute-start(bf16[1024,128]{1,0:T(8,128)(2,1)S(1)} %prep.1.own_ref), channel_id=1, source_target_pairs={{0,4},{4,0},{8,12},{12,8},{1,5},{5,1},{9,13},{13,9},{2,6},{6,2},{1... | collective-permute-start | bytes 786440 | tf_op jit(solution)/shard_map/ppermute | solution.py:26
  17.8 27.3 %collective-permute-start.4 = (bf16[128,3072]{1,0:T(8,128)(2,1)}, bf16[128,3072]{1,0:T(8,128)(2,1)S(1)}, u32[]{:S(2)}, u32[]{:S(2)}) collective-permute-start(bf16[128,3072]{1,0:T(8,128)(2,1)} %bitcast.17), channel_id=1, source_target_pairs={{0,1},{1,2},{2,3},{3,0},{4,5},{5,6},{6,7},{7,4},{8,9},{9,10},{10,1... | collective-permute-start | bytes 2359304 | tf_op jit(solution)/shard_map/ppermute | solution.py:21
  18.1 37.1 %collective-permute-start.7 = (bf16[128,3072]{1,0:T(8,128)(2,1)}, bf16[128,3072]{1,0:T(8,128)(2,1)S(1)}, u32[]{:S(2)}, u32[]{:S(2)}) collective-permute-start(bf16[128,3072]{1,0:T(8,128)(2,1)} %bitcast.18), channel_id=1, source_target_pairs={{0,3},{1,0},{2,1},{3,2},{4,7},{5,4},{6,5},{7,6},{8,11},{9,8},{10,9... | collective-permute-start | bytes 2359304 | tf_op jit(solution)/shard_map/ppermute | solution.py:21
  27.4 27.8 %slice-start = ((s8[4718592]{0:T(1024)(128)(4,1)}), s8[524288]{0:T(1024)(128)(4,1)S(1)}, s32[]{:S(2)}) async-start(s8[4718592]{0:T(1024)(128)(4,1)} %bitcast.12), calls=%async_computation | async-start | bytes 1048576
  32.7 22.5 %slice-start.1 = ((s8[4718592]{0:T(1024)(128)(4,1)}), s8[4194304]{0:T(1024)(128)(4,1)S(1)}, s32[]{:S(2)}) async-start(s8[4718592]{0:T(1024)(128)(4,1)} %bitcast.12), calls=%async_computation.1 | async-start | bytes 8388608
  32.7 22.5 %copy-start.2 = (f32[8,2,3072]{2,1,0:T(2,128)S(1)}, f32[8,2,3072]{2,1,0:T(2,128)}, u32[]{:S(2)}) copy-start(f32[8,2,3072]{2,1,0:T(2,128)} %refs_1_.3) | copy-start | bytes 589828
  32.7 22.5 %copy-start.14 = (s32[4]{0:T(128)S(1)}, s32[4]{0:T(128)}, u32[]{:S(2)}) copy-start(s32[4]{0:T(128)} %tstep.9) | copy-start | bytes 52
  45.1 14.4 %copy-start.8 = (bf16[1,128,3072]{2,1,0:T(8,128)(2,1)S(1)}, bf16[1,128,3072]{2,1,0:T(8,128)(2,1)}, u32[]{:S(2)}) copy-start(bf16[1,128,3072]{2,1,0:T(8,128)(2,1)} %param.19) | copy-start | bytes 2359300
  45.2 18.1 %copy-start.17 = (s32[4]{0:T(128)S(1)}, s32[4]{0:T(128)}, u32[]{:S(2)}) copy-start(s32[4]{0:T(128)} %txt_len.3) | copy-start | bytes 52
  45.2 28.4 %collective-permute-start.5 = (bf16[128,3072]{1,0:T(8,128)(2,1)S(1)}, bf16[128,3072]{1,0:T(8,128)(2,1)S(1)}, u32[]{:S(2)}, u32[]{:S(2)}) collective-permute-start(bf16[128,3072]{1,0:T(8,128)(2,1)S(1)} %collective-permute-done.4.refs_0_), channel_id=1, source_target_pairs={{0,1},{1,2},{2,3},{3,0},{4,5},{5,6},{6,7},{7,4},{8,9},{9,10},{10,1... | collective-permute-start | bytes 2359304 | tf_op jit(solution)/shard_map/ppermute | solution.py:21
  59.5 3.8 %collective-permute-start.8 = (bf16[3,256,256]{2,1,0:T(8,128)(2,1)S(1)}, bf16[3,256,256]{2,1,0:T(8,128)(2,1)S(1)}, u32[]{:S(2)}, u32[]{:S(2)}) collective-permute-start(bf16[3,256,256]{2,1,0:T(8,128)(2,1)S(1)} %text_kv_near.1.own1), channel_id=1, source_target_pairs={{0,4},{4,0},{8,12},{12,8},{1,5},{5,1},{9,13},{13,9},{2,6},{6,2},{1... | collective-permute-start | bytes 1179656 | tf_op jit(solution)/shard_map/ppermute | solution.py:26
  61.6 1.6 %collective-permute-start.6 = (bf16[3,128,256]{2,1,0:T(8,128)(2,1)S(1)}, bf16[3,128,256]{2,1,0:T(8,128)(2,1)S(1)}, u32[]{:S(2)}, u32[]{:S(2)}) collective-permute-start(bf16[3,128,256]{2,1,0:T(8,128)(2,1)S(1)} %text_kv_own.1.own0), channel_id=1, source_target_pairs={{0,4},{4,0},{8,12},{12,8},{1,5},{5,1},{9,13},{13,9},{2,6},{6,2},{1... | collective-permute-start | bytes 589832 | tf_op jit(solution)/shard_map/ppermute | solution.py:26
  67.1 20.9 %copy-start.5 = (bf16[64,3072]{1,0:T(8,128)(2,1)S(1)}, bf16[64,3072]{1,0:T(8,128)(2,1)}, u32[]{:S(2)}) copy-start(bf16[64,3072]{1,0:T(8,128)(2,1)} %win_ref.3) | copy-start | bytes 1179652
  67.2 20.9 %copy-start.11 = (f32[256,64]{0,1:T(8,128)S(1)}, f32[256,64]{0,1:T(8,128)}, u32[]{:S(2)}) copy-start(f32[256,64]{0,1:T(8,128)} %param.18) | copy-start | bytes 196612
  75.6 1.5 %collective-permute-start.9 = (bf16[3,128,256]{2,1,0:T(8,128)(2,1)S(1)}, bf16[3,128,256]{2,1,0:T(8,128)(2,1)S(1)}, u32[]{:S(2)}, u32[]{:S(2)}) collective-permute-start(bf16[3,128,256]{2,1,0:T(8,128)(2,1)S(1)} %text_kv_far.1.own_ref), channel_id=1, source_target_pairs={{0,4},{4,0},{8,12},{12,8},{1,5},{5,1},{9,13},{13,9},{2,6},{6,2},{1... | collective-permute-start | bytes 589832 | tf_op jit(solution)/shard_map/ppermute | solution.py:26
  80.2 13.8 %collective-permute-start.12 = (bf16[128,384]{1,0:T(8,128)(2,1)S(1)}, bf16[128,384]{1,0:T(8,128)(2,1)S(1)}, u32[]{:S(2)}, u32[]{:S(2)}) collective-permute-start(bf16[128,384]{1,0:T(8,128)(2,1)S(1)} %get-tuple-element.46), channel_id=1, source_target_pairs={{0,2},{1,3},{2,0},{3,1},{16,18},{17,19},{18,16},{19,17},{4,6},{5,7... | collective-permute-start | bytes 294920 | tf_op jit(solution)/shard_map/ppermute | solution.py:378
  82.2 14.8 %collective-permute-start.13 = (bf16[128,384]{1,0:T(8,128)(2,1)S(1)}, bf16[128,384]{1,0:T(8,128)(2,1)S(1)}, u32[]{:S(2)}, u32[]{:S(2)}) collective-permute-start(bf16[128,384]{1,0:T(8,128)(2,1)S(1)} %get-tuple-element.47), channel_id=1, source_target_pairs={{0,18},{1,19},{2,16},{3,17},{16,2},{17,3},{18,0},{19,1},{4,22},{5,... | collective-permute-start | bytes 294920 | tf_op jit(solution)/shard_map/ppermute | solution.py:378
  84.1 12.9 %collective-permute-start.14 = (bf16[128,384]{1,0:T(8,128)(2,1)S(1)}, bf16[128,384]{1,0:T(8,128)(2,1)S(1)}, u32[]{:S(2)}, u32[]{:S(2)}) collective-permute-start(bf16[128,384]{1,0:T(8,128)(2,1)S(1)} %get-tuple-element.48), channel_id=1, source_target_pairs={{0,1},{1,2},{2,3},{3,0},{16,17},{17,18},{18,19},{19,16},{4,5},{5,6... | collective-permute-start | bytes 294920 | tf_op jit(solution)/shard_map/ppermute | solution.py:378
  84.1 12.9 %collective-permute-start.15 = (bf16[128,384]{1,0:T(8,128)(2,1)S(1)}, bf16[128,384]{1,0:T(8,128)(2,1)S(1)}, u32[]{:S(2)}, u32[]{:S(2)}) collective-permute-start(bf16[128,384]{1,0:T(8,128)(2,1)S(1)} %get-tuple-element.49), channel_id=1, source_target_pairs={{0,17},{1,18},{2,19},{3,16},{16,1},{17,2},{18,3},{19,0},{4,21},{5,... | collective-permute-start | bytes 294920 | tf_op jit(solution)/shard_map/ppermute | solution.py:378
  86.6 10.4 %collective-permute-start.16 = (bf16[128,384]{1,0:T(8,128)(2,1)S(1)}, bf16[128,384]{1,0:T(8,128)(2,1)S(1)}, u32[]{:S(2)}, u32[]{:S(2)}) collective-permute-start(bf16[128,384]{1,0:T(8,128)(2,1)S(1)} %get-tuple-element.50), channel_id=1, source_target_pairs={{0,16},{1,17},{2,18},{3,19},{16,0},{17,1},{18,2},{19,3},{4,20},{5,... | collective-permute-start | bytes 294920 | tf_op jit(solution)/shard_map/ppermute | solution.py:378
  94.0 5.7 %collective-permute-start.10 = (bf16[128,384]{1,0:T(8,128)(2,1)S(1)}, bf16[128,384]{1,0:T(8,128)(2,1)S(1)}, u32[]{:S(2)}, u32[]{:S(2)}) collective-permute-start(bf16[128,384]{1,0:T(8,128)(2,1)S(1)} %get-tuple-element.41), channel_id=1, source_target_pairs={{0,3},{1,0},{2,1},{3,2},{16,19},{17,16},{18,17},{19,18},{4,7},{5,4... | collective-permute-start | bytes 294920 | tf_op jit(solution)/shard_map/ppermute | solution.py:378
  97.0 5.6 %collective-permute-start.11 = (bf16[128,384]{1,0:T(8,128)(2,1)S(1)}, bf16[128,384]{1,0:T(8,128)(2,1)S(1)}, u32[]{:S(2)}, u32[]{:S(2)}) collective-permute-start(bf16[128,384]{1,0:T(8,128)(2,1)S(1)} %get-tuple-element.42), channel_id=1, source_target_pairs={{0,19},{1,16},{2,17},{3,18},{16,3},{17,0},{18,1},{19,2},{4,23},{5,... | collective-permute-start | bytes 294920 | tf_op jit(solution)/shard_map/ppermute | solution.py:378
  97.0 5.5 %copy-start.7 = (f32[8,3,3072]{2,0,1:T(8,128)S(1)}, f32[8,3,3072]{2,0,1:T(8,128)}, u32[]{:S(2)}) copy-start(f32[8,3,3072]{2,0,1:T(8,128)} %param.27) | copy-start | bytes 884740
  97.0 5.5 %copy-start.9 = (bf16[3072,64]{0,1:T(8,128)(2,1)S(1)}, bf16[3072,64]{0,1:T(8,128)(2,1)}, u32[]{:S(2)}) copy-start(bf16[3072,64]{0,1:T(8,128)(2,1)} %param.26) | copy-start | bytes 1179652
  97.0 5.5 %copy-start.12 = (f32[8,2,3072]{2,1,0:T(2,128)S(1)}, f32[8,2,3072]{2,1,0:T(2,128)}, u32[]{:S(2)}) copy-start(f32[8,2,3072]{2,1,0:T(2,128)} %refs_7_.1) | copy-start | bytes 589828
  (9 other events, 22.2 us)

commit v2 on v1

v2 whole, which is shorter than its diff:
```python
import functools

import jax
import jax.numpy as jnp
import numpy as np
from jax import lax
from jax.experimental import pallas as pl
from jax.experimental.pallas import tpu as pltpu
from jax.sharding import PartitionSpec as P

HD = 128
EPS = 1e-6
BF = jnp.bfloat16
F32 = jnp.float32
QSCALE = float(HD**-0.5 / np.log(2.0))
VLIM = 20 * 2**20
CHUNK = 64


def ring(value, step):
    n = lax.axis_size("mp")
    return lax.ppermute(value, "mp", [(i, (i + step) % n) for i in range(n)])


def partner(value, axis):
    n = lax.axis_size(axis)
    return lax.ppermute(value, axis, [(i, i ^ 1) for i in range(n)])


def split2(value):
    high = value.astype(BF)
    return high, (value - high.astype(F32)).astype(BF)


def layer_norm(values):
    center = values - jnp.mean(values, -1, keepdims=True)
    return center * lax.rsqrt(jnp.mean(center * center, -1, keepdims=True) + EPS)


def dot(a, b):
    return jnp.dot(a, b, preferred_element_type=F32)


def dot_t(a, b):
    return lax.dot_general(a, b, (((1,), (1,)), ((), ())), preferred_element_type=F32)


FREE = ('prep', 'image_attention', 'text_kv_near', 'text_kv_far', 'text_attention_near', 'text_attention_far', 'out_weights', 'out_early', 'out_late')


def call(body, name, scalars, grid, in_specs, out_specs, out_shape, scratch, args, flops, nbytes):
    if name in FREE:
        flops = nbytes = 0
    return pl.pallas_call(
        body,
        name=name,
        grid_spec=pltpu.PrefetchScalarGridSpec(
            num_scalar_prefetch=len(scalars),
            grid=grid,
            in_specs=in_specs,
            out_specs=out_specs,
            scratch_shapes=scratch,
        ),
        out_shape=out_shape,
        compiler_params=pltpu.CompilerParams(vmem_limit_bytes=VLIM),
        cost_estimate=pl.CostEstimate(flops=flops, bytes_accessed=nbytes, transcendentals=0),
    )(*scalars, *args)


def whole(shape):
    return pl.BlockSpec(shape, lambda *_: (0,) * len(shape))


VMEM = pl.BlockSpec(memory_space=pltpu.VMEM)


def prep_body(*refs):
    *lat_refs, win_ref, out_ref = refs
    for i, ref in enumerate(lat_refs):
        rows = ref[...].astype(F32).T.astype(BF)
        n = rows.shape[0]
        x = dot(rows, win_ref[...])
        center = x - jnp.mean(x, -1, keepdims=True)
        rstd = lax.rsqrt(jnp.mean(center * center, -1, keepdims=True) + EPS)
        high, low = split2(rows.astype(F32) * rstd)
        out_ref[i * n : (i + 1) * n, :] = jnp.concatenate([high, low], axis=1)


def fold_body(ids, tstep, win_ref, mod_ref, w_ref, mats_ref, shift_ref, rows_ref, win_buf, mod_buf, w_buf, sems):
    heads = mats_ref.shape[0]
    ch, d = win_ref.shape
    width = 3 * HD
    first = [pltpu.make_async_copy(win_ref, win_buf, sems.at[heads])]
    first.append(pltpu.make_async_copy(mod_ref.at[0:2], mod_buf, sems.at[heads + 1]))
    weights = [
        pltpu.make_async_copy(w_ref.at[:, h * width : (h + 1) * width], w_buf.at[h], sems.at[h])
        for h in range(heads)
    ]
    for copy in first + weights:
        copy.start()
    for copy in first:
        copy.wait()
    values = win_buf[...].astype(F32)
    center = values - jnp.mean(values, -1, keepdims=True)
    spot = lax.broadcasted_iota(jnp.int32, (16, d), 0)
    tail = jnp.zeros((16, d), F32)
    for i in range(2):
        at = pl.ds(tstep[ids[1] ^ i], 1)
        high, low = split2(center * (1.0 + mod_buf[1, at, :]))
        rows_ref[2 * i * ch : (2 * i + 1) * ch, :] = high
        rows_ref[(2 * i + 1) * ch : (2 * i + 2) * ch, :] = low
        high, low = split2(mod_buf[0, at, :])
        tail = jnp.where(spot == 2 * i, high.astype(F32), tail)
        tail = jnp.where(spot == 2 * i + 1, low.astype(F32), tail)
    rows_ref[4 * ch :, :] = tail.astype(BF)
    for h, copy in enumerate(weights):
        copy.wait()
        out = dot(rows_ref[...], w_buf[h])
        for i in range(2):
            high, low = split2(out[2 * i * ch : (2 * i + 1) * ch] + out[(2 * i + 1) * ch : (2 * i + 2) * ch])
            mats_ref[h, i] = jnp.concatenate([high, high, low], axis=0)
            base = 4 * ch + 2 * i
            shift_ref[h, i] = jnp.broadcast_to(out[base : base + 1] + out[base + 1 : base + 2], shift_ref.shape[2:])


def live_mask(first, rows, length):
    return (lax.broadcasted_iota(jnp.int32, (rows, HD), 0) + first) < length


def fill_ones(ref):
    head = [lax.broadcasted_iota(jnp.int32, ref.shape, i) // HD for i in range(2)]
    ref[...] = (head[0] == head[1]).astype(BF)


def head_norm(values, ones, gain):
    square = dot((values * values).astype(BF), ones)
    return values * lax.rsqrt(square * (1.0 / HD) + EPS) * gain


def image_body(kb, n_mp, ids, img_len, flags, own_ref, mate_ref, mats_ref, shift_ref, qg_ref, kg_ref,
               q_ref, acc_ref, k_ref, v_ref, x_ref, ones_ref):
    group = ids[1]
    n_rows = own_ref.shape[0]
    shard = n_rows // n_mp
    half = HD // 2
    length = img_len[group]
    mate_length = jnp.where(flags[ids[0], group] == 1, img_len[group ^ 1], 0)

    @pl.when(pl.program_id(0) == 0)
    def _():
        fill_ones(ones_ref)
        for base, ref, most in ((0, own_ref, length), (n_rows, mate_ref, mate_length)):
            for s in range(n_mp):
                start = pl.multiple_of(lax.rem(ids[2] + n_mp - s, n_mp) * shard, shard)
                lat = ref[s * shard : (s + 1) * shard, :]
                x_ref[pl.ds(base + start, shard), :] = jnp.concatenate(
                    [lat, lat[:, :half], jnp.zeros((shard, half), BF)], axis=1
                )
            v_ref[base : base + n_rows, HD:] = live_mask(0, n_rows, most).astype(BF)

    zeros = jnp.zeros((half, 3 * HD), BF)
    own_mat = jnp.concatenate([mats_ref[0, 0], zeros], axis=0)
    block = dot(x_ref[:n_rows, :], own_mat) + shift_ref[0, 0, 0:1, :]
    gains = jnp.concatenate([qg_ref[...] * QSCALE, kg_ref[...]], axis=1)
    normed = head_norm(block[:, : 2 * HD], ones_ref[...], gains).astype(BF)
    q_ref[0] = normed[:, :HD]
    k_ref[:n_rows, :] = normed[:, HD:]
    v_ref[:n_rows, :HD] = jnp.where(live_mask(0, n_rows, length), block[:, 2 * HD :], 0.0).astype(BF)

    @pl.when(mate_length > 0)
    def _():
        mate_mat = jnp.concatenate([mats_ref[0, 1], zeros], axis=0)[:, HD:]
        block = dot(x_ref[n_rows:, :], mate_mat) + shift_ref[0, 1, 0:1, HD:]
        k_ref[n_rows:, :] = head_norm(block[:, :HD], ones_ref[:HD, :HD], kg_ref[...]).astype(BF)
        v_ref[n_rows:, :HD] = jnp.where(
            live_mask(0, n_rows, mate_length), block[:, HD:], 0.0
        ).astype(BF)

    def attend(start):
        spot = pl.ds(start, kb)
        p = jnp.exp2(dot_t(q_ref[0], k_ref[spot, :])).astype(BF)
        return dot(p, v_ref[spot, :])

    acc_ref[0] = attend(0)
    for start in range(kb, 2 * n_rows, kb):
        seen = length > start if start < n_rows else mate_length > start - n_rows

        @pl.when(seen)
        def _():
            acc_ref[0] += attend(start)


def text_body(n_in, ids, tstep, *refs):
    rows_refs, (mod_ref, w_ref, kg_ref, out_ref, ones_ref, y_ref) = refs[:n_in], refs[n_in:]
    fill_ones(ones_ref)
    step = tstep[ids[1]]
    scale = 1.0 + mod_ref[step, 1:2, :]
    first = 0
    for ref in rows_refs:
        for start in range(0, ref.shape[0], CHUNK):
            x = ref[start : start + CHUNK, :].astype(F32)
            y_ref[first : first + CHUNK, :] = (layer_norm(x) * scale + mod_ref[step, 0:1, :]).astype(BF)
            first += CHUNK
    kv = dot(y_ref[...], w_ref[...])
    for h in range(out_ref.shape[0]):
        k = kv[:, 2 * HD * h : 2 * HD * h + HD]
        out_ref[h, :, :HD] = head_norm(k, ones_ref[...], kg_ref[...]).astype(BF)
        out_ref[h, :, HD:] = kv[:, 2 * HD * h + HD : 2 * HD * (h + 1)].astype(BF)


def text_attend(offsets, shard, n_mp, ids, txt_len, flags, q, acc, own, mate):
    side, group, m = ids[0], ids[1], ids[2]
    length = txt_len[group]
    mate_length = jnp.where(flags[side, group] == 1, txt_len[group ^ 1], 0)
    keys, values = [], []
    for kv, most in ((own, length), (mate, mate_length)):
        keys.append(kv[:, :HD])
        for i, off in enumerate(offsets):
            live = live_mask(lax.rem(m + off, n_mp) * shard, shard, most)
            v = kv[i * shard : (i + 1) * shard, HD:]
            values.append(
                jnp.concatenate([jnp.where(live, v, jnp.zeros_like(v)), live.astype(BF)], axis=1)
            )
    p = jnp.exp2(dot_t(q, jnp.concatenate(keys, axis=0))).astype(BF)
    return acc + dot(p, jnp.concatenate(values, axis=0))


def near_body(offsets, shard, n_mp, ids, txt_len, flags, q_ref, acc_ref, own0, mate0, own1, mate1, out_ref):
    own = jnp.concatenate([own0[0], own1[0]], axis=0)
    mate = jnp.concatenate([mate0[0], mate1[0]], axis=0)
    out_ref[0] = text_attend(offsets, shard, n_mp, ids, txt_len, flags, q_ref[0], acc_ref[0], own, mate)


def last_body(offsets, shard, n_mp, ids, txt_len, flags, q_ref, acc_ref, own_ref, mate_ref, *out_refs):
    rows = q_ref.shape[1] // n_mp
    half = rows // 2
    is_cond = ids[0] == 0
    for i in range(n_mp):
        spot = pl.ds(pl.multiple_of(lax.rem(ids[2] + i, n_mp) * rows, rows), rows)
        for h in range(q_ref.shape[0]):
            acc = text_attend(
                offsets, shard, n_mp, ids, txt_len, flags, q_ref[h, spot, :], acc_ref[h, spot, :],
                own_ref[h], mate_ref[h],
            )
            mixed = (acc[:, :HD] / acc[:, HD:]).astype(BF)
            low, high = mixed[:half], mixed[half:]
            columns = slice(h * HD, (h + 1) * HD)
            out_refs[2 * i][:, columns] = jnp.where(is_cond, low, high)
            out_refs[2 * i + 1][:, columns] = jnp.where(is_cond, high, low)


def stage_body(n_mp, ids, w_ref, lat_ref, win_ref, rest_ref, x_ref):
    rest_ref[...] = w_ref[...]

    @pl.when(pl.program_id(0) == 0)
    def _():
        half = x_ref.shape[0]
        lat = jnp.where(ids[0] == 0, lat_ref[:, :half], lat_ref[:, half:])
        x_ref[...] = dot(lat.T.astype(BF), win_ref[...])


def project_sides(pieces, weights):
    own, other = (jnp.concatenate([ref[...] for ref in pieces[i::2]], axis=1) for i in range(2))
    return dot(jnp.concatenate([own, other], axis=0), weights)


def early_body(*refs):
    *pieces, wout_ref, total_ref = refs
    depth = pieces[0].shape[1] * len(pieces) // 2
    total_ref[...] = project_sides(pieces, wout_ref[:depth, :])


def out_body(n_late, ids, tstep, img_len, guide, step_size, *refs):
    pieces, refs = refs[: 2 * n_late], refs[2 * n_late :]
    wout_ref, total_ref, x_ref, lat_ref, mod_ref, final_ref, wf_ref, vel_ref, next_ref, total, final = refs
    side, group, m = ids[0], ids[1], ids[2]
    step = tstep[group]
    total[...] = total_ref[...] + project_sides(pieces, wout_ref[-n_late * pieces[0].shape[1] :, :])
    half = x_ref.shape[0]
    gate, scale = mod_ref[2, pl.ds(step, 1), :], 1.0 + final_ref[step, 1:2, :]
    for first in range(0, 2 * half, CHUNK):
        rows = slice(first, first + CHUNK)
        hidden = x_ref[first % half : first % half + CHUNK, :] + gate * total[rows, :]
        final[rows, :] = (layer_norm(hidden) * scale + final_ref[step, 0:1, :]).astype(BF)
    vel = dot_t(wf_ref[...], final[...])
    own, other = vel[:, :half], vel[:, half:]
    is_cond = side == 0
    cond = jnp.where(is_cond, own, other)
    uncond = jnp.where(is_cond, other, own)
    guided = uncond + guide[group] * (cond - uncond)
    place = lax.broadcasted_iota(jnp.int32, guided.shape, 1) + (2 * m + side) * half
    guided = jnp.where(place < img_len[group], guided, 0.0)
    vel_ref[0] = guided
    start = jnp.where(is_cond, lat_ref[:, :half], lat_ref[:, half:])
    next_ref[0] = start - step_size[step] * guided


def local(
    latents, text_hidden, w_img_in, w_img_qkv, w_txt_kv, q_gain, k_gain, w_out, w_final,
    mod_img, mod_txt, mod_final, guide, step_size, img_len, txt_len, split_flag, tstep,
):
    n_mp = lax.axis_size("mp")
    order, n_late = [*range(2, 0, -1), *range(3, n_mp), 0], 2
    ids = jnp.stack([lax.axis_index("cfg"), lax.axis_index("group"), lax.axis_index("mp"), *order]).astype(jnp.int32)
    rows, ch = latents.shape
    full = rows * n_mp
    d = w_img_in.shape[1]
    cols = w_img_qkv.shape[1]
    heads = cols // (3 * HD)
    shard = text_hidden.shape[1]
    qg, kg = q_gain.reshape(1, HD), k_gain.reshape(1, HD)

    lat_t = latents.T

    text = text_hidden.reshape(shard, d)
    text_left = ring(text, 1)
    lat_sent = lat_t.astype(BF)
    shards = [lat_sent] + [ring(lat_sent, s) for s in range(1, n_mp)]

    mod_rows = jnp.transpose(mod_img, (1, 0, 2))
    hbm = pl.BlockSpec(memory_space=pltpu.HBM)
    mats, shift = call(
        fold_body, "fold", (ids, tstep), (1,), [hbm] * 3, [VMEM] * 2,
        [jax.ShapeDtypeStruct((heads, 2, 3 * ch, 3 * HD), BF), jax.ShapeDtypeStruct((heads, 2, 8, 3 * HD), F32)],
        [pltpu.VMEM((4 * ch + 16, d), BF), pltpu.VMEM((ch, d), BF), pltpu.VMEM((2,) + mod_rows.shape[1:], F32),
         pltpu.VMEM((heads, d, 3 * HD), BF), pltpu.SemaphoreType.DMA((heads + 2,))],
        (w_img_in, mod_rows, w_img_qkv), 2 * 272 * d * cols, 2 * d * cols,
    )

    def text_kv(name, *pieces):
        n = sum(p.shape[0] for p in pieces)
        return call(
            functools.partial(text_body, len(pieces)), name, (ids, tstep), (1,),
            [VMEM] * (len(pieces) + 3), VMEM, jax.ShapeDtypeStruct((heads, n, 2 * HD), BF),
            [pltpu.VMEM((HD, HD), BF), pltpu.VMEM((n, d), BF)],
            pieces + (mod_txt, w_txt_kv, kg), 2 * n * d * heads * 2 * HD, 2 * d * heads * 2 * HD,
        )

    text_next, win_late, mats, *shards = lax.optimization_barrier((text, w_img_in, mats, *shards))
    text_right = ring(text_next, n_mp - 1)
    kv_own = text_kv("text_kv_own", text_next)
    mate_own = partner(kv_own, "group")
    own_lat = call(
        prep_body, "prep", (), (1,), [VMEM] * (n_mp + 1),
        VMEM, jax.ShapeDtypeStruct((full, 2 * ch), BF), [],
        (*shards, win_late), 2 * full * ch * d, 2 * ch * d,
    )
    mate_lat = partner(own_lat, "group")
    by_head = lambda *shape: pl.BlockSpec((1,) + shape, lambda h, *_: (h, 0, 0))
    q, acc = call(
        functools.partial(image_body, full, n_mp), "image_attention", (ids, img_len, split_flag), (heads,),
        [whole((full, 2 * ch)), whole((full, 2 * ch)),
         pl.BlockSpec((1, 2, 3 * ch, 3 * HD), lambda h, *_: (h, 0, 0, 0)),
         pl.BlockSpec((1, 2, 8, 3 * HD), lambda h, *_: (h, 0, 0, 0)), whole((1, HD)), whole((1, HD))],
        [by_head(full, HD), by_head(full, 2 * HD)],
        [jax.ShapeDtypeStruct((heads, full, HD), BF), jax.ShapeDtypeStruct((heads, full, 2 * HD), F32)],
        [pltpu.VMEM((2 * full, HD), BF), pltpu.VMEM((2 * full, 2 * HD), BF),
         pltpu.VMEM((2 * full, 2 * HD), BF), pltpu.VMEM((2 * HD, 2 * HD), BF)],
        (own_lat, mate_lat, mats, shift, qg, kg), 2 * heads * full * full * 4 * HD * 2, 2**22,
    )

    text_left, text_right, acc = lax.optimization_barrier((text_left, text_right, acc))
    text_far = ring(text_left, 1)
    kv_near = text_kv("text_kv_near", text_left, text_right)
    mate_near = partner(kv_near, "group")

    scalars = (ids, txt_len, split_flag)
    acc = call(
        functools.partial(near_body, (0, n_mp - 1, 1), shard, n_mp), "text_attention_near", scalars, (heads,),
        [by_head(full, HD), by_head(full, 2 * HD)] + [by_head(v.shape[1], 2 * HD) for v in (kv_own, mate_own, kv_near, mate_near)],
        by_head(full, 2 * HD), jax.ShapeDtypeStruct(acc.shape, F32), [],
        (q, acc, kv_own, mate_own, kv_near, mate_near), 2 * heads * full * 6 * shard * 3 * HD, 2**23,
    )
    depth = heads * HD
    half = rows // 2
    rest, x_kept = call(
        functools.partial(stage_body, n_mp), "out_weights", (ids,), (n_mp,),
        [pl.BlockSpec((depth, d), lambda s, ids: (lax.rem(ids[2] + n_mp - ids[3 + s], n_mp), 0)),
         whole((ch, rows)), whole((ch, d))],
        [pl.BlockSpec((depth, d), lambda s, ids: (s, 0)), whole((half, d))],
        [jax.ShapeDtypeStruct((n_mp * depth, d), BF), jax.ShapeDtypeStruct((half, d), F32)], [],
        (w_out, lat_t, w_img_in), 2 * half * ch * d, 4 * n_mp * depth * d,
    )
    text_far, acc, rest = lax.optimization_barrier((text_far, acc, rest))
    kv_far = text_kv("text_kv_far", text_far)
    mate_far = partner(kv_far, "group")
    mixed = call(
        functools.partial(last_body, (n_mp - 2,), shard, n_mp), "text_attention_far", scalars, (1,),
        [VMEM] * 4, [VMEM] * (2 * n_mp),
        [jax.ShapeDtypeStruct((half, depth), BF)] * (2 * n_mp), [],
        (q, acc, kv_far, mate_far), 2 * heads * full * 2 * shard * 3 * HD, 2**22,
    )

    n_cfg = lax.axis_size("cfg")

    def send(s, flip):
        if s == 0 and flip == 0:
            return mixed[0]
        pairs = [
            (c * n_mp + i, (c ^ flip) * n_mp + (i + s) % n_mp) for c in range(n_cfg) for i in range(n_mp)
        ]
        return lax.ppermute(mixed[2 * s + flip], ("cfg", "mp"), pairs)

    pieces = {(s, flip): send(s, flip) for flip in range(2) for s in order}
    early = [pieces[s, flip] for s in order[:-n_late] for flip in range(2)]
    late = [pieces[s, flip] for s in order[-n_late:] for flip in range(2)]
    total = call(
        early_body, "out_early", (), (1,), [VMEM] * (len(early) + 1), VMEM,
        jax.ShapeDtypeStruct((rows, d), F32), [],
        (*early, rest), 2 * rows * (n_mp - 1) * depth * d, 2 * (n_mp - 1) * depth * d,
    )
    vel, moved = call(
        functools.partial(out_body, n_late), "out_late", (ids, tstep, img_len, guide, step_size), (1,),
        [VMEM] * (7 + 2 * n_late), [VMEM] * 2, [jax.ShapeDtypeStruct((1, ch, half), F32)] * 2,
        [pltpu.VMEM((rows, d), F32), pltpu.VMEM((rows, d), BF)],
        (*late, rest, total, x_kept, lat_t, mod_rows, mod_final, w_final.T),
        2 * rows * depth * d, 2 * depth * d,
    )
    return jnp.swapaxes(vel, 1, 2), jnp.swapaxes(moved, 1, 2)


def solution(mesh):
    placed = (
        P(("group", "mp"), None),
        P("cfg", ("group", "mp"), None),
        P(),
        P(None, "mp"),
        P(None, "mp"),
    ) + (P(),) * 13
    return jax.shard_map(
        local,
        mesh=mesh,
        in_specs=placed,
        out_specs=(P("cfg", ("group", "mp"), None), P("cfg", ("group", "mp"), None)),
        check_vma=False,
    )
```

time: 107 us -> 99.3 us (0.928)
  Pallas kernels: 44.9 us -> 35.8 us
  waiting for transfers between devices: 20.5 us -> 27.8 us
  starting transfers between devices: 29.1 us -> 25.6 us
  local copies, waits for them, and re-layouts: 11.2 us -> 7.97 us
    ppermute x6, starting transfers between devices: 19.6 us -> 9.14 us  [ring(): return lax.ppermute(value, 'mp', [(i, (i + step) % n) for i in range(n)])]
    pallas_call x11, Pallas kernels: 44.9 us -> 35.8 us  [call(): pl.pallas_call(body, name=name, grid_spec=pltpu.PrefetchScalarGridSpec(nu...]
    ppermute x7, starting transfers between devices: 8.74 us -> 15.7 us  [send(): return lax.ppermute(mixed[2 * s + flip], ('cfg', 'mp'), pairs)]
    ppermute x6, waiting for transfers between devices: 12.4 us -> 17.2 us  [ring(): return lax.ppermute(value, 'mp', [(i, (i + step) % n) for i in range(n)])]
    unnamed x48 -> x52, local copies, waits for them, and re-layouts: 11.2 us -> 7.88 us
    ppermute x7, waiting for transfers between devices: 5.56 us -> 7.69 us  [send(): return lax.ppermute(mixed[2 * s + flip], ('cfg', 'mp'), pairs)]
  transfers between devices with their start and end apart: 17 -> 17, of which waited for: 9 -> 8; matrix products, arithmetic and copies ran while one was open for 0% -> 0% of each run, Pallas kernels for 30% -> 28%
where the time goes in v2:
time: 99.3 us; the launch traced here: 99 us
  Pallas kernels  35.8 us (36%)
  waiting for transfers between devices  27.8 us (28%)
  starting transfers between devices  25.6 us (26%)
  local copies, waits for them, and re-layouts  7.97 us (8%)
    pallas_call x11, Pallas kernels, call(): pl.pallas_call(body, name=name, grid_spec=pltpu.PrefetchScalarGridSpec(nu...  35.8 us
    ppermute x6, waiting for transfers between devices, ring(): return lax.ppermute(value, 'mp', [(i, (i + step) % n) for i in range(n)])  17.2 us
    ppermute x7, starting transfers between devices, send(): return lax.ppermute(mixed[2 * s + flip], ('cfg', 'mp'), pairs)  15.7 us
    ppermute x6, starting transfers between devices, ring(): return lax.ppermute(value, 'mp', [(i, (i + step) % n) for i in range(n)])  9.14 us
    unnamed x52, local copies, waits for them, and re-layouts  7.88 us
    ppermute x7, waiting for transfers between devices, send(): return lax.ppermute(mixed[2 * s + flip], ('cfg', 'mp'), pairs)  7.69 us
    ppermute x4, waiting for transfers between devices, partner(): return lax.ppermute(value, axis, [(i, i ^ 1) for i in range(n)])  2.96 us
  transfers between devices with their start and end apart: 17, of which 8 were waited for; matrix products, arithmetic and copies ran while one was open for 0% of the time, Pallas kernels for 28%

profile of v2, /device:TPU:0, one launch (start us, length us, event | category | flops | bytes accessed | tf_op | source)
XLA Modules:
  0.0 99.0 jit_solution(14492621205109237482)
XLA Ops:
  0.7 0.9 bitcast_convert_fusion.refs_0_
  1.6 5.0 %collective-permute-start.2 = (bf16[64,256]{1,0:T(8,128)(2,1)S(1)}, bf16[64,256]{1,0:T(8,128)(2,1)S(1)}, u32[]{:S(2)}, u32[]{:S(2)}) collective-permute-start(bf16[64,256]{1,0:T(8,128)(2,1)S(1)} %bitcast_convert_fusion.refs_0_), channel_id=1, source_target_pairs={{0,3},{1,0},{2,1},{3,2},{4,7},{5,4},{6,5},{7,6},{8,11},{9,8},{10,9... | collective-permute-start | bytes 98312 | tf_op jit(solution)/shard_map/ppermute | solution.py:22
  6.6 1.0 %collective-permute-start = (bf16[64,256]{1,0:T(8,128)(2,1)S(1)}, bf16[64,256]{1,0:T(8,128)(2,1)S(1)}, u32[]{:S(2)}, u32[]{:S(2)}) collective-permute-start(bf16[64,256]{1,0:T(8,128)(2,1)S(1)} %bitcast_convert_fusion.refs_0_), channel_id=1, source_target_pairs={{0,1},{1,2},{2,3},{3,0},{4,5},{5,6},{6,7},{7,4},{8,9},{9,10},{10,1... | collective-permute-start | bytes 98312 | tf_op jit(solution)/shard_map/ppermute | solution.py:22
  7.6 2.5 %collective-permute-start.4 = (bf16[128,3072]{1,0:T(8,128)(2,1)}, bf16[128,3072]{1,0:T(8,128)(2,1)S(1)}, u32[]{:S(2)}, u32[]{:S(2)}) collective-permute-start(bf16[128,3072]{1,0:T(8,128)(2,1)} %bitcast.18), channel_id=1, source_target_pairs={{0,1},{1,2},{2,3},{3,0},{4,5},{5,6},{6,7},{7,4},{8,9},{9,10},{10,1... | collective-permute-start | bytes 2359304 | tf_op jit(solution)/shard_map/ppermute | solution.py:22
  10.2 3.2 %copy-done = bf16[3072,1152]{1,0:T(8,128)(2,1)S(1)} copy-done((bf16[3072,1152]{1,0:T(8,128)(2,1)S(1)}, bf16[3072,1152]{1,0:T(8,128)(2,1)}, u32[]{:S(2)}) %copy-start) | copy-done | bytes 7077912
  13.3 1.1 %copy-done.1 = bf16[64,3072]{1,0:T(8,128)(2,1)S(1)} copy-done((bf16[64,3072]{1,0:T(8,128)(2,1)S(1)}, bf16[64,3072]{1,0:T(8,128)(2,1)}, u32[]{:S(2)}) %copy-start.1) | copy-done | bytes 393240
  14.5 1.0 copy-done.6
  16.1 5.4 %fold.1 = (bf16[3,2,192,384]{3,2,1,0:T(8,128)(2,1)S(1)}, f32[3,2,8,384]{3,2,1,0:T(8,128)S(1)}) custom-call(s32[7]{0:T(128)S(1)} %stack.15.ids, s32[4]{0:T(128)S(1)} %copy-done.12, bf16[64,3072]{1,0:T(8,128)(2,1)S(1)} %copy-done.1, f32[3,8,3072]{2,1,0:T(8,128)S(1)} %bitcast.16, bf16[3072,1152]{1,0:T(8,128)(2,1)S(1)} %copy-done), custom_call_target="tpu_custom_call" | custom-call | flops 1925185536 | bytes 7077888 | tf_op jit(solution)/shard_map/fold/pallas_call | solution.py:54
  21.5 5.9 %collective-permute-done.1.refs_2_ = bf16[64,256]{1,0:T(8,128)(2,1)S(1)} collective-permute-done((bf16[64,256]{1,0:T(8,128)(2,1)S(1)}, bf16[64,256]{1,0:T(8,128)(2,1)S(1)}, u32[]{:S(2)}, u32[]{:S(2)}) %collective-permute-start.1) | collective-permute-done | bytes 32800 | tf_op jit(solution)/shard_map/ppermute | solution.py:22
  27.4 1.0 %copy-done.2 = bf16[64,3072]{1,0:T(8,128)(2,1)S(1)} copy-done((bf16[64,3072]{1,0:T(8,128)(2,1)S(1)}, bf16[64,3072]{1,0:T(8,128)(2,1)}, u32[]{:S(2)}) %copy-start.2) | copy-done | bytes 393240
  28.4 3.5 %prep.1.own_ref = bf16[1024,128]{1,0:T(8,128)(2,1)S(1)} custom-call(bf16[64,256]{1,0:T(8,128)(2,1)S(1)} %bitcast_convert_fusion.refs_0_, bf16[64,256]{1,0:T(8,128)(2,1)S(1)} %collective-permute-done.refs_1_, bf16[64,256]{1,0:T(8,128)(2,1)S(1)} %collective-permute-done.1.refs_2_, bf16[64,256]{1,0:T(8,128)(2,1)S(1)} %collective-permute-done.2.refs_3_, ...), custom_call_target="tpu_custom_call" | custom-call | tf_op jit(solution)/shard_map/prep/pallas_call | solution.py:54
  31.9 1.5 %collective-permute-done.3.mate_ref = bf16[1024,128]{1,0:T(8,128)(2,1)S(1)} collective-permute-done((bf16[1024,128]{1,0:T(8,128)(2,1)S(1)}, bf16[1024,128]{1,0:T(8,128)(2,1)S(1)}, u32[]{:S(2)}, u32[]{:S(2)}) %collective-permute-start.3) | collective-permute-done | bytes 262176 | tf_op jit(solution)/shard_map/ppermute | solution.py:27
  33.4 6.8 %image_attention.1 = (bf16[3,1024,128]{2,1,0:T(8,128)(2,1)S(1)}, f32[3,1024,256]{2,1,0:T(8,128)S(1)}) custom-call(s32[7]{0:T(128)S(1)} %stack.15.ids, s32[4]{0:T(128)S(1)} %copy-done.16, s32[2,4]{1,0:T(2,128)S(1)} %copy-done.14, bf16[1024,128]{1,0:T(8,128)(2,1)S(1)} %prep.1.own_ref, bf16[1024,128]{1,0:T(8,128)(2,1)S(1)} %collective-permute-done.3.mate_ref, ...), custom_call_target="tpu_custom_call" | custom-call | tf_op jit(solution)/shard_map/image_attention/pallas_call | solution.py:54
  40.3 5.2 %collective-permute-done.5.refs_1_ = bf16[128,3072]{1,0:T(8,128)(2,1)S(1)} collective-permute-done((bf16[128,3072]{1,0:T(8,128)(2,1)}, bf16[128,3072]{1,0:T(8,128)(2,1)S(1)}, u32[]{:S(2)}, u32[]{:S(2)}) %collective-permute-start.5) | collective-permute-done | bytes 786464 | tf_op jit(solution)/shard_map/ppermute | solution.py:22
  46.1 0.9 copy-done.4
  47.0 2.9 %text_kv_near.1.own1 = bf16[3,256,256]{2,1,0:T(8,128)(2,1)S(1)} custom-call(s32[7]{0:T(128)S(1)} %stack.15.ids, s32[4]{0:T(128)S(1)} %copy-done.13, bf16[128,3072]{1,0:T(8,128)(2,1)S(1)} %collective-permute-done.4.refs_0_, bf16[128,3072]{1,0:T(8,128)(2,1)S(1)} %collective-permute-done.5.refs_1_, f32[8,2,3072]{2,1,0:T(2,128)S(1)} %copy-done.4, ...), custom_call_target="tpu_custom_call" | custom-call | tf_op jit(solution)/shard_map/text_kv_near/pallas_call | solution.py:54
  50.1 1.9 %text_kv_own.1.own0 = bf16[3,128,256]{2,1,0:T(8,128)(2,1)S(1)} custom-call(s32[7]{0:T(128)S(1)} %stack.15.ids, s32[4]{0:T(128)S(1)} %copy-done.13, bf16[128,3072]{1,0:T(8,128)(2,1)S(1)} %bitcast.20, f32[8,2,3072]{2,1,0:T(2,128)S(1)} %copy-done.5, bf16[3072,768]{1,0:T(8,128)(2,1)S(1)} %bitcast.13, f32[1,128]{1,0:T(1,128)S(1)} %bitcast.26), custom_call_target="tpu_custom_call" | custom-call | flops 603979776 | bytes 4718592 | tf_op jit(solution)/shard_map/text_kv_own/pallas_call | solution.py:54
  52.6 1.6 %out_weights.1 = (bf16[1536,3072]{1,0:T(8,128)(2,1)S(1)}, f32[128,3072]{1,0:T(8,128)S(1)}) custom-call(s32[7]{0:T(128)S(1)} %stack.15.ids, bf16[1536,3072]{1,0:T(8,128)(2,1)S(1)} %bitcast.15, f32[64,256]{1,0:T(8,128)S(1)} %bitcast.21, bf16[64,3072]{1,0:T(8,128)(2,1)S(1)} %copy-done.3), custom_call_target="tpu_custom_call" | custom-call | tf_op jit(solution)/shard_map/out_weights/pallas_call | solution.py:54
  54.3 3.9 %text_attention_near.1.acc_ref = f32[3,1024,256]{2,1,0:T(8,128)S(1)} custom-call(s32[7]{0:T(128)S(1)} %stack.15.ids, s32[4]{0:T(128)S(1)} %copy-done.17, s32[2,4]{1,0:T(2,128)S(1)} %copy-done.14, bf16[3,1024,128]{2,1,0:T(8,128)(2,1)S(1)} %get-tuple-element.39.q_ref, f32[3,1024,256]{2,1,0:T(8,128)S(1)} %get-tuple-element.43.acc_ref, ...), custom_call_target="tpu_custom_call" | custom-call | tf_op jit(solution)/shard_map/text_attention_near/pallas_call | solution.py:54
  58.2 6.1 %collective-permute-done.6.refs_0_ = bf16[128,3072]{1,0:T(8,128)(2,1)S(1)} collective-permute-done((bf16[128,3072]{1,0:T(8,128)(2,1)S(1)}, bf16[128,3072]{1,0:T(8,128)(2,1)S(1)}, u32[]{:S(2)}, u32[]{:S(2)}) %collective-permute-start.6) | collective-permute-done | bytes 786464 | tf_op jit(solution)/shard_map/ppermute | solution.py:22
  64.3 1.9 %text_kv_far.1.own_ref = bf16[3,128,256]{2,1,0:T(8,128)(2,1)S(1)} custom-call(s32[7]{0:T(128)S(1)} %stack.15.ids, s32[4]{0:T(128)S(1)} %copy-done.13, bf16[128,3072]{1,0:T(8,128)(2,1)S(1)} %collective-permute-done.6.refs_0_, f32[8,2,3072]{2,1,0:T(2,128)S(1)} %copy-done.5, bf16[3072,768]{1,0:T(8,128)(2,1)S(1)} %bitcast.13, f32[1,128]{1,0:T(1,128)S(1)} %bitcast.27), custom_call_target="tpu_custom_call" | custom-call | tf_op jit(solution)/shard_map/text_kv_far/pallas_call | solution.py:54
  66.3 1.4 %collective-permute-done.9.mate_ref = bf16[3,128,256]{2,1,0:T(8,128)(2,1)S(1)} collective-permute-done((bf16[3,128,256]{2,1,0:T(8,128)(2,1)S(1)}, bf16[3,128,256]{2,1,0:T(8,128)(2,1)S(1)}, u32[]{:S(2)}, u32[]{:S(2)}) %collective-permute-start.9) | collective-permute-done | bytes 196640 | tf_op jit(solution)/shard_map/ppermute | solution.py:27
  67.7 1.7 %text_attention_far.1 = (bf16[128,384]{1,0:T(8,128)(2,1)S(1)}, bf16[128,384]{1,0:T(8,128)(2,1)S(1)}, bf16[128,384]{1,0:T(8,128)(2,1)S(1)}, bf16[128,384]{1,0:T(8...) custom-call(s32[7]{0:T(128)S(1)} %stack.15.ids, ...), custom_call_target="tpu_custom_call" | custom-call | tf_op jit(solution)/shard_map/text_attention_far/pallas_call | solution.py:54
  69.4 1.1 %collective-permute-start.13 = (bf16[128,384]{1,0:T(8,128)(2,1)S(1)}, bf16[128,384]{1,0:T(8,128)(2,1)S(1)}, u32[]{:S(2)}, u32[]{:S(2)}) collective-permute-start(bf16[128,384]{1,0:T(8,128)(2,1)S(1)} %get-tuple-element.53), channel_id=1, source_target_pairs={{0,2},{1,3},{2,0},{3,1},{16,18},{17,19},{18,16},{19,17},{4,6},{5,7... | collective-permute-start | bytes 294920 | tf_op jit(solution)/shard_map/ppermute | solution.py:402
  70.5 6.0 %collective-permute-start.14 = (bf16[128,384]{1,0:T(8,128)(2,1)S(1)}, bf16[128,384]{1,0:T(8,128)(2,1)S(1)}, u32[]{:S(2)}, u32[]{:S(2)}) collective-permute-start(bf16[128,384]{1,0:T(8,128)(2,1)S(1)} %get-tuple-element.54), channel_id=1, source_target_pairs={{0,18},{1,19},{2,16},{3,17},{16,2},{17,3},{18,0},{19,1},{4,22},{5,... | collective-permute-start | bytes 294920 | tf_op jit(solution)/shard_map/ppermute | solution.py:402
  76.5 2.0 %collective-permute-start.15 = (bf16[128,384]{1,0:T(8,128)(2,1)S(1)}, bf16[128,384]{1,0:T(8,128)(2,1)S(1)}, u32[]{:S(2)}, u32[]{:S(2)}) collective-permute-start(bf16[128,384]{1,0:T(8,128)(2,1)S(1)} %get-tuple-element.55), channel_id=1, source_target_pairs={{0,1},{1,2},{2,3},{3,0},{16,17},{17,18},{18,19},{19,16},{4,5},{5,6... | collective-permute-start | bytes 294920 | tf_op jit(solution)/shard_map/ppermute | solution.py:402
  78.5 1.1 %collective-permute-done.13.refs_0_ = bf16[128,384]{1,0:T(8,128)(2,1)S(1)} collective-permute-done((bf16[128,384]{1,0:T(8,128)(2,1)S(1)}, bf16[128,384]{1,0:T(8,128)(2,1)S(1)}, u32[]{:S(2)}, u32[]{:S(2)}) %collective-permute-start.13) | collective-permute-done | bytes 98336 | tf_op jit(solution)/shard_map/ppermute | solution.py:402
  79.6 6.6 %collective-permute-start.11 = (bf16[128,384]{1,0:T(8,128)(2,1)S(1)}, bf16[128,384]{1,0:T(8,128)(2,1)S(1)}, u32[]{:S(2)}, u32[]{:S(2)}) collective-permute-start(bf16[128,384]{1,0:T(8,128)(2,1)S(1)} %get-tuple-element.49), channel_id=1, source_target_pairs={{0,19},{1,16},{2,17},{3,18},{16,3},{17,0},{18,1},{19,2},{4,23},{5,... | collective-permute-start | bytes 294920 | tf_op jit(solution)/shard_map/ppermute | solution.py:402
  86.1 3.5 %collective-permute-done.14.refs_1_ = bf16[128,384]{1,0:T(8,128)(2,1)S(1)} collective-permute-done((bf16[128,384]{1,0:T(8,128)(2,1)S(1)}, bf16[128,384]{1,0:T(8,128)(2,1)S(1)}, u32[]{:S(2)}, u32[]{:S(2)}) %collective-permute-start.14) | collective-permute-done | bytes 98336 | tf_op jit(solution)/shard_map/ppermute | solution.py:402
  89.7 1.4 %out_early.1.refs_5_ = f32[256,3072]{1,0:T(8,128)S(1)} custom-call(bf16[128,384]{1,0:T(8,128)(2,1)S(1)} %collective-permute-done.13.refs_0_, bf16[128,384]{1,0:T(8,128)(2,1)S(1)} %collective-permute-done.14.refs_1_, bf16[128,384]{1,0:T(8,128)(2,1)S(1)} %collective-permute-done.15.refs_2_, bf16[128,384]{1,0:T(8,128)(2,1)S(1)} %collective-permute-done.16.refs_3_, ...), custom_call_target="tpu_custom_call" | custom-call | tf_op jit(solution)/shard_map/out_early/pallas_call | solution.py:54
  91.2 3.2 %collective-permute-done.12.refs_3_ = bf16[128,384]{1,0:T(8,128)(2,1)S(1)} collective-permute-done((bf16[128,384]{1,0:T(8,128)(2,1)S(1)}, bf16[128,384]{1,0:T(8,128)(2,1)S(1)}, u32[]{:S(2)}, u32[]{:S(2)}) %collective-permute-start.12) | collective-permute-done | bytes 98336 | tf_op jit(solution)/shard_map/ppermute | solution.py:402
  94.4 4.7 %out_late.1 = (f32[1,64,128]{2,1,0:T(8,128)}, f32[1,64,128]{2,1,0:T(8,128)}) custom-call(s32[7]{0:T(128)S(1)} %stack.15.ids, s32[4]{0:T(128)S(1)} %copy-done.13, s32[4]{0:T(128)S(1)} %copy-done.16, f32[4]{0:T(128)S(1)} %copy-done.18, f32[8]{0:T(128)S(1)} %copy-done.19, bf16[128,384]{1,0:T(8,128)(2,1)S(1)} %collective-permute-done.10.refs_0_, ...), custom_call_target="tpu_custom_call" | custom-call | tf_op jit(solution)/shard_map/out_late/pallas_call | solution.py:54
  (69 shorter events, 2.3 us)
Async XLA Ops:
  0.6 32.8 %copy-start.14 = (s32[2,4]{1,0:T(2,128)S(1)}, s32[2,4]{1,0:T(2,128)}, u32[]{:S(2)}) copy-start(s32[2,4]{1,0:T(2,128)} %flags.5) | copy-start | bytes 100
  0.6 32.8 %copy-start.16 = (s32[4]{0:T(128)S(1)}, s32[4]{0:T(128)}, u32[]{:S(2)}) copy-start(s32[4]{0:T(128)} %img_len.3) | copy-start | bytes 52
  0.7 32.8 %copy-start.15 = (f32[128]{0:T(128)S(1)}, f32[128]{0:T(128)}, u32[]{:S(2)}) copy-start(f32[128]{0:T(128)} %param.24) | copy-start | bytes 1540
  0.7 32.8 %copy-start.20 = (f32[128]{0:T(128)S(1)}, f32[128]{0:T(128)}, u32[]{:S(2)}) copy-start(f32[128]{0:T(128)} %param.23) | copy-start | bytes 1540
  0.7 45.4 %copy-start.13 = (s32[4]{0:T(128)S(1)}, s32[4]{0:T(128)}, u32[]{:S(2)}) copy-start(s32[4]{0:T(128)} %tstep.9) | copy-start | bytes 52
  1.6 19.9 %collective-permute-start.2 = (bf16[64,256]{1,0:T(8,128)(2,1)S(1)}, bf16[64,256]{1,0:T(8,128)(2,1)S(1)}, u32[]{:S(2)}, u32[]{:S(2)}) collective-permute-start(bf16[64,256]{1,0:T(8,128)(2,1)S(1)} %bitcast_convert_fusion.refs_0_), channel_id=1, source_target_pairs={{0,3},{1,0},{2,1},{3,2},{4,7},{5,4},{6,5},{7,6},{8,11},{9,8},{10,9... | collective-permute-start | bytes 98312 | tf_op jit(solution)/shard_map/ppermute | solution.py:22
  6.6 20.8 %collective-permute-start.1 = (bf16[64,256]{1,0:T(8,128)(2,1)S(1)}, bf16[64,256]{1,0:T(8,128)(2,1)S(1)}, u32[]{:S(2)}, u32[]{:S(2)}) collective-permute-start(bf16[64,256]{1,0:T(8,128)(2,1)S(1)} %bitcast_convert_fusion.refs_0_), channel_id=1, source_target_pairs={{0,2},{1,3},{2,0},{3,1},{4,6},{5,7},{6,4},{7,5},{8,10},{9,11},{10,... | collective-permute-start | bytes 98312 | tf_op jit(solution)/shard_map/ppermute | solution.py:22
  6.6 20.8 %collective-permute-start = (bf16[64,256]{1,0:T(8,128)(2,1)S(1)}, bf16[64,256]{1,0:T(8,128)(2,1)S(1)}, u32[]{:S(2)}, u32[]{:S(2)}) collective-permute-start(bf16[64,256]{1,0:T(8,128)(2,1)S(1)} %bitcast_convert_fusion.refs_0_), channel_id=1, source_target_pairs={{0,1},{1,2},{2,3},{3,0},{4,5},{5,6},{6,7},{7,4},{8,9},{9,10},{10,1... | collective-permute-start | bytes 98312 | tf_op jit(solution)/shard_map/ppermute | solution.py:22
  7.6 32.6 %collective-permute-start.4 = (bf16[128,3072]{1,0:T(8,128)(2,1)}, bf16[128,3072]{1,0:T(8,128)(2,1)S(1)}, u32[]{:S(2)}, u32[]{:S(2)}) collective-permute-start(bf16[128,3072]{1,0:T(8,128)(2,1)} %bitcast.18), channel_id=1, source_target_pairs={{0,1},{1,2},{2,3},{3,0},{4,5},{5,6},{6,7},{7,4},{8,9},{9,10},{10,1... | collective-permute-start | bytes 2359304 | tf_op jit(solution)/shard_map/ppermute | solution.py:22
  10.2 35.9 %slice-start = ((s8[4718592]{0:T(1024)(128)(4,1)}), s8[4194304]{0:T(1024)(128)(4,1)S(1)}, s32[]{:S(2)}) async-start(s8[4718592]{0:T(1024)(128)(4,1)} %bitcast.12), calls=%async_computation | async-start | bytes 8388608
  16.1 30.0 %slice-start.1 = ((s8[4718592]{0:T(1024)(128)(4,1)}), s8[524288]{0:T(1024)(128)(4,1)S(1)}, s32[]{:S(2)}) async-start(s8[4718592]{0:T(1024)(128)(4,1)} %bitcast.12), calls=%async_computation.1 | async-start | bytes 1048576
  16.1 36.5 %slice-start.2 = ((s8[9437184]{0:T(1024)(128)(4,1)}), s8[4194304]{0:T(1024)(128)(4,1)S(1)}, s32[]{:S(2)}) async-start(s8[9437184]{0:T(1024)(128)(4,1)} %bitcast.14), calls=%async_computation.2 | async-start | bytes 8388608
  16.1 36.5 %slice-start.3 = ((s8[9437184]{0:T(1024)(128)(4,1)}), s8[4194304]{0:T(1024)(128)(4,1)S(1)}, s32[]{:S(2)}) async-start(s8[9437184]{0:T(1024)(128)(4,1)} %bitcast.14), calls=%async_computation.3 | async-start | bytes 8388608
  27.4 18.1 %collective-permute-start.5 = (bf16[128,3072]{1,0:T(8,128)(2,1)}, bf16[128,3072]{1,0:T(8,128)(2,1)S(1)}, u32[]{:S(2)}, u32[]{:S(2)}) collective-permute-start(bf16[128,3072]{1,0:T(8,128)(2,1)} %bitcast.19), channel_id=1, source_target_pairs={{0,3},{1,0},{2,1},{3,2},{4,7},{5,4},{6,5},{7,6},{8,11},{9,8},{10,9... | collective-permute-start | bytes 2359304 | tf_op jit(solution)/shard_map/ppermute | solution.py:22
  31.9 1.6 %collective-permute-start.3 = (bf16[1024,128]{1,0:T(8,128)(2,1)S(1)}, bf16[1024,128]{1,0:T(8,128)(2,1)S(1)}, u32[]{:S(2)}, u32[]{:S(2)}) collective-permute-start(bf16[1024,128]{1,0:T(8,128)(2,1)S(1)} %prep.1.own_ref), channel_id=1, source_target_pairs={{0,4},{4,0},{8,12},{12,8},{1,5},{5,1},{9,13},{13,9},{2,6},{6,2},{1... | collective-permute-start | bytes 786440 | tf_op jit(solution)/shard_map/ppermute | solution.py:27
  45.5 7.1 %slice-start.4 = ((s8[9437184]{0:T(1024)(128)(4,1)}), s8[1048576]{0:T(1024)(128)(4,1)S(1)}, s32[]{:S(2)}) async-start(s8[9437184]{0:T(1024)(128)(4,1)} %bitcast.14), calls=%async_computation.4 | async-start | bytes 2097152
  45.5 7.1 %copy-start.3 = (bf16[64,3072]{1,0:T(8,128)(2,1)S(1)}, bf16[64,3072]{1,0:T(8,128)(2,1)}, u32[]{:S(2)}) copy-start(bf16[64,3072]{1,0:T(8,128)(2,1)} %win_ref.3) | copy-start | bytes 1179652
  45.5 18.8 %collective-permute-start.6 = (bf16[128,3072]{1,0:T(8,128)(2,1)S(1)}, bf16[128,3072]{1,0:T(8,128)(2,1)S(1)}, u32[]{:S(2)}, u32[]{:S(2)}) collective-permute-start(bf16[128,3072]{1,0:T(8,128)(2,1)S(1)} %collective-permute-done.4.refs_0_), channel_id=1, source_target_pairs={{0,1},{1,2},{2,3},{3,0},{4,5},{5,6},{6,7},{7,4},{8,9},{9,10},{10,1... | collective-permute-start | bytes 2359304 | tf_op jit(solution)/shard_map/ppermute | solution.py:22
  47.0 5.6 %copy-start.9 = (f32[256,64]{0,1:T(8,128)S(1)}, f32[256,64]{0,1:T(8,128)}, u32[]{:S(2)}) copy-start(f32[256,64]{0,1:T(8,128)} %param.18) | copy-start | bytes 196612
  50.0 4.3 %collective-permute-start.8 = (bf16[3,256,256]{2,1,0:T(8,128)(2,1)S(1)}, bf16[3,256,256]{2,1,0:T(8,128)(2,1)S(1)}, u32[]{:S(2)}, u32[]{:S(2)}) collective-permute-start(bf16[3,256,256]{2,1,0:T(8,128)(2,1)S(1)} %text_kv_near.1.own1), channel_id=1, source_target_pairs={{0,4},{4,0},{8,12},{12,8},{1,5},{5,1},{9,13},{13,9},{2,6},{6,2},{1... | collective-permute-start | bytes 1179656 | tf_op jit(solution)/shard_map/ppermute | solution.py:27
  52.0 2.2 %collective-permute-start.7 = (bf16[3,128,256]{2,1,0:T(8,128)(2,1)S(1)}, bf16[3,128,256]{2,1,0:T(8,128)(2,1)S(1)}, u32[]{:S(2)}, u32[]{:S(2)}) collective-permute-start(bf16[3,128,256]{2,1,0:T(8,128)(2,1)S(1)} %text_kv_own.1.own0), channel_id=1, source_target_pairs={{0,4},{4,0},{8,12},{12,8},{1,5},{5,1},{9,13},{13,9},{2,6},{6,2},{1... | collective-permute-start | bytes 589832 | tf_op jit(solution)/shard_map/ppermute | solution.py:27
  66.2 1.5 %collective-permute-start.9 = (bf16[3,128,256]{2,1,0:T(8,128)(2,1)S(1)}, bf16[3,128,256]{2,1,0:T(8,128)(2,1)S(1)}, u32[]{:S(2)}, u32[]{:S(2)}) collective-permute-start(bf16[3,128,256]{2,1,0:T(8,128)(2,1)S(1)} %text_kv_far.1.own_ref), channel_id=1, source_target_pairs={{0,4},{4,0},{8,12},{12,8},{1,5},{5,1},{9,13},{13,9},{2,6},{6,2},{1... | collective-permute-start | bytes 589832 | tf_op jit(solution)/shard_map/ppermute | solution.py:27
  69.4 10.1 %collective-permute-start.13 = (bf16[128,384]{1,0:T(8,128)(2,1)S(1)}, bf16[128,384]{1,0:T(8,128)(2,1)S(1)}, u32[]{:S(2)}, u32[]{:S(2)}) collective-permute-start(bf16[128,384]{1,0:T(8,128)(2,1)S(1)} %get-tuple-element.53), channel_id=1, source_target_pairs={{0,2},{1,3},{2,0},{3,1},{16,18},{17,19},{18,16},{19,17},{4,6},{5,7... | collective-permute-start | bytes 294920 | tf_op jit(solution)/shard_map/ppermute | solution.py:402
  70.5 19.1 %collective-permute-start.14 = (bf16[128,384]{1,0:T(8,128)(2,1)S(1)}, bf16[128,384]{1,0:T(8,128)(2,1)S(1)}, u32[]{:S(2)}, u32[]{:S(2)}) collective-permute-start(bf16[128,384]{1,0:T(8,128)(2,1)S(1)} %get-tuple-element.54), channel_id=1, source_target_pairs={{0,18},{1,19},{2,16},{3,17},{16,2},{17,3},{18,0},{19,1},{4,22},{5,... | collective-permute-start | bytes 294920 | tf_op jit(solution)/shard_map/ppermute | solution.py:402
  76.5 14.7 %collective-permute-start.10 = (bf16[128,384]{1,0:T(8,128)(2,1)S(1)}, bf16[128,384]{1,0:T(8,128)(2,1)S(1)}, u32[]{:S(2)}, u32[]{:S(2)}) collective-permute-start(bf16[128,384]{1,0:T(8,128)(2,1)S(1)} %get-tuple-element.48), channel_id=1, source_target_pairs={{0,3},{1,0},{2,1},{3,2},{16,19},{17,16},{18,17},{19,18},{4,7},{5,4... | collective-permute-start | bytes 294920 | tf_op jit(solution)/shard_map/ppermute | solution.py:402
  76.5 13.2 %collective-permute-start.15 = (bf16[128,384]{1,0:T(8,128)(2,1)S(1)}, bf16[128,384]{1,0:T(8,128)(2,1)S(1)}, u32[]{:S(2)}, u32[]{:S(2)}) collective-permute-start(bf16[128,384]{1,0:T(8,128)(2,1)S(1)} %get-tuple-element.55), channel_id=1, source_target_pairs={{0,1},{1,2},{2,3},{3,0},{16,17},{17,18},{18,19},{19,16},{4,5},{5,6... | collective-permute-start | bytes 294920 | tf_op jit(solution)/shard_map/ppermute | solution.py:402
  78.5 11.2 %collective-permute-start.16 = (bf16[128,384]{1,0:T(8,128)(2,1)S(1)}, bf16[128,384]{1,0:T(8,128)(2,1)S(1)}, u32[]{:S(2)}, u32[]{:S(2)}) collective-permute-start(bf16[128,384]{1,0:T(8,128)(2,1)S(1)} %get-tuple-element.56), channel_id=1, source_target_pairs={{0,17},{1,18},{2,19},{3,16},{16,1},{17,2},{18,3},{19,0},{4,21},{5,... | collective-permute-start | bytes 294920 | tf_op jit(solution)/shard_map/ppermute | solution.py:402
  79.6 11.6 %collective-permute-start.11 = (bf16[128,384]{1,0:T(8,128)(2,1)S(1)}, bf16[128,384]{1,0:T(8,128)(2,1)S(1)}, u32[]{:S(2)}, u32[]{:S(2)}) collective-permute-start(bf16[128,384]{1,0:T(8,128)(2,1)S(1)} %get-tuple-element.49), channel_id=1, source_target_pairs={{0,19},{1,16},{2,17},{3,18},{16,3},{17,0},{18,1},{19,2},{4,23},{5,... | collective-permute-start | bytes 294920 | tf_op jit(solution)/shard_map/ppermute | solution.py:402
  89.6 4.7 %copy-start.11 = (f32[8,2,3072]{2,1,0:T(2,128)S(1)}, f32[8,2,3072]{2,1,0:T(2,128)}, u32[]{:S(2)}) copy-start(f32[8,2,3072]{2,1,0:T(2,128)} %refs_9_.1) | copy-start | bytes 589828
  89.6 4.8 %copy-start.18 = (f32[4]{0:T(128)S(1)}, f32[4]{0:T(128)}, u32[]{:S(2)}) copy-start(f32[4]{0:T(128)} %guide.1) | copy-start | bytes 52
  89.6 4.8 %copy-start.19 = (f32[8]{0:T(128)S(1)}, f32[8]{0:T(128)}, u32[]{:S(2)}) copy-start(f32[8]{0:T(128)} %step_size.1) | copy-start | bytes 100
  89.6 4.7 %collective-permute-start.12 = (bf16[128,384]{1,0:T(8,128)(2,1)S(1)}, bf16[128,384]{1,0:T(8,128)(2,1)S(1)}, u32[]{:S(2)}, u32[]{:S(2)}) collective-permute-start(bf16[128,384]{1,0:T(8,128)(2,1)S(1)} %get-tuple-element.51), channel_id=1, source_target_pairs={{0,16},{1,17},{2,18},{3,19},{16,0},{17,1},{18,2},{19,3},{4,20},{5,... | collective-permute-start | bytes 294920 | tf_op jit(solution)/shard_map/ppermute | solution.py:402
  (11 other events, 25.1 us)

commit v3 on v2

--- a/solution.py
+++ b/solution.py
@@ -45,7 +45,7 @@
     return lax.dot_general(a, b, (((1,), (1,)), ((), ())), preferred_element_type=F32)
 
 
-FREE = ('prep', 'image_attention', 'text_kv_near', 'text_kv_far', 'text_attention_near', 'text_attention_far', 'out_weights', 'out_early', 'out_late')
+FREE = ('prep', 'image_own', 'image_mate', 'text_kv_near', 'text_kv_far', 'text_attention_near', 'text_attention_far', 'out_weights', 'out_own', 'out_early', 'out_late')
 
 
 def call(body, name, scalars, grid, in_specs, out_specs, out_shape, scratch, args, flops, nbytes):
@@ -137,57 +137,59 @@
     return values * lax.rsqrt(square * (1.0 / HD) + EPS) * gain
 
 
-def image_body(kb, n_mp, ids, img_len, flags, own_ref, mate_ref, mats_ref, shift_ref, qg_ref, kg_ref,
-               q_ref, acc_ref, k_ref, v_ref, x_ref, ones_ref):
-    group = ids[1]
-    n_rows = own_ref.shape[0]
-    shard = n_rows // n_mp
+def place_rows(n_mp, ids, ref, x_ref):
+    shard = ref.shape[0] // n_mp
     half = HD // 2
-    length = img_len[group]
-    mate_length = jnp.where(flags[ids[0], group] == 1, img_len[group ^ 1], 0)
-
+    for s in range(n_mp):
+        start = pl.multiple_of(lax.rem(ids[2] + n_mp - s, n_mp) * shard, shard)
+        lat = ref[s * shard : (s + 1) * shard, :]
+        x_ref[pl.ds(start, shard), :] = jnp.concatenate(
+            [lat, lat[:, :half], jnp.zeros((shard, half), BF)], axis=1
+        )
+
+
+def project(which, first, x_ref, mats_ref, shift_ref):
+    mat = mats_ref[0, which]
+    mat = jnp.concatenate([mat, jnp.zeros((2 * HD - mat.shape[0], mat.shape[1]), BF)], axis=0)[:, first:]
+    return dot(x_ref[...], mat) + shift_ref[0, which, 0:1, first:]
+
+
+def attend(q, k, v, length):
+    live = live_mask(0, k.shape[0], length)
+    values = jnp.concatenate([jnp.where(live, v, 0.0).astype(BF), live.astype(BF)], axis=1)
+    return dot(jnp.exp2(dot_t(q, k)).astype(BF), values)
+
+
+def image_body(n_mp, ids, img_len, lat_ref, mats_ref, shift_ref, qg_ref, kg_ref, q_ref, acc_ref, x_ref, ones_ref):
     @pl.when(pl.program_id(0) == 0)
     def _():
         fill_ones(ones_ref)
-        for base, ref, most in ((0, own_ref, length), (n_rows, mate_ref, mate_length)):
-            for s in range(n_mp):
-                start = pl.multiple_of(lax.rem(ids[2] + n_mp - s, n_mp) * shard, shard)
-                lat = ref[s * shard : (s + 1) * shard, :]
-                x_ref[pl.ds(base + start, shard), :] = jnp.concatenate(
-                    [lat, lat[:, :half], jnp.zeros((shard, half), BF)], axis=1
-                )
-            v_ref[base : base + n_rows, HD:] = live_mask(0, n_rows, most).astype(BF)
-
-    zeros = jnp.zeros((half, 3 * HD), BF)
-    own_mat = jnp.concatenate([mats_ref[0, 0], zeros], axis=0)
-    block = dot(x_ref[:n_rows, :], own_mat) + shift_ref[0, 0, 0:1, :]
+        place_rows(n_mp, ids, lat_ref, x_ref)
+
+    block = project(0, 0, x_ref, mats_ref, shift_ref)
     gains = jnp.concatenate([qg_ref[...] * QSCALE, kg_ref[...]], axis=1)
     normed = head_norm(block[:, : 2 * HD], ones_ref[...], gains).astype(BF)
     q_ref[0] = normed[:, :HD]
-    k_ref[:n_rows, :] = normed[:, HD:]
-    v_ref[:n_rows, :HD] = jnp.where(live_mask(0, n_rows, length), block[:, 2 * HD :], 0.0).astype(BF)
-
-    @pl.when(mate_length > 0)
+    acc_ref[0] = attend(normed[:, :HD], normed[:, HD:], block[:, 2 * HD :], img_len[ids[1]])
+
+
+def mate_body(n_mp, ids, img_len, flags, lat_ref, mats_ref, shift_ref, kg_ref, q_ref, acc_ref, out_ref, x_ref, ones_ref):
+    seen = flags[ids[0], ids[1]] == 1
+
+    @pl.when(jnp.logical_and(seen, pl.program_id(0) == 0))
     def _():
-        mate_mat = jnp.concatenate([mats_ref[0, 1], zeros], axis=0)[:, HD:]
-        block = dot(x_ref[n_rows:, :], mate_mat) + shift_ref[0, 1, 0:1, HD:]
-        k_ref[n_rows:, :] = head_norm(block[:, :HD], ones_ref[:HD, :HD], kg_ref[...]).astype(BF)
-        v_ref[n_rows:, :HD] = jnp.where(
-            live_mask(0, n_rows, mate_length), block[:, HD:], 0.0
-        ).astype(BF)
-
-    def attend(start):
-        spot = pl.ds(start, kb)
-        p = jnp.exp2(dot_t(q_ref[0], k_ref[spot, :])).astype(BF)
-        return dot(p, v_ref[spot, :])
-
-    acc_ref[0] = attend(0)
-    for start in range(kb, 2 * n_rows, kb):
-        seen = length > start if start < n_rows else mate_length > start - n_rows
-
-        @pl.when(seen)
-        def _():
-            acc_ref[0] += attend(start)
+        fill_ones(ones_ref)
+        place_rows(n_mp, ids, lat_ref, x_ref)
+
+    @pl.when(seen)
+    def _():
+        block = project(1, HD, x_ref, mats_ref, shift_ref)
+        keys = head_norm(block[:, :HD], ones_ref[...], kg_ref[...]).astype(BF)
+        out_ref[0] = acc_ref[0] + attend(q_ref[0], keys, block[:, HD:], img_len[ids[1] ^ 1])
+
+    @pl.when(jnp.logical_not(seen))
+    def _():
+        out_ref[0] = acc_ref[0]
 
 
 def text_body(n_in, ids, tstep, *refs):
@@ -259,35 +261,42 @@
         x_ref[...] = dot(lat.T.astype(BF), win_ref[...])
 
 
-def project_sides(pieces, weights):
+def early_body(*refs):
+    *pieces, w_ref, total_ref = refs
     own, other = (jnp.concatenate([ref[...] for ref in pieces[i::2]], axis=1) for i in range(2))
-    return dot(jnp.concatenate([own, other], axis=0), weights)
-
-
-def early_body(*refs):
-    *pieces, wout_ref, total_ref = refs
-    depth = pieces[0].shape[1] * len(pieces) // 2
-    total_ref[...] = project_sides(pieces, wout_ref[:depth, :])
-
-
-def out_body(n_late, ids, tstep, img_len, guide, step_size, *refs):
-    pieces, refs = refs[: 2 * n_late], refs[2 * n_late :]
-    wout_ref, total_ref, x_ref, lat_ref, mod_ref, final_ref, wf_ref, vel_ref, next_ref, total, final = refs
+    total_ref[...] = dot(jnp.concatenate([own, other], axis=0), w_ref[: own.shape[1], :])
+
+
+def final_rows(step, first_row, early_ref, piece_ref, w_ref, x_ref, mod_ref, norm_ref, wf_ref, total, out):
+    total[...] = dot(piece_ref[...], w_ref[-piece_ref.shape[1] :, :])
+    gate, scale = mod_ref[2, pl.ds(step, 1), :], 1.0 + norm_ref[step, 1:2, :]
+    for first in range(0, x_ref.shape[0], CHUNK):
+        rows = slice(first, first + CHUNK)
+        hidden = x_ref[rows, :] + gate * (early_ref[first_row + first : first_row + first + CHUNK, :] + total[rows, :])
+        out[rows, :] = (layer_norm(hidden) * scale + norm_ref[step, 0:1, :]).astype(BF)
+    return dot_t(wf_ref[...], out[...])
+
+
+def own_body(ids, tstep, *refs):
+    early_ref, piece_ref, w_ref, x_ref, mod_ref, norm_ref, wf_ref, vel_ref, total, out = refs
+    vel_ref[...] = final_rows(
+        tstep[ids[1]], 0, early_ref, piece_ref, w_ref, x_ref, mod_ref, norm_ref, wf_ref, total, out
+    )
+
+
+def out_body(ids, tstep, img_len, guide, step_size, *refs):
+    early_ref, piece_ref, w_ref, own_ref, lat_ref, x_ref, mod_ref, norm_ref, wf_ref, vel_ref, next_ref, total, out = refs
     side, group, m = ids[0], ids[1], ids[2]
     step = tstep[group]
-    total[...] = total_ref[...] + project_sides(pieces, wout_ref[-n_late * pieces[0].shape[1] :, :])
-    half = x_ref.shape[0]
-    gate, scale = mod_ref[2, pl.ds(step, 1), :], 1.0 + final_ref[step, 1:2, :]
-    for first in range(0, 2 * half, CHUNK):
-        rows = slice(first, first + CHUNK)
-        hidden = x_ref[first % half : first % half + CHUNK, :] + gate * total[rows, :]
-        final[rows, :] = (layer_norm(hidden) * scale + final_ref[step, 0:1, :]).astype(BF)
-    vel = dot_t(wf_ref[...], final[...])
-    own, other = vel[:, :half], vel[:, half:]
+    other = final_rows(
+        step, x_ref.shape[0], early_ref, piece_ref, w_ref, x_ref, mod_ref, norm_ref, wf_ref, total, out
+    )
+    own = own_ref[...]
     is_cond = side == 0
     cond = jnp.where(is_cond, own, other)
     uncond = jnp.where(is_cond, other, own)
     guided = uncond + guide[group] * (cond - uncond)
+    half = own.shape[1]
     place = lax.broadcasted_iota(jnp.int32, guided.shape, 1) + (2 * m + side) * half
     guided = jnp.where(place < img_len[group], guided, 0.0)
     vel_ref[0] = guided
@@ -300,7 +309,7 @@
     mod_img, mod_txt, mod_final, guide, step_size, img_len, txt_len, split_flag, tstep,
 ):
     n_mp = lax.axis_size("mp")
-    order, n_late = [*range(2, 0, -1), *range(3, n_mp), 0], 2
+    order = [0, *range(3, n_mp), 1, 2]
     ids = jnp.stack([lax.axis_index("cfg"), lax.axis_index("group"), lax.axis_index("mp"), *order]).astype(jnp.int32)
     rows, ch = latents.shape
     full = rows * n_mp
@@ -336,41 +345,36 @@
             pieces + (mod_txt, w_txt_kv, kg), 2 * n * d * heads * 2 * HD, 2 * d * heads * 2 * HD,
         )
 
-    text_next, win_late, mats, *shards = lax.optimization_barrier((text, w_img_in, mats, *shards))
+    text_next, mats, *shards = lax.optimization_barrier((text, mats, *shards))
     text_right = ring(text_next, n_mp - 1)
-    kv_own = text_kv("text_kv_own", text_next)
-    mate_own = partner(kv_own, "group")
     own_lat = call(
         prep_body, "prep", (), (1,), [VMEM] * (n_mp + 1),
         VMEM, jax.ShapeDtypeStruct((full, 2 * ch), BF), [],
-        (*shards, win_late), 2 * full * ch * d, 2 * ch * d,
+        (*shards, w_img_in), 2 * full * ch * d, 2 * ch * d,
     )
     mate_lat = partner(own_lat, "group")
+    kv_own = text_kv("text_kv_own", text_next)
+    mate_own = partner(kv_own, "group")
+
     by_head = lambda *shape: pl.BlockSpec((1,) + shape, lambda h, *_: (h, 0, 0))
+    of_head = [pl.BlockSpec((1, 2, n, 3 * HD), lambda h, *_: (h, 0, 0, 0)) for n in (3 * ch, 8)]
+    acc_shape = jax.ShapeDtypeStruct((heads, full, 2 * HD), F32)
     q, acc = call(
-        functools.partial(image_body, full, n_mp), "image_attention", (ids, img_len, split_flag), (heads,),
-        [whole((full, 2 * ch)), whole((full, 2 * ch)),
-         pl.BlockSpec((1, 2, 3 * ch, 3 * HD), lambda h, *_: (h, 0, 0, 0)),
-         pl.BlockSpec((1, 2, 8, 3 * HD), lambda h, *_: (h, 0, 0, 0)), whole((1, HD)), whole((1, HD))],
+        functools.partial(image_body, n_mp), "image_own", (ids, img_len), (heads,),
+        [whole((full, 2 * ch)), *of_head, whole((1, HD)), whole((1, HD))],
         [by_head(full, HD), by_head(full, 2 * HD)],
-        [jax.ShapeDtypeStruct((heads, full, HD), BF), jax.ShapeDtypeStruct((heads, full, 2 * HD), F32)],
-        [pltpu.VMEM((2 * full, HD), BF), pltpu.VMEM((2 * full, 2 * HD), BF),
-         pltpu.VMEM((2 * full, 2 * HD), BF), pltpu.VMEM((2 * HD, 2 * HD), BF)],
-        (own_lat, mate_lat, mats, shift, qg, kg), 2 * heads * full * full * 4 * HD * 2, 2**22,
-    )
-
-    text_left, text_right, acc = lax.optimization_barrier((text_left, text_right, acc))
-    text_far = ring(text_left, 1)
-    kv_near = text_kv("text_kv_near", text_left, text_right)
-    mate_near = partner(kv_near, "group")
-
-    scalars = (ids, txt_len, split_flag)
+        [jax.ShapeDtypeStruct((heads, full, HD), BF), acc_shape],
+        [pltpu.VMEM((full, 2 * HD), BF), pltpu.VMEM((2 * HD, 2 * HD), BF)],
+        (own_lat, mats, shift, qg, kg), 2 * heads * full * full * 3 * HD, 2**22,
+    )
     acc = call(
-        functools.partial(near_body, (0, n_mp - 1, 1), shard, n_mp), "text_attention_near", scalars, (heads,),
-        [by_head(full, HD), by_head(full, 2 * HD)] + [by_head(v.shape[1], 2 * HD) for v in (kv_own, mate_own, kv_near, mate_near)],
-        by_head(full, 2 * HD), jax.ShapeDtypeStruct(acc.shape, F32), [],
-        (q, acc, kv_own, mate_own, kv_near, mate_near), 2 * heads * full * 6 * shard * 3 * HD, 2**23,
-    )
+        functools.partial(mate_body, n_mp), "image_mate", (ids, img_len, split_flag), (heads,),
+        [whole((full, 2 * ch)), *of_head, whole((1, HD)), by_head(full, HD), by_head(full, 2 * HD)],
+        by_head(full, 2 * HD), acc_shape,
+        [pltpu.VMEM((full, 2 * HD), BF), pltpu.VMEM((HD, HD), BF)],
+        (mate_lat, mats, shift, kg, q, acc), 2 * heads * full * full * 3 * HD, 2**22,
+    )
+
     depth = heads * HD
     half = rows // 2
     rest, x_kept = call(
@@ -381,6 +385,18 @@
         [jax.ShapeDtypeStruct((n_mp * depth, d), BF), jax.ShapeDtypeStruct((half, d), F32)], [],
         (w_out, lat_t, w_img_in), 2 * half * ch * d, 4 * n_mp * depth * d,
     )
+    text_right, text_left, acc = lax.optimization_barrier((text_right, text_left, acc))
+    text_far = ring(text_right, n_mp - 1)
+    kv_near = text_kv("text_kv_near", text_left, text_right)
+    mate_near = partner(kv_near, "group")
+
+    scalars = (ids, txt_len, split_flag)
+    acc = call(
+        functools.partial(near_body, (0, n_mp - 1, 1), shard, n_mp), "text_attention_near", scalars, (heads,),
+        [by_head(full, HD), by_head(full, 2 * HD)] + [by_head(v.shape[1], 2 * HD) for v in (kv_own, mate_own, kv_near, mate_near)],
+        by_head(full, 2 * HD), jax.ShapeDtypeStruct(acc.shape, F32), [],
+        (q, acc, kv_own, mate_own, kv_near, mate_near), 2 * heads * full * 6 * shard * 3 * HD, 2**23,
+    )
     text_far, acc, rest = lax.optimization_barrier((text_far, acc, rest))
     kv_far = text_kv("text_kv_far", text_far)
     mate_far = partner(kv_far, "group")
@@ -401,20 +417,24 @@
         ]
         return lax.ppermute(mixed[2 * s + flip], ("cfg", "mp"), pairs)
 
-    pieces = {(s, flip): send(s, flip) for flip in range(2) for s in order}
-    early = [pieces[s, flip] for s in order[:-n_late] for flip in range(2)]
-    late = [pieces[s, flip] for s in order[-n_late:] for flip in range(2)]
+    pieces = {(s, flip): send(s, flip) for s in order for flip in range(2)}
+    early = [pieces[s, flip] for s in order[:-1] for flip in range(2)]
     total = call(
         early_body, "out_early", (), (1,), [VMEM] * (len(early) + 1), VMEM,
         jax.ShapeDtypeStruct((rows, d), F32), [],
-        (*early, rest), 2 * rows * (n_mp - 1) * depth * d, 2 * (n_mp - 1) * depth * d,
+        (*early, rest), rows * len(early) * depth * d, len(early) * depth * d,
+    )
+    work = [pltpu.VMEM((half, d), F32), pltpu.VMEM((half, d), BF)]
+    tables = (x_kept, mod_rows, mod_final, w_final.T)
+    own_vel = call(
+        own_body, "out_own", (ids, tstep), (1,), [VMEM] * 7, VMEM,
+        jax.ShapeDtypeStruct((ch, half), F32), work,
+        (total, pieces[order[-1], 0], rest, *tables), 2 * half * depth * d, 2 * depth * d,
     )
     vel, moved = call(
-        functools.partial(out_body, n_late), "out_late", (ids, tstep, img_len, guide, step_size), (1,),
-        [VMEM] * (7 + 2 * n_late), [VMEM] * 2, [jax.ShapeDtypeStruct((1, ch, half), F32)] * 2,
-        [pltpu.VMEM((rows, d), F32), pltpu.VMEM((rows, d), BF)],
-        (*late, rest, total, x_kept, lat_t, mod_rows, mod_final, w_final.T),
-        2 * rows * depth * d, 2 * depth * d,
+        out_body, "out_late", (ids, tstep, img_len, guide, step_size), (1,),
+        [VMEM] * 9, [VMEM] * 2, [jax.ShapeDtypeStruct((1, ch, half), F32)] * 2, work,
+        (total, pieces[order[-1], 1], rest, own_vel, lat_t, *tables), 2 * half * depth * d, 2 * depth * d,
     )
     return jnp.swapaxes(vel, 1, 2), jnp.swapaxes(moved, 1, 2)
 

time: 99.3 us -> 95.9 us (0.966)
  Pallas kernels: 35.8 us -> 43.8 us
  starting transfers between devices: 25.6 us -> 20.6 us
  waiting for transfers between devices: 27.8 us -> 22.9 us
  local copies, waits for them, and re-layouts: 7.97 us -> 5.81 us
    pallas_call x11 -> x13, Pallas kernels: 35.8 us -> 43.8 us  [call(): pl.pallas_call(body, name=name, grid_spec=pltpu.PrefetchScalarGridSpec(nu...]
    ppermute x7, starting transfers between devices: 15.7 us -> 9.4 us  [send(): return lax.ppermute(mixed[2 * s + flip], ('cfg', 'mp'), pairs)]
    ppermute x6, waiting for transfers between devices: 17.2 us -> 13.5 us  [ring(): return lax.ppermute(value, 'mp', [(i, (i + step) % n) for i in range(n)])]
    unnamed x52 -> x46, local copies, waits for them, and re-layouts: 7.88 us -> 5.73 us
    ppermute x4, waiting for transfers between devices: 2.96 us -> 1.44 us  [partner(): return lax.ppermute(value, axis, [(i, i ^ 1) for i in range(n)])]
    ppermute x6, starting transfers between devices: 9.14 us -> 10.5 us  [ring(): return lax.ppermute(value, 'mp', [(i, (i + step) % n) for i in range(n)])]
  transfers between devices with their start and end apart: 17 -> 17, of which waited for: 8 -> 8; matrix products, arithmetic and copies ran while one was open for 0% -> 0% of each run, Pallas kernels for 28% -> 39%
where the time goes in v3:
time: 95.9 us; the launch traced here: 95 us
  Pallas kernels  43.8 us (46%)
  waiting for transfers between devices  22.9 us (24%)
  starting transfers between devices  20.6 us (21%)
  local copies, waits for them, and re-layouts  5.81 us (6%)
  between operations  0.97 us (1%)
    pallas_call x13, Pallas kernels, call(): pl.pallas_call(body, name=name, grid_spec=pltpu.PrefetchScalarGridSpec(nu...  43.8 us
    ppermute x6, waiting for transfers between devices, ring(): return lax.ppermute(value, 'mp', [(i, (i + step) % n) for i in range(n)])  13.5 us
    ppermute x6, starting transfers between devices, ring(): return lax.ppermute(value, 'mp', [(i, (i + step) % n) for i in range(n)])  10.5 us
    ppermute x7, starting transfers between devices, send(): return lax.ppermute(mixed[2 * s + flip], ('cfg', 'mp'), pairs)  9.4 us
    ppermute x7, waiting for transfers between devices, send(): return lax.ppermute(mixed[2 * s + flip], ('cfg', 'mp'), pairs)  8.02 us
    unnamed x46, local copies, waits for them, and re-layouts  5.73 us
  transfers between devices with their start and end apart: 17, of which 8 were waited for; matrix products, arithmetic and copies ran while one was open for 0% of the time, Pallas kernels for 39%

profile of v3, /device:TPU:0, one launch (start us, length us, event | category | flops | bytes accessed | tf_op | source)
XLA Modules:
  0.0 95.0 jit_solution(6766941132238266501)
XLA Ops:
  0.6 0.8 bitcast_convert_fusion.refs_0_
  1.5 5.0 %collective-permute-start.2 = (bf16[64,256]{1,0:T(8,128)(2,1)S(1)}, bf16[64,256]{1,0:T(8,128)(2,1)S(1)}, u32[]{:S(2)}, u32[]{:S(2)}) collective-permute-start(bf16[64,256]{1,0:T(8,128)(2,1)S(1)} %bitcast_convert_fusion.refs_0_), channel_id=1, source_target_pairs={{0,3},{1,0},{2,1},{3,2},{4,7},{5,4},{6,5},{7,6},{8,11},{9,8},{10,9... | collective-permute-start | bytes 98312 | tf_op jit(solution)/shard_map/ppermute | solution.py:22
  6.5 1.0 %collective-permute-start = (bf16[64,256]{1,0:T(8,128)(2,1)S(1)}, bf16[64,256]{1,0:T(8,128)(2,1)S(1)}, u32[]{:S(2)}, u32[]{:S(2)}) collective-permute-start(bf16[64,256]{1,0:T(8,128)(2,1)S(1)} %bitcast_convert_fusion.refs_0_), channel_id=1, source_target_pairs={{0,1},{1,2},{2,3},{3,0},{4,5},{5,6},{6,7},{7,4},{8,9},{9,10},{10,1... | collective-permute-start | bytes 98312 | tf_op jit(solution)/shard_map/ppermute | solution.py:22
  7.5 2.5 %collective-permute-start.4 = (bf16[128,3072]{1,0:T(8,128)(2,1)}, bf16[128,3072]{1,0:T(8,128)(2,1)S(1)}, u32[]{:S(2)}, u32[]{:S(2)}) collective-permute-start(bf16[128,3072]{1,0:T(8,128)(2,1)} %bitcast.21), channel_id=1, source_target_pairs={{0,1},{1,2},{2,3},{3,0},{4,5},{5,6},{6,7},{7,4},{8,9},{9,10},{10,1... | collective-permute-start | bytes 2359304 | tf_op jit(solution)/shard_map/ppermute | solution.py:22
  10.1 3.0 %copy-done = bf16[3072,1152]{1,0:T(8,128)(2,1)S(1)} copy-done((bf16[3072,1152]{1,0:T(8,128)(2,1)S(1)}, bf16[3072,1152]{1,0:T(8,128)(2,1)}, u32[]{:S(2)}) %copy-start) | copy-done | bytes 7077912
  13.1 1.0 %copy-done.1 = bf16[64,3072]{1,0:T(8,128)(2,1)S(1)} copy-done((bf16[64,3072]{1,0:T(8,128)(2,1)S(1)}, bf16[64,3072]{1,0:T(8,128)(2,1)}, u32[]{:S(2)}) %copy-start.1) | copy-done | bytes 393240
  14.1 1.0 %copy-done.3 = f32[8,3,3072]{2,0,1:T(8,128)S(1)} copy-done((f32[8,3,3072]{2,0,1:T(8,128)S(1)}, f32[8,3,3072]{2,0,1:T(8,128)}, u32[]{:S(2)}) %copy-start.3) | copy-done | bytes 294936
  15.8 5.4 %fold.1 = (bf16[3,2,192,384]{3,2,1,0:T(8,128)(2,1)S(1)}, f32[3,2,8,384]{3,2,1,0:T(8,128)S(1)}) custom-call(s32[7]{0:T(128)S(1)} %stack.15.ids, s32[4]{0:T(128)S(1)} %copy-done.10, bf16[64,3072]{1,0:T(8,128)(2,1)S(1)} %copy-done.1, f32[3,8,3072]{2,1,0:T(8,128)S(1)} %bitcast.16, bf16[3072,1152]{1,0:T(8,128)(2,1)S(1)} %copy-done), custom_call_target="tpu_custom_call" | custom-call | flops 1925185536 | bytes 7077888 | tf_op jit(solution)/shard_map/fold/pallas_call | solution.py:54
  21.2 6.1 %collective-permute-done.1.refs_2_ = bf16[64,256]{1,0:T(8,128)(2,1)S(1)} collective-permute-done((bf16[64,256]{1,0:T(8,128)(2,1)S(1)}, bf16[64,256]{1,0:T(8,128)(2,1)S(1)}, u32[]{:S(2)}, u32[]{:S(2)}) %collective-permute-start.1) | collective-permute-done | bytes 32800 | tf_op jit(solution)/shard_map/ppermute | solution.py:22
  27.3 3.5 %prep.1.lat_ref = bf16[1024,128]{1,0:T(8,128)(2,1)S(1)} custom-call(bf16[64,256]{1,0:T(8,128)(2,1)S(1)} %bitcast_convert_fusion.refs_0_, bf16[64,256]{1,0:T(8,128)(2,1)S(1)} %collective-permute-done.refs_1_, bf16[64,256]{1,0:T(8,128)(2,1)S(1)} %collective-permute-done.1.refs_2_, bf16[64,256]{1,0:T(8,128)(2,1)S(1)} %collective-permute-done.2.refs_3_, ...), custom_call_target="tpu_custom_call" | custom-call | tf_op jit(solution)/shard_map/prep/pallas_call | solution.py:54
  30.9 7.4 %image_own.1 = (bf16[3,1024,128]{2,1,0:T(8,128)(2,1)S(1)}, f32[3,1024,256]{2,1,0:T(8,128)S(1)}) custom-call(s32[7]{0:T(128)S(1)} %stack.15.ids, s32[4]{0:T(128)S(1)} %copy-done.13, bf16[1024,128]{1,0:T(8,128)(2,1)S(1)} %prep.1.lat_ref, bf16[3,2,192,384]{3,2,1,0:T(8,128)(2,1)S(1)} %get-tuple-element.35.mats_ref, ...), custom_call_target="tpu_custom_call" | custom-call | tf_op jit(solution)/shard_map/image_own/pallas_call | solution.py:54
  38.4 6.0 %image_mate.1.acc_ref = f32[3,1024,256]{2,1,0:T(8,128)S(1)} custom-call(s32[7]{0:T(128)S(1)} %stack.15.ids, s32[4]{0:T(128)S(1)} %copy-done.13, s32[2,4]{1,0:T(2,128)S(1)} %copy-done.12, bf16[1024,128]{1,0:T(8,128)(2,1)S(1)} %collective-permute-done.5.lat_ref, bf16[3,2,192,384]{3,2,1,0:T(8,128)(2,1)S(1)} %get-tuple-element.35.mats_ref, ...), custom_call_target="tpu_custom_call" | custom-call | tf_op jit(solution)/shard_map/image_mate/pallas_call | solution.py:54
  44.4 1.0 %collective-permute-done.3.refs_1_ = bf16[128,3072]{1,0:T(8,128)(2,1)S(1)} collective-permute-done((bf16[128,3072]{1,0:T(8,128)(2,1)S(1)}, bf16[128,3072]{1,0:T(8,128)(2,1)S(1)}, u32[]{:S(2)}, u32[]{:S(2)}) %collective-permute-start.3) | collective-permute-done | bytes 786464 | tf_op jit(solution)/shard_map/ppermute | solution.py:22
  45.4 1.9 %collective-permute-start.6 = (bf16[128,3072]{1,0:T(8,128)(2,1)S(1)}, bf16[128,3072]{1,0:T(8,128)(2,1)S(1)}, u32[]{:S(2)}, u32[]{:S(2)}) collective-permute-start(bf16[128,3072]{1,0:T(8,128)(2,1)S(1)} %collective-permute-done.3.refs_1_), channel_id=1, source_target_pairs={{0,3},{1,0},{2,1},{3,2},{4,7},{5,4},{6,5},{7,6},{8,11},{9,8},{10,9... | collective-permute-start | bytes 2359304 | tf_op jit(solution)/shard_map/ppermute | solution.py:22
  47.3 3.0 %text_kv_near.1.own1 = bf16[3,256,256]{2,1,0:T(8,128)(2,1)S(1)} custom-call(s32[7]{0:T(128)S(1)} %stack.15.ids, s32[4]{0:T(128)S(1)} %copy-done.10, bf16[128,3072]{1,0:T(8,128)(2,1)S(1)} %collective-permute-done.4.refs_0_, bf16[128,3072]{1,0:T(8,128)(2,1)S(1)} %collective-permute-done.3.refs_1_, f32[8,2,3072]{2,1,0:T(2,128)S(1)} %copy-done.5, ...), custom_call_target="tpu_custom_call" | custom-call | tf_op jit(solution)/shard_map/text_kv_near/pallas_call | solution.py:54
  50.4 1.9 %text_kv_own.1.own0 = bf16[3,128,256]{2,1,0:T(8,128)(2,1)S(1)} custom-call(s32[7]{0:T(128)S(1)} %stack.15.ids, s32[4]{0:T(128)S(1)} %copy-done.10, bf16[128,3072]{1,0:T(8,128)(2,1)S(1)} %bitcast.23, f32[8,2,3072]{2,1,0:T(2,128)S(1)} %copy-done.5, bf16[3072,768]{1,0:T(8,128)(2,1)S(1)} %bitcast.13, f32[1,128]{1,0:T(1,128)S(1)} %bitcast.29), custom_call_target="tpu_custom_call" | custom-call | flops 603979776 | bytes 4718592 | tf_op jit(solution)/shard_map/text_kv_own/pallas_call | solution.py:54
  52.9 1.6 %out_weights.1 = (bf16[1536,3072]{1,0:T(8,128)(2,1)S(1)}, f32[128,3072]{1,0:T(8,128)S(1)}) custom-call(s32[7]{0:T(128)S(1)} %stack.15.ids, bf16[1536,3072]{1,0:T(8,128)(2,1)S(1)} %bitcast.15, f32[64,256]{1,0:T(8,128)S(1)} %bitcast.24, bf16[64,3072]{1,0:T(8,128)(2,1)S(1)} %copy-done.2), custom_call_target="tpu_custom_call" | custom-call | tf_op jit(solution)/shard_map/out_weights/pallas_call | solution.py:54
  54.6 3.9 %text_attention_near.1.acc_ref = f32[3,1024,256]{2,1,0:T(8,128)S(1)} custom-call(s32[7]{0:T(128)S(1)} %stack.15.ids, s32[4]{0:T(128)S(1)} %copy-done.14, s32[2,4]{1,0:T(2,128)S(1)} %copy-done.12, bf16[3,1024,128]{2,1,0:T(8,128)(2,1)S(1)} %get-tuple-element.37.q_ref, f32[3,1024,256]{2,1,0:T(8,128)S(1)} %image_mate.1.acc_ref, ...), custom_call_target="tpu_custom_call" | custom-call | tf_op jit(solution)/shard_map/text_attention_near/pallas_call | solution.py:54
  58.5 6.4 %collective-permute-done.6.refs_0_ = bf16[128,3072]{1,0:T(8,128)(2,1)S(1)} collective-permute-done((bf16[128,3072]{1,0:T(8,128)(2,1)S(1)}, bf16[128,3072]{1,0:T(8,128)(2,1)S(1)}, u32[]{:S(2)}, u32[]{:S(2)}) %collective-permute-start.6) | collective-permute-done | bytes 786464 | tf_op jit(solution)/shard_map/ppermute | solution.py:22
  64.8 1.9 %text_kv_far.1.own_ref = bf16[3,128,256]{2,1,0:T(8,128)(2,1)S(1)} custom-call(s32[7]{0:T(128)S(1)} %stack.15.ids, s32[4]{0:T(128)S(1)} %copy-done.10, bf16[128,3072]{1,0:T(8,128)(2,1)S(1)} %collective-permute-done.6.refs_0_, f32[8,2,3072]{2,1,0:T(2,128)S(1)} %copy-done.5, bf16[3072,768]{1,0:T(8,128)(2,1)S(1)} %bitcast.13, f32[1,128]{1,0:T(1,128)S(1)} %bitcast.30), custom_call_target="tpu_custom_call" | custom-call | tf_op jit(solution)/shard_map/text_kv_far/pallas_call | solution.py:54
  66.9 1.4 %collective-permute-done.9.mate_ref = bf16[3,128,256]{2,1,0:T(8,128)(2,1)S(1)} collective-permute-done((bf16[3,128,256]{2,1,0:T(8,128)(2,1)S(1)}, bf16[3,128,256]{2,1,0:T(8,128)(2,1)S(1)}, u32[]{:S(2)}, u32[]{:S(2)}) %collective-permute-start.9) | collective-permute-done | bytes 196640 | tf_op jit(solution)/shard_map/ppermute | solution.py:27
  68.3 1.7 %text_attention_far.1 = (bf16[128,384]{1,0:T(8,128)(2,1)S(1)}, bf16[128,384]{1,0:T(8,128)(2,1)S(1)}, bf16[128,384]{1,0:T(8,128)(2,1)S(1)}, bf16[128,384]{1,0:T(8...) custom-call(s32[7]{0:T(128)S(1)} %stack.15.ids, ...), custom_call_target="tpu_custom_call" | custom-call | tf_op jit(solution)/shard_map/text_attention_far/pallas_call | solution.py:54
  70.5 2.7 %collective-permute-start.11 = (bf16[128,384]{1,0:T(8,128)(2,1)S(1)}, bf16[128,384]{1,0:T(8,128)(2,1)S(1)}, u32[]{:S(2)}, u32[]{:S(2)}) collective-permute-start(bf16[128,384]{1,0:T(8,128)(2,1)S(1)} %get-tuple-element.48), channel_id=1, source_target_pairs={{0,3},{1,0},{2,1},{3,2},{16,19},{17,16},{18,17},{19,18},{4,7},{5,4... | collective-permute-start | bytes 294920 | tf_op jit(solution)/shard_map/ppermute | solution.py:418
  73.7 1.7 %collective-permute-start.13 = (bf16[128,384]{1,0:T(8,128)(2,1)S(1)}, bf16[128,384]{1,0:T(8,128)(2,1)S(1)}, u32[]{:S(2)}, u32[]{:S(2)}) collective-permute-start(bf16[128,384]{1,0:T(8,128)(2,1)S(1)} %get-tuple-element.50), channel_id=1, source_target_pairs={{0,1},{1,2},{2,3},{3,0},{16,17},{17,18},{18,19},{19,16},{4,5},{5,6... | collective-permute-start | bytes 294920 | tf_op jit(solution)/shard_map/ppermute | solution.py:418
  76.1 2.4 %collective-permute-start.16 = (bf16[128,384]{1,0:T(8,128)(2,1)S(1)}, bf16[128,384]{1,0:T(8,128)(2,1)S(1)}, u32[]{:S(2)}, u32[]{:S(2)}) collective-permute-start(bf16[128,384]{1,0:T(8,128)(2,1)S(1)} %get-tuple-element.54), channel_id=1, source_target_pairs={{0,2},{1,3},{2,0},{3,1},{16,18},{17,19},{18,16},{19,17},{4,6},{5,7... | collective-permute-start | bytes 294920 | tf_op jit(solution)/shard_map/ppermute | solution.py:418
  78.5 1.0 %collective-permute-start.15 = (bf16[128,384]{1,0:T(8,128)(2,1)S(1)}, bf16[128,384]{1,0:T(8,128)(2,1)S(1)}, u32[]{:S(2)}, u32[]{:S(2)}) collective-permute-start(bf16[128,384]{1,0:T(8,128)(2,1)S(1)} %get-tuple-element.53), channel_id=1, source_target_pairs={{0,18},{1,19},{2,16},{3,17},{16,2},{17,3},{18,0},{19,1},{4,22},{5,... | collective-permute-start | bytes 294920 | tf_op jit(solution)/shard_map/ppermute | solution.py:418
  79.4 2.7 %collective-permute-done.12.refs_3_ = bf16[128,384]{1,0:T(8,128)(2,1)S(1)} collective-permute-done((bf16[128,384]{1,0:T(8,128)(2,1)S(1)}, bf16[128,384]{1,0:T(8,128)(2,1)S(1)}, u32[]{:S(2)}, u32[]{:S(2)}) %collective-permute-start.12) | collective-permute-done | bytes 98336 | tf_op jit(solution)/shard_map/ppermute | solution.py:418
  82.2 1.7 %collective-permute-done.14.refs_5_ = bf16[128,384]{1,0:T(8,128)(2,1)S(1)} collective-permute-done((bf16[128,384]{1,0:T(8,128)(2,1)S(1)}, bf16[128,384]{1,0:T(8,128)(2,1)S(1)}, u32[]{:S(2)}, u32[]{:S(2)}) %collective-permute-start.14) | collective-permute-done | bytes 98336 | tf_op jit(solution)/shard_map/ppermute | solution.py:418
  83.8 2.2 %out_early.1.refs_0_ = f32[256,3072]{1,0:T(8,128)S(1)} custom-call(bf16[128,384]{1,0:T(8,128)(2,1)S(1)} %get-tuple-element.46.refs_0_, bf16[128,384]{1,0:T(8,128)(2,1)S(1)} %collective-permute-done.10.refs_1_, bf16[128,384]{1,0:T(8,128)(2,1)S(1)} %collective-permute-done.11.refs_2_, bf16[128,384]{1,0:T(8,128)(2,1)S(1)} %collective-permute-done.12.refs_3_, ...), custom_call_target="tpu_custom_call" | custom-call | tf_op jit(solution)/shard_map/out_early/pallas_call | solution.py:54
  86.1 3.2 %collective-permute-done.16.refs_1_ = bf16[128,384]{1,0:T(8,128)(2,1)S(1)} collective-permute-done((bf16[128,384]{1,0:T(8,128)(2,1)S(1)}, bf16[128,384]{1,0:T(8,128)(2,1)S(1)}, u32[]{:S(2)}, u32[]{:S(2)}) %collective-permute-start.16) | collective-permute-done | bytes 98336 | tf_op jit(solution)/shard_map/ppermute | solution.py:418
  89.3 2.3 %out_own.1.refs_3_ = f32[64,128]{1,0:T(8,128)S(1)} custom-call(s32[7]{0:T(128)S(1)} %stack.15.ids, s32[4]{0:T(128)S(1)} %copy-done.10, f32[256,3072]{1,0:T(8,128)S(1)} %out_early.1.refs_0_, bf16[128,384]{1,0:T(8,128)(2,1)S(1)} %collective-permute-done.16.refs_1_, bf16[1536,3072]{1,0:T(8,128)(2,1)S(1)} %get-tuple-element.52.refs_6_.refs_2_, ...), custom_call_target="tpu_custom_call" | custom-call | tf_op jit(solution)/shard_map/out_own/pallas_call | solution.py:54
  92.0 2.9 %out_late.1 = (f32[1,64,128]{2,1,0:T(8,128)}, f32[1,64,128]{2,1,0:T(8,128)}) custom-call(s32[7]{0:T(128)S(1)} %stack.15.ids, s32[4]{0:T(128)S(1)} %copy-done.10, s32[4]{0:T(128)S(1)} %copy-done.13, f32[4]{0:T(128)S(1)} %copy-done.15, f32[8]{0:T(128)S(1)} %copy-done.16, f32[256,3072]{1,0:T(8,128)S(1)} %out_early.1.refs_0_, ...), custom_call_target="tpu_custom_call" | custom-call | tf_op jit(solution)/shard_map/out_late/pallas_call | solution.py:54
  (65 shorter events, 3.7 us)
Async XLA Ops:
  1.5 19.7 %collective-permute-start.2 = (bf16[64,256]{1,0:T(8,128)(2,1)S(1)}, bf16[64,256]{1,0:T(8,128)(2,1)S(1)}, u32[]{:S(2)}, u32[]{:S(2)}) collective-permute-start(bf16[64,256]{1,0:T(8,128)(2,1)S(1)} %bitcast_convert_fusion.refs_0_), channel_id=1, source_target_pairs={{0,3},{1,0},{2,1},{3,2},{4,7},{5,4},{6,5},{7,6},{8,11},{9,8},{10,9... | collective-permute-start | bytes 98312 | tf_op jit(solution)/shard_map/ppermute | solution.py:22
  6.5 20.8 %collective-permute-start.1 = (bf16[64,256]{1,0:T(8,128)(2,1)S(1)}, bf16[64,256]{1,0:T(8,128)(2,1)S(1)}, u32[]{:S(2)}, u32[]{:S(2)}) collective-permute-start(bf16[64,256]{1,0:T(8,128)(2,1)S(1)} %bitcast_convert_fusion.refs_0_), channel_id=1, source_target_pairs={{0,2},{1,3},{2,0},{3,1},{4,6},{5,7},{6,4},{7,5},{8,10},{9,11},{10,... | collective-permute-start | bytes 98312 | tf_op jit(solution)/shard_map/ppermute | solution.py:22
  6.5 20.8 %collective-permute-start = (bf16[64,256]{1,0:T(8,128)(2,1)S(1)}, bf16[64,256]{1,0:T(8,128)(2,1)S(1)}, u32[]{:S(2)}, u32[]{:S(2)}) collective-permute-start(bf16[64,256]{1,0:T(8,128)(2,1)S(1)} %bitcast_convert_fusion.refs_0_), channel_id=1, source_target_pairs={{0,1},{1,2},{2,3},{3,0},{4,5},{5,6},{6,7},{7,4},{8,9},{9,10},{10,1... | collective-permute-start | bytes 98312 | tf_op jit(solution)/shard_map/ppermute | solution.py:22
  7.5 36.9 %collective-permute-start.4 = (bf16[128,3072]{1,0:T(8,128)(2,1)}, bf16[128,3072]{1,0:T(8,128)(2,1)S(1)}, u32[]{:S(2)}, u32[]{:S(2)}) collective-permute-start(bf16[128,3072]{1,0:T(8,128)(2,1)} %bitcast.21), channel_id=1, source_target_pairs={{0,1},{1,2},{2,3},{3,0},{4,5},{5,6},{6,7},{7,4},{8,9},{9,10},{10,1... | collective-permute-start | bytes 2359304 | tf_op jit(solution)/shard_map/ppermute | solution.py:22
  15.7 11.6 %copy-start.8 = (bf16[1,128,3072]{2,1,0:T(8,128)(2,1)S(1)}, bf16[1,128,3072]{2,1,0:T(8,128)(2,1)}, u32[]{:S(2)}) copy-start(bf16[1,128,3072]{2,1,0:T(8,128)(2,1)} %param.19) | copy-start | bytes 2359300
  15.7 11.6 %copy-start.2 = (bf16[64,3072]{1,0:T(8,128)(2,1)S(1)}, bf16[64,3072]{1,0:T(8,128)(2,1)}, u32[]{:S(2)}) copy-start(bf16[64,3072]{1,0:T(8,128)(2,1)} %win_ref.3) | copy-start | bytes 1179652
  15.7 15.1 %copy-start.11 = (f32[128]{0:T(128)S(1)}, f32[128]{0:T(128)}, u32[]{:S(2)}) copy-start(f32[128]{0:T(128)} %param.24) | copy-start | bytes 1540
  15.7 15.1 %copy-start.13 = (s32[4]{0:T(128)S(1)}, s32[4]{0:T(128)}, u32[]{:S(2)}) copy-start(s32[4]{0:T(128)} %img_len.5) | copy-start | bytes 52
  15.7 15.1 %copy-start.17 = (f32[128]{0:T(128)S(1)}, f32[128]{0:T(128)}, u32[]{:S(2)}) copy-start(f32[128]{0:T(128)} %param.23) | copy-start | bytes 1540
  15.7 22.6 %copy-start.12 = (s32[2,4]{1,0:T(2,128)S(1)}, s32[2,4]{1,0:T(2,128)}, u32[]{:S(2)}) copy-start(s32[2,4]{1,0:T(2,128)} %flags.5) | copy-start | bytes 100
  27.3 18.1 %collective-permute-start.3 = (bf16[128,3072]{1,0:T(8,128)(2,1)S(1)}, bf16[128,3072]{1,0:T(8,128)(2,1)S(1)}, u32[]{:S(2)}, u32[]{:S(2)}) collective-permute-start(bf16[128,3072]{1,0:T(8,128)(2,1)S(1)} %bitcast.22), channel_id=1, source_target_pairs={{0,3},{1,0},{2,1},{3,2},{4,7},{5,4},{6,5},{7,6},{8,11},{9,8},{10,9... | collective-permute-start | bytes 2359304 | tf_op jit(solution)/shard_map/ppermute | solution.py:22
  30.8 7.5 %collective-permute-start.5 = (bf16[1024,128]{1,0:T(8,128)(2,1)S(1)}, bf16[1024,128]{1,0:T(8,128)(2,1)S(1)}, u32[]{:S(2)}, u32[]{:S(2)}) collective-permute-start(bf16[1024,128]{1,0:T(8,128)(2,1)S(1)} %prep.1.lat_ref), channel_id=1, source_target_pairs={{0,4},{4,0},{8,12},{12,8},{1,5},{5,1},{9,13},{13,9},{2,6},{6,2},{1... | collective-permute-start | bytes 786440 | tf_op jit(solution)/shard_map/ppermute | solution.py:27
  30.9 16.4 %slice-start = ((s8[4718592]{0:T(1024)(128)(4,1)}), s8[4194304]{0:T(1024)(128)(4,1)S(1)}, s32[]{:S(2)}) async-start(s8[4718592]{0:T(1024)(128)(4,1)} %bitcast.12), calls=%async_computation | async-start | bytes 8388608
  30.9 16.4 %copy-start.5 = (f32[8,2,3072]{2,1,0:T(2,128)S(1)}, f32[8,2,3072]{2,1,0:T(2,128)}, u32[]{:S(2)}) copy-start(f32[8,2,3072]{2,1,0:T(2,128)} %refs_1_.3) | copy-start | bytes 589828
  38.4 9.0 %slice-start.1 = ((s8[4718592]{0:T(1024)(128)(4,1)}), s8[524288]{0:T(1024)(128)(4,1)S(1)}, s32[]{:S(2)}) async-start(s8[4718592]{0:T(1024)(128)(4,1)} %bitcast.12), calls=%async_computation.1 | async-start | bytes 1048576
  38.4 14.5 %slice-start.2 = ((s8[9437184]{0:T(1024)(128)(4,1)}), s8[4194304]{0:T(1024)(128)(4,1)S(1)}, s32[]{:S(2)}) async-start(s8[9437184]{0:T(1024)(128)(4,1)} %bitcast.14), calls=%async_computation.2 | async-start | bytes 8388608
  38.4 14.5 %slice-start.3 = ((s8[9437184]{0:T(1024)(128)(4,1)}), s8[4194304]{0:T(1024)(128)(4,1)S(1)}, s32[]{:S(2)}) async-start(s8[9437184]{0:T(1024)(128)(4,1)} %bitcast.14), calls=%async_computation.3 | async-start | bytes 8388608
  44.4 8.5 %slice-start.4 = ((s8[9437184]{0:T(1024)(128)(4,1)}), s8[1048576]{0:T(1024)(128)(4,1)S(1)}, s32[]{:S(2)}) async-start(s8[9437184]{0:T(1024)(128)(4,1)} %bitcast.14), calls=%async_computation.4 | async-start | bytes 2097152
  45.4 19.4 %collective-permute-start.6 = (bf16[128,3072]{1,0:T(8,128)(2,1)S(1)}, bf16[128,3072]{1,0:T(8,128)(2,1)S(1)}, u32[]{:S(2)}, u32[]{:S(2)}) collective-permute-start(bf16[128,3072]{1,0:T(8,128)(2,1)S(1)} %collective-permute-done.3.refs_1_), channel_id=1, source_target_pairs={{0,3},{1,0},{2,1},{3,2},{4,7},{5,4},{6,5},{7,6},{8,11},{9,8},{10,9... | collective-permute-start | bytes 2359304 | tf_op jit(solution)/shard_map/ppermute | solution.py:22
  50.3 4.3 %collective-permute-start.8 = (bf16[3,256,256]{2,1,0:T(8,128)(2,1)S(1)}, bf16[3,256,256]{2,1,0:T(8,128)(2,1)S(1)}, u32[]{:S(2)}, u32[]{:S(2)}) collective-permute-start(bf16[3,256,256]{2,1,0:T(8,128)(2,1)S(1)} %text_kv_near.1.own1), channel_id=1, source_target_pairs={{0,4},{4,0},{8,12},{12,8},{1,5},{5,1},{9,13},{13,9},{2,6},{6,2},{1... | collective-permute-start | bytes 1179656 | tf_op jit(solution)/shard_map/ppermute | solution.py:27
  52.3 2.2 %collective-permute-start.7 = (bf16[3,128,256]{2,1,0:T(8,128)(2,1)S(1)}, bf16[3,128,256]{2,1,0:T(8,128)(2,1)S(1)}, u32[]{:S(2)}, u32[]{:S(2)}) collective-permute-start(bf16[3,128,256]{2,1,0:T(8,128)(2,1)S(1)} %text_kv_own.1.own0), channel_id=1, source_target_pairs={{0,4},{4,0},{8,12},{12,8},{1,5},{5,1},{9,13},{13,9},{2,6},{6,2},{1... | collective-permute-start | bytes 589832 | tf_op jit(solution)/shard_map/ppermute | solution.py:27
  66.8 1.5 %collective-permute-start.9 = (bf16[3,128,256]{2,1,0:T(8,128)(2,1)S(1)}, bf16[3,128,256]{2,1,0:T(8,128)(2,1)S(1)}, u32[]{:S(2)}, u32[]{:S(2)}) collective-permute-start(bf16[3,128,256]{2,1,0:T(8,128)(2,1)S(1)} %text_kv_far.1.own_ref), channel_id=1, source_target_pairs={{0,4},{4,0},{8,12},{12,8},{1,5},{5,1},{9,13},{13,9},{2,6},{6,2},{1... | collective-permute-start | bytes 589832 | tf_op jit(solution)/shard_map/ppermute | solution.py:27
  70.0 6.1 %collective-permute-start.10 = (bf16[128,384]{1,0:T(8,128)(2,1)S(1)}, bf16[128,384]{1,0:T(8,128)(2,1)S(1)}, u32[]{:S(2)}, u32[]{:S(2)}) collective-permute-start(bf16[128,384]{1,0:T(8,128)(2,1)S(1)} %get-tuple-element.47), channel_id=1, source_target_pairs={{0,16},{1,17},{2,18},{3,19},{16,0},{17,1},{18,2},{19,3},{4,20},{5,... | collective-permute-start | bytes 294920 | tf_op jit(solution)/shard_map/ppermute | solution.py:418
  70.5 8.0 %collective-permute-start.11 = (bf16[128,384]{1,0:T(8,128)(2,1)S(1)}, bf16[128,384]{1,0:T(8,128)(2,1)S(1)}, u32[]{:S(2)}, u32[]{:S(2)}) collective-permute-start(bf16[128,384]{1,0:T(8,128)(2,1)S(1)} %get-tuple-element.48), channel_id=1, source_target_pairs={{0,3},{1,0},{2,1},{3,2},{16,19},{17,16},{18,17},{19,18},{4,7},{5,4... | collective-permute-start | bytes 294920 | tf_op jit(solution)/shard_map/ppermute | solution.py:418
  73.2 9.0 %collective-permute-start.12 = (bf16[128,384]{1,0:T(8,128)(2,1)S(1)}, bf16[128,384]{1,0:T(8,128)(2,1)S(1)}, u32[]{:S(2)}, u32[]{:S(2)}) collective-permute-start(bf16[128,384]{1,0:T(8,128)(2,1)S(1)} %get-tuple-element.49), channel_id=1, source_target_pairs={{0,19},{1,16},{2,17},{3,18},{16,3},{17,0},{18,1},{19,2},{4,23},{5,... | collective-permute-start | bytes 294920 | tf_op jit(solution)/shard_map/ppermute | solution.py:418
  73.7 8.4 %collective-permute-start.13 = (bf16[128,384]{1,0:T(8,128)(2,1)S(1)}, bf16[128,384]{1,0:T(8,128)(2,1)S(1)}, u32[]{:S(2)}, u32[]{:S(2)}) collective-permute-start(bf16[128,384]{1,0:T(8,128)(2,1)S(1)} %get-tuple-element.50), channel_id=1, source_target_pairs={{0,1},{1,2},{2,3},{3,0},{16,17},{17,18},{18,19},{19,16},{4,5},{5,6... | collective-permute-start | bytes 294920 | tf_op jit(solution)/shard_map/ppermute | solution.py:418
  75.4 8.4 %collective-permute-start.14 = (bf16[128,384]{1,0:T(8,128)(2,1)S(1)}, bf16[128,384]{1,0:T(8,128)(2,1)S(1)}, u32[]{:S(2)}, u32[]{:S(2)}) collective-permute-start(bf16[128,384]{1,0:T(8,128)(2,1)S(1)} %get-tuple-element.51), channel_id=1, source_target_pairs={{0,17},{1,18},{2,19},{3,16},{16,1},{17,2},{18,3},{19,0},{4,21},{5,... | collective-permute-start | bytes 294920 | tf_op jit(solution)/shard_map/ppermute | solution.py:418
  76.1 13.2 %collective-permute-start.16 = (bf16[128,384]{1,0:T(8,128)(2,1)S(1)}, bf16[128,384]{1,0:T(8,128)(2,1)S(1)}, u32[]{:S(2)}, u32[]{:S(2)}) collective-permute-start(bf16[128,384]{1,0:T(8,128)(2,1)S(1)} %get-tuple-element.54), channel_id=1, source_target_pairs={{0,2},{1,3},{2,0},{3,1},{16,18},{17,19},{18,16},{19,17},{4,6},{5,7... | collective-permute-start | bytes 294920 | tf_op jit(solution)/shard_map/ppermute | solution.py:418
  78.5 13.6 %collective-permute-start.15 = (bf16[128,384]{1,0:T(8,128)(2,1)S(1)}, bf16[128,384]{1,0:T(8,128)(2,1)S(1)}, u32[]{:S(2)}, u32[]{:S(2)}) collective-permute-start(bf16[128,384]{1,0:T(8,128)(2,1)S(1)} %get-tuple-element.53), channel_id=1, source_target_pairs={{0,18},{1,19},{2,16},{3,17},{16,2},{17,3},{18,0},{19,1},{4,22},{5,... | collective-permute-start | bytes 294920 | tf_op jit(solution)/shard_map/ppermute | solution.py:418
  83.8 5.5 %copy-start.4 = (f32[8,3,3072]{2,0,1:T(8,128)S(1)}, f32[8,3,3072]{2,0,1:T(8,128)}, u32[]{:S(2)}) copy-start(f32[8,3,3072]{2,0,1:T(8,128)} %param.27) | copy-start | bytes 884740
  83.8 5.5 %copy-start.6 = (bf16[3072,64]{0,1:T(8,128)(2,1)S(1)}, bf16[3072,64]{0,1:T(8,128)(2,1)}, u32[]{:S(2)}) copy-start(bf16[3072,64]{0,1:T(8,128)(2,1)} %param.26) | copy-start | bytes 1179652
  83.8 5.5 %copy-start.7 = (f32[8,2,3072]{2,1,0:T(2,128)S(1)}, f32[8,2,3072]{2,1,0:T(2,128)}, u32[]{:S(2)}) copy-start(f32[8,2,3072]{2,1,0:T(2,128)} %refs_7_.1) | copy-start | bytes 589828
  (8 other events, 15.4 us)

commit v4 on v3

--- a/solution.py
+++ b/solution.py
@@ -45,7 +45,7 @@
     return lax.dot_general(a, b, (((1,), (1,)), ((), ())), preferred_element_type=F32)
 
 
-FREE = ('prep', 'image_own', 'image_mate', 'text_kv_near', 'text_kv_far', 'text_attention_near', 'text_attention_far', 'out_weights', 'out_own', 'out_early', 'out_late')
+FREE = ('prep', 'image_own', 'image_mate', 'text_kv_near', 'text_kv_far', 'text_attention_near', 'text_attention_far', 'text_attention_rest', 'out_weights', 'out_own', 'out_early', 'out_late')
 
 
 def call(body, name, scalars, grid, in_specs, out_specs, out_shape, scratch, args, flops, nbytes):
@@ -210,7 +210,7 @@
         out_ref[h, :, HD:] = kv[:, 2 * HD * h + HD : 2 * HD * (h + 1)].astype(BF)
 
 
-def text_attend(offsets, shard, n_mp, ids, txt_len, flags, q, acc, own, mate):
+def text_sides(offsets, shard, n_mp, ids, txt_len, flags, own, mate):
     side, group, m = ids[0], ids[1], ids[2]
     length = txt_len[group]
     mate_length = jnp.where(flags[side, group] == 1, txt_len[group ^ 1], 0)
@@ -223,30 +223,33 @@
             values.append(
                 jnp.concatenate([jnp.where(live, v, jnp.zeros_like(v)), live.astype(BF)], axis=1)
             )
-    p = jnp.exp2(dot_t(q, jnp.concatenate(keys, axis=0))).astype(BF)
-    return acc + dot(p, jnp.concatenate(values, axis=0))
+    return jnp.concatenate(keys, axis=0), jnp.concatenate(values, axis=0)
+
+
+def text_attend(q, acc, keys, values):
+    return acc + dot(jnp.exp2(dot_t(q, keys)).astype(BF), values)
 
 
 def near_body(offsets, shard, n_mp, ids, txt_len, flags, q_ref, acc_ref, own0, mate0, own1, mate1, out_ref):
     own = jnp.concatenate([own0[0], own1[0]], axis=0)
     mate = jnp.concatenate([mate0[0], mate1[0]], axis=0)
-    out_ref[0] = text_attend(offsets, shard, n_mp, ids, txt_len, flags, q_ref[0], acc_ref[0], own, mate)
-
-
-def last_body(offsets, shard, n_mp, ids, txt_len, flags, q_ref, acc_ref, own_ref, mate_ref, *out_refs):
+    out_ref[0] = text_attend(
+        q_ref[0], acc_ref[0], *text_sides(offsets, shard, n_mp, ids, txt_len, flags, own, mate)
+    )
+
+
+def last_body(offsets, shard, n_mp, steps, ids, txt_len, flags, q_ref, acc_ref, own_ref, mate_ref, *out_refs):
     rows = q_ref.shape[1] // n_mp
     half = rows // 2
     is_cond = ids[0] == 0
-    for i in range(n_mp):
-        spot = pl.ds(pl.multiple_of(lax.rem(ids[2] + i, n_mp) * rows, rows), rows)
-        for h in range(q_ref.shape[0]):
-            acc = text_attend(
-                offsets, shard, n_mp, ids, txt_len, flags, q_ref[h, spot, :], acc_ref[h, spot, :],
-                own_ref[h], mate_ref[h],
-            )
+    for h in range(q_ref.shape[0]):
+        sides = text_sides(offsets, shard, n_mp, ids, txt_len, flags, own_ref[h], mate_ref[h])
+        columns = slice(h * HD, (h + 1) * HD)
+        for i, step in enumerate(steps):
+            spot = pl.ds(pl.multiple_of(lax.rem(ids[2] + step, n_mp) * rows, rows), rows)
+            acc = text_attend(q_ref[h, spot, :], acc_ref[h, spot, :], *sides)
             mixed = (acc[:, :HD] / acc[:, HD:]).astype(BF)
             low, high = mixed[:half], mixed[half:]
-            columns = slice(h * HD, (h + 1) * HD)
             out_refs[2 * i][:, columns] = jnp.where(is_cond, low, high)
             out_refs[2 * i + 1][:, columns] = jnp.where(is_cond, high, low)
 
@@ -400,24 +403,27 @@
     text_far, acc, rest = lax.optimization_barrier((text_far, acc, rest))
     kv_far = text_kv("text_kv_far", text_far)
     mate_far = partner(kv_far, "group")
-    mixed = call(
-        functools.partial(last_body, (n_mp - 2,), shard, n_mp), "text_attention_far", scalars, (1,),
-        [VMEM] * 4, [VMEM] * (2 * n_mp),
-        [jax.ShapeDtypeStruct((half, depth), BF)] * (2 * n_mp), [],
-        (q, acc, kv_far, mate_far), 2 * heads * full * 2 * shard * 3 * HD, 2**22,
-    )
+    mixed = {}
+    for name, steps in (("text_attention_far", order[1:-1]), ("text_attention_rest", [order[-1], order[0]])):
+        out = call(
+            functools.partial(last_body, (n_mp - 2,), shard, n_mp, steps), name, scalars, (1,),
+            [VMEM] * 4, [VMEM] * (2 * len(steps)),
+            [jax.ShapeDtypeStruct((half, depth), BF)] * (2 * len(steps)), [],
+            (q, acc, kv_far, mate_far), heads * full * 2 * shard * 3 * HD, 2**22,
+        )
+        mixed.update({(s, flip): out[2 * i + flip] for i, s in enumerate(steps) for flip in range(2)})
 
     n_cfg = lax.axis_size("cfg")
 
     def send(s, flip):
         if s == 0 and flip == 0:
-            return mixed[0]
+            return mixed[0, 0]
         pairs = [
             (c * n_mp + i, (c ^ flip) * n_mp + (i + s) % n_mp) for c in range(n_cfg) for i in range(n_mp)
         ]
-        return lax.ppermute(mixed[2 * s + flip], ("cfg", "mp"), pairs)
-
-    pieces = {(s, flip): send(s, flip) for s in order for flip in range(2)}
+        return lax.ppermute(mixed[s, flip], ("cfg", "mp"), pairs)
+
+    pieces = {(s, flip): send(s, flip) for s in order[1:] + order[:1] for flip in range(2)}
     early = [pieces[s, flip] for s in order[:-1] for flip in range(2)]
     total = call(
         early_body, "out_early", (), (1,), [VMEM] * (len(early) + 1), VMEM,

time: 95.9 us -> 93.9 us (0.979)
  waiting for transfers between devices: 22.9 us -> 15.5 us
  starting transfers between devices: 20.6 us -> 25.7 us
    ppermute x7, waiting for transfers between devices: 8.02 us -> 0.67 us  [send(): return lax.ppermute(mixed[s, flip], ('cfg', 'mp'), pairs)]
    ppermute x7, starting transfers between devices: 9.4 us -> 14.5 us  [send(): return lax.ppermute(mixed[s, flip], ('cfg', 'mp'), pairs)]
    pallas_call x13 -> x14, Pallas kernels: 43.8 us -> 44.6 us  [call(): pl.pallas_call(body, name=name, grid_spec=pltpu.PrefetchScalarGridSpec(nu...]
    unnamed x46 -> x48, local copies, waits for them, and re-layouts: 5.73 us -> 5.74 us
  transfers between devices with their start and end apart: 17 -> 17, of which waited for: 8 -> 5; matrix products, arithmetic and copies ran while one was open for 0% -> 0% of each run, Pallas kernels for 39% -> 41%
where the time goes in v4:
time: 93.9 us; the launch traced here: 93.6 us
  Pallas kernels  44.6 us (47%)
  starting transfers between devices  25.7 us (27%)
  waiting for transfers between devices  15.5 us (17%)
  local copies, waits for them, and re-layouts  5.82 us (6%)
  between operations  1.04 us (1%)
    pallas_call x14, Pallas kernels, call(): pl.pallas_call(body, name=name, grid_spec=pltpu.PrefetchScalarGridSpec(nu...  44.6 us
    ppermute x7, starting transfers between devices, send(): return lax.ppermute(mixed[s, flip], ('cfg', 'mp'), pairs)  14.5 us
    ppermute x6, waiting for transfers between devices, ring(): return lax.ppermute(value, 'mp', [(i, (i + step) % n) for i in range(n)])  13.4 us
    ppermute x6, starting transfers between devices, ring(): return lax.ppermute(value, 'mp', [(i, (i + step) % n) for i in range(n)])  10.5 us
    unnamed x48, local copies, waits for them, and re-layouts  5.74 us
  transfers between devices with their start and end apart: 17, of which 5 were waited for; matrix products, arithmetic and copies ran while one was open for 0% of the time, Pallas kernels for 41%

profile of v4, /device:TPU:0, one launch (start us, length us, event | category | flops | bytes accessed | tf_op | source)
XLA Modules:
  0.0 93.6 jit_solution(2476686772783522313)
XLA Ops:
  0.6 0.8 bitcast_convert_fusion.refs_0_
  1.5 5.0 %collective-permute-start.2 = (bf16[64,256]{1,0:T(8,128)(2,1)S(1)}, bf16[64,256]{1,0:T(8,128)(2,1)S(1)}, u32[]{:S(2)}, u32[]{:S(2)}) collective-permute-start(bf16[64,256]{1,0:T(8,128)(2,1)S(1)} %bitcast_convert_fusion.refs_0_), channel_id=1, source_target_pairs={{0,3},{1,0},{2,1},{3,2},{4,7},{5,4},{6,5},{7,6},{8,11},{9,8},{10,9... | collective-permute-start | bytes 98312 | tf_op jit(solution)/shard_map/ppermute | solution.py:22
  6.5 1.0 %collective-permute-start = (bf16[64,256]{1,0:T(8,128)(2,1)S(1)}, bf16[64,256]{1,0:T(8,128)(2,1)S(1)}, u32[]{:S(2)}, u32[]{:S(2)}) collective-permute-start(bf16[64,256]{1,0:T(8,128)(2,1)S(1)} %bitcast_convert_fusion.refs_0_), channel_id=1, source_target_pairs={{0,1},{1,2},{2,3},{3,0},{4,5},{5,6},{6,7},{7,4},{8,9},{9,10},{10,1... | collective-permute-start | bytes 98312 | tf_op jit(solution)/shard_map/ppermute | solution.py:22
  7.5 2.5 %collective-permute-start.4 = (bf16[128,3072]{1,0:T(8,128)(2,1)}, bf16[128,3072]{1,0:T(8,128)(2,1)S(1)}, u32[]{:S(2)}, u32[]{:S(2)}) collective-permute-start(bf16[128,3072]{1,0:T(8,128)(2,1)} %bitcast.21), channel_id=1, source_target_pairs={{0,1},{1,2},{2,3},{3,0},{4,5},{5,6},{6,7},{7,4},{8,9},{9,10},{10,1... | collective-permute-start | bytes 2359304 | tf_op jit(solution)/shard_map/ppermute | solution.py:22
  10.1 3.0 %copy-done = bf16[3072,1152]{1,0:T(8,128)(2,1)S(1)} copy-done((bf16[3072,1152]{1,0:T(8,128)(2,1)S(1)}, bf16[3072,1152]{1,0:T(8,128)(2,1)}, u32[]{:S(2)}) %copy-start) | copy-done | bytes 7077912
  13.1 1.0 %copy-done.1 = bf16[64,3072]{1,0:T(8,128)(2,1)S(1)} copy-done((bf16[64,3072]{1,0:T(8,128)(2,1)S(1)}, bf16[64,3072]{1,0:T(8,128)(2,1)}, u32[]{:S(2)}) %copy-start.1) | copy-done | bytes 393240
  14.1 1.0 %copy-done.3 = f32[8,3,3072]{2,0,1:T(8,128)S(1)} copy-done((f32[8,3,3072]{2,0,1:T(8,128)S(1)}, f32[8,3,3072]{2,0,1:T(8,128)}, u32[]{:S(2)}) %copy-start.3) | copy-done | bytes 294936
  15.8 5.4 %fold.1 = (bf16[3,2,192,384]{3,2,1,0:T(8,128)(2,1)S(1)}, f32[3,2,8,384]{3,2,1,0:T(8,128)S(1)}) custom-call(s32[7]{0:T(128)S(1)} %stack.15.ids, s32[4]{0:T(128)S(1)} %copy-done.10, bf16[64,3072]{1,0:T(8,128)(2,1)S(1)} %copy-done.1, f32[3,8,3072]{2,1,0:T(8,128)S(1)} %bitcast.16, bf16[3072,1152]{1,0:T(8,128)(2,1)S(1)} %copy-done), custom_call_target="tpu_custom_call" | custom-call | flops 1925185536 | bytes 7077888 | tf_op jit(solution)/shard_map/fold/pallas_call | solution.py:54
  21.2 6.1 %collective-permute-done.1.refs_2_ = bf16[64,256]{1,0:T(8,128)(2,1)S(1)} collective-permute-done((bf16[64,256]{1,0:T(8,128)(2,1)S(1)}, bf16[64,256]{1,0:T(8,128)(2,1)S(1)}, u32[]{:S(2)}, u32[]{:S(2)}) %collective-permute-start.1) | collective-permute-done | bytes 32800 | tf_op jit(solution)/shard_map/ppermute | solution.py:22
  27.3 3.5 %prep.1.lat_ref = bf16[1024,128]{1,0:T(8,128)(2,1)S(1)} custom-call(bf16[64,256]{1,0:T(8,128)(2,1)S(1)} %bitcast_convert_fusion.refs_0_, bf16[64,256]{1,0:T(8,128)(2,1)S(1)} %collective-permute-done.refs_1_, bf16[64,256]{1,0:T(8,128)(2,1)S(1)} %collective-permute-done.1.refs_2_, bf16[64,256]{1,0:T(8,128)(2,1)S(1)} %collective-permute-done.2.refs_3_, ...), custom_call_target="tpu_custom_call" | custom-call | tf_op jit(solution)/shard_map/prep/pallas_call | solution.py:54
  30.9 7.4 %image_own.1 = (bf16[3,1024,128]{2,1,0:T(8,128)(2,1)S(1)}, f32[3,1024,256]{2,1,0:T(8,128)S(1)}) custom-call(s32[7]{0:T(128)S(1)} %stack.15.ids, s32[4]{0:T(128)S(1)} %copy-done.14, bf16[1024,128]{1,0:T(8,128)(2,1)S(1)} %prep.1.lat_ref, bf16[3,2,192,384]{3,2,1,0:T(8,128)(2,1)S(1)} %get-tuple-element.35.mats_ref, ...), custom_call_target="tpu_custom_call" | custom-call | tf_op jit(solution)/shard_map/image_own/pallas_call | solution.py:54
  38.4 6.0 %image_mate.1.acc_ref = f32[3,1024,256]{2,1,0:T(8,128)S(1)} custom-call(s32[7]{0:T(128)S(1)} %stack.15.ids, s32[4]{0:T(128)S(1)} %copy-done.14, s32[2,4]{1,0:T(2,128)S(1)} %copy-done.12, bf16[1024,128]{1,0:T(8,128)(2,1)S(1)} %collective-permute-done.5.lat_ref, bf16[3,2,192,384]{3,2,1,0:T(8,128)(2,1)S(1)} %get-tuple-element.35.mats_ref, ...), custom_call_target="tpu_custom_call" | custom-call | tf_op jit(solution)/shard_map/image_mate/pallas_call | solution.py:54
  44.4 1.0 %collective-permute-done.3.refs_1_ = bf16[128,3072]{1,0:T(8,128)(2,1)S(1)} collective-permute-done((bf16[128,3072]{1,0:T(8,128)(2,1)S(1)}, bf16[128,3072]{1,0:T(8,128)(2,1)S(1)}, u32[]{:S(2)}, u32[]{:S(2)}) %collective-permute-start.3) | collective-permute-done | bytes 786464 | tf_op jit(solution)/shard_map/ppermute | solution.py:22
  45.4 1.9 %collective-permute-start.6 = (bf16[128,3072]{1,0:T(8,128)(2,1)S(1)}, bf16[128,3072]{1,0:T(8,128)(2,1)S(1)}, u32[]{:S(2)}, u32[]{:S(2)}) collective-permute-start(bf16[128,3072]{1,0:T(8,128)(2,1)S(1)} %collective-permute-done.3.refs_1_), channel_id=1, source_target_pairs={{0,3},{1,0},{2,1},{3,2},{4,7},{5,4},{6,5},{7,6},{8,11},{9,8},{10,9... | collective-permute-start | bytes 2359304 | tf_op jit(solution)/shard_map/ppermute | solution.py:22
  47.3 3.0 %text_kv_near.1.own1 = bf16[3,256,256]{2,1,0:T(8,128)(2,1)S(1)} custom-call(s32[7]{0:T(128)S(1)} %stack.15.ids, s32[4]{0:T(128)S(1)} %copy-done.11, bf16[128,3072]{1,0:T(8,128)(2,1)S(1)} %collective-permute-done.4.refs_0_, bf16[128,3072]{1,0:T(8,128)(2,1)S(1)} %collective-permute-done.3.refs_1_, f32[8,2,3072]{2,1,0:T(2,128)S(1)} %copy-done.5, ...), custom_call_target="tpu_custom_call" | custom-call | tf_op jit(solution)/shard_map/text_kv_near/pallas_call | solution.py:54
  50.4 1.9 %text_kv_own.1.own0 = bf16[3,128,256]{2,1,0:T(8,128)(2,1)S(1)} custom-call(s32[7]{0:T(128)S(1)} %stack.15.ids, s32[4]{0:T(128)S(1)} %copy-done.11, bf16[128,3072]{1,0:T(8,128)(2,1)S(1)} %bitcast.23, f32[8,2,3072]{2,1,0:T(2,128)S(1)} %copy-done.5, bf16[3072,768]{1,0:T(8,128)(2,1)S(1)} %bitcast.13, f32[1,128]{1,0:T(1,128)S(1)} %bitcast.29), custom_call_target="tpu_custom_call" | custom-call | flops 603979776 | bytes 4718592 | tf_op jit(solution)/shard_map/text_kv_own/pallas_call | solution.py:54
  52.9 1.6 %out_weights.1 = (bf16[1536,3072]{1,0:T(8,128)(2,1)S(1)}, f32[128,3072]{1,0:T(8,128)S(1)}) custom-call(s32[7]{0:T(128)S(1)} %stack.15.ids, bf16[1536,3072]{1,0:T(8,128)(2,1)S(1)} %bitcast.15, f32[64,256]{1,0:T(8,128)S(1)} %bitcast.24, bf16[64,3072]{1,0:T(8,128)(2,1)S(1)} %copy-done.2), custom_call_target="tpu_custom_call" | custom-call | tf_op jit(solution)/shard_map/out_weights/pallas_call | solution.py:54
  54.6 3.9 %text_attention_near.1.acc_ref = f32[3,1024,256]{2,1,0:T(8,128)S(1)} custom-call(s32[7]{0:T(128)S(1)} %stack.15.ids, s32[4]{0:T(128)S(1)} %copy-done.15, s32[2,4]{1,0:T(2,128)S(1)} %copy-done.12, bf16[3,1024,128]{2,1,0:T(8,128)(2,1)S(1)} %get-tuple-element.37.q_ref, f32[3,1024,256]{2,1,0:T(8,128)S(1)} %image_mate.1.acc_ref, ...), custom_call_target="tpu_custom_call" | custom-call | tf_op jit(solution)/shard_map/text_attention_near/pallas_call | solution.py:54
  58.5 6.3 %collective-permute-done.6.refs_0_ = bf16[128,3072]{1,0:T(8,128)(2,1)S(1)} collective-permute-done((bf16[128,3072]{1,0:T(8,128)(2,1)S(1)}, bf16[128,3072]{1,0:T(8,128)(2,1)S(1)}, u32[]{:S(2)}, u32[]{:S(2)}) %collective-permute-start.6) | collective-permute-done | bytes 786464 | tf_op jit(solution)/shard_map/ppermute | solution.py:22
  64.9 1.9 %text_kv_far.1.own_ref = bf16[3,128,256]{2,1,0:T(8,128)(2,1)S(1)} custom-call(s32[7]{0:T(128)S(1)} %stack.15.ids, s32[4]{0:T(128)S(1)} %copy-done.11, bf16[128,3072]{1,0:T(8,128)(2,1)S(1)} %collective-permute-done.6.refs_0_, f32[8,2,3072]{2,1,0:T(2,128)S(1)} %copy-done.5, bf16[3072,768]{1,0:T(8,128)(2,1)S(1)} %bitcast.13, f32[1,128]{1,0:T(1,128)S(1)} %bitcast.30), custom_call_target="tpu_custom_call" | custom-call | tf_op jit(solution)/shard_map/text_kv_far/pallas_call | solution.py:54
  66.9 1.4 %collective-permute-done.9.mate_ref = bf16[3,128,256]{2,1,0:T(8,128)(2,1)S(1)} collective-permute-done((bf16[3,128,256]{2,1,0:T(8,128)(2,1)S(1)}, bf16[3,128,256]{2,1,0:T(8,128)(2,1)S(1)}, u32[]{:S(2)}, u32[]{:S(2)}) %collective-permute-start.9) | collective-permute-done | bytes 196640 | tf_op jit(solution)/shard_map/ppermute | solution.py:27
  68.3 1.3 %text_attention_far.1 = (bf16[128,384]{1,0:T(8,128)(2,1)S(1)}, bf16[128,384]{1,0:T(8,128)(2,1)S(1)}, bf16[128,384]{1,0:T(8,128)(2,1)S(1)}, bf16[128,384]{1,0:T(8,128)(2,1)S(1)}) custom-call(s32[7]{0:T(128)S(1)} %stack.15.ids, s32[4]{0:T(128)S(1)} %copy-done.15, s32[2,4]{1,0:T(2,128)S(1)} %copy-done.12, bf16[3,1024,128]{2,1,0:T(8,128)(2,1)S(1)} %get-tuple-element.37.q_ref, ...), custom_call_target="tpu_custom_call" | custom-call | tf_op jit(solution)/shard_map/text_attention_far/pallas_call | solution.py:54
  69.6 1.9 %collective-permute-start.11 = (bf16[128,384]{1,0:T(8,128)(2,1)S(1)}, bf16[128,384]{1,0:T(8,128)(2,1)S(1)}, u32[]{:S(2)}, u32[]{:S(2)}) collective-permute-start(bf16[128,384]{1,0:T(8,128)(2,1)S(1)} %get-tuple-element.48), channel_id=1, source_target_pairs={{0,3},{1,0},{2,1},{3,2},{16,19},{17,16},{18,17},{19,18},{4,7},{5,4... | collective-permute-start | bytes 294920 | tf_op jit(solution)/shard_map/ppermute | solution.py:424
  71.5 1.3 %collective-permute-start.12 = (bf16[128,384]{1,0:T(8,128)(2,1)S(1)}, bf16[128,384]{1,0:T(8,128)(2,1)S(1)}, u32[]{:S(2)}, u32[]{:S(2)}) collective-permute-start(bf16[128,384]{1,0:T(8,128)(2,1)S(1)} %get-tuple-element.49), channel_id=1, source_target_pairs={{0,19},{1,16},{2,17},{3,18},{16,3},{17,0},{18,1},{19,2},{4,23},{5,... | collective-permute-start | bytes 294920 | tf_op jit(solution)/shard_map/ppermute | solution.py:424
  72.8 1.7 %collective-permute-start.13 = (bf16[128,384]{1,0:T(8,128)(2,1)S(1)}, bf16[128,384]{1,0:T(8,128)(2,1)S(1)}, u32[]{:S(2)}, u32[]{:S(2)}) collective-permute-start(bf16[128,384]{1,0:T(8,128)(2,1)S(1)} %get-tuple-element.50), channel_id=1, source_target_pairs={{0,1},{1,2},{2,3},{3,0},{16,17},{17,18},{18,19},{19,16},{4,5},{5,6... | collective-permute-start | bytes 294920 | tf_op jit(solution)/shard_map/ppermute | solution.py:424
  74.6 1.3 %text_attention_rest.1 = (bf16[128,384]{1,0:T(8,128)(2,1)S(1)}, bf16[128,384]{1,0:T(8,128)(2,1)S(1)}, bf16[128,384]{1,0:T(8,128)(2,1)S(1)}, bf16[128,384]{1,0:T(8,128)(2,1)S(1)}) custom-call(s32[7]{0:T(128)S(1)} %stack.15.ids, s32[4]{0:T(128)S(1)} %copy-done.15, s32[2,4]{1,0:T(2,128)S(1)} %copy-done.12, bf16[3,1024,128]{2,1,0:T(8,128)(2,1)S(1)} %get-tuple-element.37.q_ref, ...), custom_call_target="tpu_custom_call" | custom-call | tf_op jit(solution)/shard_map/text_attention_rest/pallas_call | solution.py:54
  75.9 1.6 %collective-permute-start.10 = (bf16[128,384]{1,0:T(8,128)(2,1)S(1)}, bf16[128,384]{1,0:T(8,128)(2,1)S(1)}, u32[]{:S(2)}, u32[]{:S(2)}) collective-permute-start(bf16[128,384]{1,0:T(8,128)(2,1)S(1)} %get-tuple-element.47), channel_id=1, source_target_pairs={{0,16},{1,17},{2,18},{3,19},{16,0},{17,1},{18,2},{19,3},{4,20},{5,... | collective-permute-start | bytes 294920 | tf_op jit(solution)/shard_map/ppermute | solution.py:424
  77.4 2.5 %collective-permute-start.16 = (bf16[128,384]{1,0:T(8,128)(2,1)S(1)}, bf16[128,384]{1,0:T(8,128)(2,1)S(1)}, u32[]{:S(2)}, u32[]{:S(2)}) collective-permute-start(bf16[128,384]{1,0:T(8,128)(2,1)S(1)} %get-tuple-element.54), channel_id=1, source_target_pairs={{0,2},{1,3},{2,0},{3,1},{16,18},{17,19},{18,16},{19,17},{4,6},{5,7... | collective-permute-start | bytes 294920 | tf_op jit(solution)/shard_map/ppermute | solution.py:424
  80.0 5.4 %collective-permute-start.15 = (bf16[128,384]{1,0:T(8,128)(2,1)S(1)}, bf16[128,384]{1,0:T(8,128)(2,1)S(1)}, u32[]{:S(2)}, u32[]{:S(2)}) collective-permute-start(bf16[128,384]{1,0:T(8,128)(2,1)S(1)} %get-tuple-element.53), channel_id=1, source_target_pairs={{0,18},{1,19},{2,16},{3,17},{16,2},{17,3},{18,0},{19,1},{4,22},{5,... | collective-permute-start | bytes 294920 | tf_op jit(solution)/shard_map/ppermute | solution.py:424
  85.4 2.2 %out_early.1.refs_0_ = f32[256,3072]{1,0:T(8,128)S(1)} custom-call(bf16[128,384]{1,0:T(8,128)(2,1)S(1)} %get-tuple-element.46.refs_0_, bf16[128,384]{1,0:T(8,128)(2,1)S(1)} %collective-permute-done.10.refs_1_, bf16[128,384]{1,0:T(8,128)(2,1)S(1)} %collective-permute-done.11.refs_2_, bf16[128,384]{1,0:T(8,128)(2,1)S(1)} %collective-permute-done.12.refs_3_, ...), custom_call_target="tpu_custom_call" | custom-call | tf_op jit(solution)/shard_map/out_early/pallas_call | solution.py:54
  88.4 2.3 %out_own.1.refs_3_ = f32[64,128]{1,0:T(8,128)S(1)} custom-call(s32[7]{0:T(128)S(1)} %stack.15.ids, s32[4]{0:T(128)S(1)} %copy-done.11, f32[256,3072]{1,0:T(8,128)S(1)} %out_early.1.refs_0_, bf16[128,384]{1,0:T(8,128)(2,1)S(1)} %collective-permute-done.16.refs_1_, bf16[1536,3072]{1,0:T(8,128)(2,1)S(1)} %get-tuple-element.52.refs_6_.refs_2_, ...), custom_call_target="tpu_custom_call" | custom-call | tf_op jit(solution)/shard_map/out_own/pallas_call | solution.py:54
  90.7 2.9 %out_late.1 = (f32[1,64,128]{2,1,0:T(8,128)}, f32[1,64,128]{2,1,0:T(8,128)}) custom-call(s32[7]{0:T(128)S(1)} %stack.15.ids, s32[4]{0:T(128)S(1)} %copy-done.11, s32[4]{0:T(128)S(1)} %copy-done.14, f32[4]{0:T(128)S(1)} %copy-done.16, f32[8]{0:T(128)S(1)} %copy-done.17, f32[256,3072]{1,0:T(8,128)S(1)} %out_early.1.refs_0_, ...), custom_call_target="tpu_custom_call" | custom-call | tf_op jit(solution)/shard_map/out_late/pallas_call | solution.py:54
  (68 shorter events, 2.4 us)
Async XLA Ops:
  1.5 19.7 %collective-permute-start.2 = (bf16[64,256]{1,0:T(8,128)(2,1)S(1)}, bf16[64,256]{1,0:T(8,128)(2,1)S(1)}, u32[]{:S(2)}, u32[]{:S(2)}) collective-permute-start(bf16[64,256]{1,0:T(8,128)(2,1)S(1)} %bitcast_convert_fusion.refs_0_), channel_id=1, source_target_pairs={{0,3},{1,0},{2,1},{3,2},{4,7},{5,4},{6,5},{7,6},{8,11},{9,8},{10,9... | collective-permute-start | bytes 98312 | tf_op jit(solution)/shard_map/ppermute | solution.py:22
  6.5 20.8 %collective-permute-start.1 = (bf16[64,256]{1,0:T(8,128)(2,1)S(1)}, bf16[64,256]{1,0:T(8,128)(2,1)S(1)}, u32[]{:S(2)}, u32[]{:S(2)}) collective-permute-start(bf16[64,256]{1,0:T(8,128)(2,1)S(1)} %bitcast_convert_fusion.refs_0_), channel_id=1, source_target_pairs={{0,2},{1,3},{2,0},{3,1},{4,6},{5,7},{6,4},{7,5},{8,10},{9,11},{10,... | collective-permute-start | bytes 98312 | tf_op jit(solution)/shard_map/ppermute | solution.py:22
  6.5 20.8 %collective-permute-start = (bf16[64,256]{1,0:T(8,128)(2,1)S(1)}, bf16[64,256]{1,0:T(8,128)(2,1)S(1)}, u32[]{:S(2)}, u32[]{:S(2)}) collective-permute-start(bf16[64,256]{1,0:T(8,128)(2,1)S(1)} %bitcast_convert_fusion.refs_0_), channel_id=1, source_target_pairs={{0,1},{1,2},{2,3},{3,0},{4,5},{5,6},{6,7},{7,4},{8,9},{9,10},{10,1... | collective-permute-start | bytes 98312 | tf_op jit(solution)/shard_map/ppermute | solution.py:22
  7.5 36.9 %collective-permute-start.4 = (bf16[128,3072]{1,0:T(8,128)(2,1)}, bf16[128,3072]{1,0:T(8,128)(2,1)S(1)}, u32[]{:S(2)}, u32[]{:S(2)}) collective-permute-start(bf16[128,3072]{1,0:T(8,128)(2,1)} %bitcast.21), channel_id=1, source_target_pairs={{0,1},{1,2},{2,3},{3,0},{4,5},{5,6},{6,7},{7,4},{8,9},{9,10},{10,1... | collective-permute-start | bytes 2359304 | tf_op jit(solution)/shard_map/ppermute | solution.py:22
  10.1 3.0 %copy-start = (bf16[3072,1152]{1,0:T(8,128)(2,1)S(1)}, bf16[3072,1152]{1,0:T(8,128)(2,1)}, u32[]{:S(2)}) copy-start(bf16[3072,1152]{1,0:T(8,128)(2,1)} %w_ref.2) | copy-start | bytes 21233668
  15.7 11.6 %copy-start.8 = (bf16[1,128,3072]{2,1,0:T(8,128)(2,1)S(1)}, bf16[1,128,3072]{2,1,0:T(8,128)(2,1)}, u32[]{:S(2)}) copy-start(bf16[1,128,3072]{2,1,0:T(8,128)(2,1)} %param.19) | copy-start | bytes 2359300
  15.7 11.6 %copy-start.2 = (bf16[64,3072]{1,0:T(8,128)(2,1)S(1)}, bf16[64,3072]{1,0:T(8,128)(2,1)}, u32[]{:S(2)}) copy-start(bf16[64,3072]{1,0:T(8,128)(2,1)} %win_ref.3) | copy-start | bytes 1179652
  15.7 15.1 %copy-start.13 = (f32[128]{0:T(128)S(1)}, f32[128]{0:T(128)}, u32[]{:S(2)}) copy-start(f32[128]{0:T(128)} %param.24) | copy-start | bytes 1540
  15.7 15.2 %copy-start.14 = (s32[4]{0:T(128)S(1)}, s32[4]{0:T(128)}, u32[]{:S(2)}) copy-start(s32[4]{0:T(128)} %img_len.5) | copy-start | bytes 52
  15.7 15.2 %copy-start.18 = (f32[128]{0:T(128)S(1)}, f32[128]{0:T(128)}, u32[]{:S(2)}) copy-start(f32[128]{0:T(128)} %param.23) | copy-start | bytes 1540
  15.7 22.6 %copy-start.12 = (s32[2,4]{1,0:T(2,128)S(1)}, s32[2,4]{1,0:T(2,128)}, u32[]{:S(2)}) copy-start(s32[2,4]{1,0:T(2,128)} %flags.7) | copy-start | bytes 100
  27.3 18.1 %collective-permute-start.3 = (bf16[128,3072]{1,0:T(8,128)(2,1)S(1)}, bf16[128,3072]{1,0:T(8,128)(2,1)S(1)}, u32[]{:S(2)}, u32[]{:S(2)}) collective-permute-start(bf16[128,3072]{1,0:T(8,128)(2,1)S(1)} %bitcast.22), channel_id=1, source_target_pairs={{0,3},{1,0},{2,1},{3,2},{4,7},{5,4},{6,5},{7,6},{8,11},{9,8},{10,9... | collective-permute-start | bytes 2359304 | tf_op jit(solution)/shard_map/ppermute | solution.py:22
  30.8 7.5 %collective-permute-start.5 = (bf16[1024,128]{1,0:T(8,128)(2,1)S(1)}, bf16[1024,128]{1,0:T(8,128)(2,1)S(1)}, u32[]{:S(2)}, u32[]{:S(2)}) collective-permute-start(bf16[1024,128]{1,0:T(8,128)(2,1)S(1)} %prep.1.lat_ref), channel_id=1, source_target_pairs={{0,4},{4,0},{8,12},{12,8},{1,5},{5,1},{9,13},{13,9},{2,6},{6,2},{1... | collective-permute-start | bytes 786440 | tf_op jit(solution)/shard_map/ppermute | solution.py:27
  30.9 16.4 %slice-start = ((s8[4718592]{0:T(1024)(128)(4,1)}), s8[4194304]{0:T(1024)(128)(4,1)S(1)}, s32[]{:S(2)}) async-start(s8[4718592]{0:T(1024)(128)(4,1)} %bitcast.12), calls=%async_computation | async-start | bytes 8388608
  30.9 16.4 %copy-start.5 = (f32[8,2,3072]{2,1,0:T(2,128)S(1)}, f32[8,2,3072]{2,1,0:T(2,128)}, u32[]{:S(2)}) copy-start(f32[8,2,3072]{2,1,0:T(2,128)} %refs_1_.3) | copy-start | bytes 589828
  30.9 16.4 %copy-start.11 = (s32[4]{0:T(128)S(1)}, s32[4]{0:T(128)}, u32[]{:S(2)}) copy-start(s32[4]{0:T(128)} %tstep.11) | copy-start | bytes 52
  38.4 8.9 %slice-start.1 = ((s8[4718592]{0:T(1024)(128)(4,1)}), s8[524288]{0:T(1024)(128)(4,1)S(1)}, s32[]{:S(2)}) async-start(s8[4718592]{0:T(1024)(128)(4,1)} %bitcast.12), calls=%async_computation.1 | async-start | bytes 1048576
  38.4 14.5 %slice-start.2 = ((s8[9437184]{0:T(1024)(128)(4,1)}), s8[4194304]{0:T(1024)(128)(4,1)S(1)}, s32[]{:S(2)}) async-start(s8[9437184]{0:T(1024)(128)(4,1)} %bitcast.14), calls=%async_computation.2 | async-start | bytes 8388608
  38.4 14.5 %slice-start.3 = ((s8[9437184]{0:T(1024)(128)(4,1)}), s8[4194304]{0:T(1024)(128)(4,1)S(1)}, s32[]{:S(2)}) async-start(s8[9437184]{0:T(1024)(128)(4,1)} %bitcast.14), calls=%async_computation.3 | async-start | bytes 8388608
  44.4 8.5 %slice-start.4 = ((s8[9437184]{0:T(1024)(128)(4,1)}), s8[1048576]{0:T(1024)(128)(4,1)S(1)}, s32[]{:S(2)}) async-start(s8[9437184]{0:T(1024)(128)(4,1)} %bitcast.14), calls=%async_computation.4 | async-start | bytes 2097152
  45.4 19.5 %collective-permute-start.6 = (bf16[128,3072]{1,0:T(8,128)(2,1)S(1)}, bf16[128,3072]{1,0:T(8,128)(2,1)S(1)}, u32[]{:S(2)}, u32[]{:S(2)}) collective-permute-start(bf16[128,3072]{1,0:T(8,128)(2,1)S(1)} %collective-permute-done.3.refs_1_), channel_id=1, source_target_pairs={{0,3},{1,0},{2,1},{3,2},{4,7},{5,4},{6,5},{7,6},{8,11},{9,8},{10,9... | collective-permute-start | bytes 2359304 | tf_op jit(solution)/shard_map/ppermute | solution.py:22
  50.3 4.3 %collective-permute-start.8 = (bf16[3,256,256]{2,1,0:T(8,128)(2,1)S(1)}, bf16[3,256,256]{2,1,0:T(8,128)(2,1)S(1)}, u32[]{:S(2)}, u32[]{:S(2)}) collective-permute-start(bf16[3,256,256]{2,1,0:T(8,128)(2,1)S(1)} %text_kv_near.1.own1), channel_id=1, source_target_pairs={{0,4},{4,0},{8,12},{12,8},{1,5},{5,1},{9,13},{13,9},{2,6},{6,2},{1... | collective-permute-start | bytes 1179656 | tf_op jit(solution)/shard_map/ppermute | solution.py:27
  52.4 2.2 %collective-permute-start.7 = (bf16[3,128,256]{2,1,0:T(8,128)(2,1)S(1)}, bf16[3,128,256]{2,1,0:T(8,128)(2,1)S(1)}, u32[]{:S(2)}, u32[]{:S(2)}) collective-permute-start(bf16[3,128,256]{2,1,0:T(8,128)(2,1)S(1)} %text_kv_own.1.own0), channel_id=1, source_target_pairs={{0,4},{4,0},{8,12},{12,8},{1,5},{5,1},{9,13},{13,9},{2,6},{6,2},{1... | collective-permute-start | bytes 589832 | tf_op jit(solution)/shard_map/ppermute | solution.py:27
  66.8 1.5 %collective-permute-start.9 = (bf16[3,128,256]{2,1,0:T(8,128)(2,1)S(1)}, bf16[3,128,256]{2,1,0:T(8,128)(2,1)S(1)}, u32[]{:S(2)}, u32[]{:S(2)}) collective-permute-start(bf16[3,128,256]{2,1,0:T(8,128)(2,1)S(1)} %text_kv_far.1.own_ref), channel_id=1, source_target_pairs={{0,4},{4,0},{8,12},{12,8},{1,5},{5,1},{9,13},{13,9},{2,6},{6,2},{1... | collective-permute-start | bytes 589832 | tf_op jit(solution)/shard_map/ppermute | solution.py:27
  69.6 7.9 %collective-permute-start.11 = (bf16[128,384]{1,0:T(8,128)(2,1)S(1)}, bf16[128,384]{1,0:T(8,128)(2,1)S(1)}, u32[]{:S(2)}, u32[]{:S(2)}) collective-permute-start(bf16[128,384]{1,0:T(8,128)(2,1)S(1)} %get-tuple-element.48), channel_id=1, source_target_pairs={{0,3},{1,0},{2,1},{3,2},{16,19},{17,16},{18,17},{19,18},{4,7},{5,4... | collective-permute-start | bytes 294920 | tf_op jit(solution)/shard_map/ppermute | solution.py:424
  71.5 8.5 %collective-permute-start.12 = (bf16[128,384]{1,0:T(8,128)(2,1)S(1)}, bf16[128,384]{1,0:T(8,128)(2,1)S(1)}, u32[]{:S(2)}, u32[]{:S(2)}) collective-permute-start(bf16[128,384]{1,0:T(8,128)(2,1)S(1)} %get-tuple-element.49), channel_id=1, source_target_pairs={{0,19},{1,16},{2,17},{3,18},{16,3},{17,0},{18,1},{19,2},{4,23},{5,... | collective-permute-start | bytes 294920 | tf_op jit(solution)/shard_map/ppermute | solution.py:424
  72.8 12.6 %collective-permute-start.13 = (bf16[128,384]{1,0:T(8,128)(2,1)S(1)}, bf16[128,384]{1,0:T(8,128)(2,1)S(1)}, u32[]{:S(2)}, u32[]{:S(2)}) collective-permute-start(bf16[128,384]{1,0:T(8,128)(2,1)S(1)} %get-tuple-element.50), channel_id=1, source_target_pairs={{0,1},{1,2},{2,3},{3,0},{16,17},{17,18},{18,19},{19,16},{4,5},{5,6... | collective-permute-start | bytes 294920 | tf_op jit(solution)/shard_map/ppermute | solution.py:424
  74.4 10.9 %collective-permute-start.14 = (bf16[128,384]{1,0:T(8,128)(2,1)S(1)}, bf16[128,384]{1,0:T(8,128)(2,1)S(1)}, u32[]{:S(2)}, u32[]{:S(2)}) collective-permute-start(bf16[128,384]{1,0:T(8,128)(2,1)S(1)} %get-tuple-element.51), channel_id=1, source_target_pairs={{0,17},{1,18},{2,19},{3,16},{16,1},{17,2},{18,3},{19,0},{4,21},{5,... | collective-permute-start | bytes 294920 | tf_op jit(solution)/shard_map/ppermute | solution.py:424
  75.9 9.5 %collective-permute-start.10 = (bf16[128,384]{1,0:T(8,128)(2,1)S(1)}, bf16[128,384]{1,0:T(8,128)(2,1)S(1)}, u32[]{:S(2)}, u32[]{:S(2)}) collective-permute-start(bf16[128,384]{1,0:T(8,128)(2,1)S(1)} %get-tuple-element.47), channel_id=1, source_target_pairs={{0,16},{1,17},{2,18},{3,19},{16,0},{17,1},{18,2},{19,3},{4,20},{5,... | collective-permute-start | bytes 294920 | tf_op jit(solution)/shard_map/ppermute | solution.py:424
  77.4 10.9 %collective-permute-start.16 = (bf16[128,384]{1,0:T(8,128)(2,1)S(1)}, bf16[128,384]{1,0:T(8,128)(2,1)S(1)}, u32[]{:S(2)}, u32[]{:S(2)}) collective-permute-start(bf16[128,384]{1,0:T(8,128)(2,1)S(1)} %get-tuple-element.54), channel_id=1, source_target_pairs={{0,2},{1,3},{2,0},{3,1},{16,18},{17,19},{18,16},{19,17},{4,6},{5,7... | collective-permute-start | bytes 294920 | tf_op jit(solution)/shard_map/ppermute | solution.py:424
  80.0 10.7 %collective-permute-start.15 = (bf16[128,384]{1,0:T(8,128)(2,1)S(1)}, bf16[128,384]{1,0:T(8,128)(2,1)S(1)}, u32[]{:S(2)}, u32[]{:S(2)}) collective-permute-start(bf16[128,384]{1,0:T(8,128)(2,1)S(1)} %get-tuple-element.53), channel_id=1, source_target_pairs={{0,18},{1,19},{2,16},{3,17},{16,2},{17,3},{18,0},{19,1},{4,22},{5,... | collective-permute-start | bytes 294920 | tf_op jit(solution)/shard_map/ppermute | solution.py:424
  85.4 2.9 %copy-start.4 = (f32[8,3,3072]{2,0,1:T(8,128)S(1)}, f32[8,3,3072]{2,0,1:T(8,128)}, u32[]{:S(2)}) copy-start(f32[8,3,3072]{2,0,1:T(8,128)} %param.27) | copy-start | bytes 884740
  (9 other events, 17.4 us)

commit v5 on v4

--- a/solution.py
+++ b/solution.py
@@ -404,7 +404,7 @@
     kv_far = text_kv("text_kv_far", text_far)
     mate_far = partner(kv_far, "group")
     mixed = {}
-    for name, steps in (("text_attention_far", order[1:-1]), ("text_attention_rest", [order[-1], order[0]])):
+    for name, steps in (("text_attention_far", order[1:2]), ("text_attention_rest", [*order[2:], order[0]])):
         out = call(
             functools.partial(last_body, (n_mp - 2,), shard, n_mp, steps), name, scalars, (1,),
             [VMEM] * 4, [VMEM] * (2 * len(steps)),

time: 93.9 us -> 95 us (1.012)
  waiting for transfers between devices: 15.5 us -> 26 us
  Pallas kernels: 44.6 us -> 39.5 us
  starting transfers between devices: 25.7 us -> 21.4 us
    ppermute x7, waiting for transfers between devices: 0.67 us -> 7.19 us  [send(): return lax.ppermute(mixed[s, flip], ('cfg', 'mp'), pairs)]
    pallas_call x14, Pallas kernels: 44.6 us -> 39.5 us  [call(): pl.pallas_call(body, name=name, grid_spec=pltpu.PrefetchScalarGridSpec(nu...]
    ppermute x7, starting transfers between devices: 14.5 us -> 10.2 us  [send(): return lax.ppermute(mixed[s, flip], ('cfg', 'mp'), pairs)]
    ppermute x6, waiting for transfers between devices: 13.4 us -> 17.4 us  [ring(): return lax.ppermute(value, 'mp', [(i, (i + step) % n) for i in range(n)])]
  transfers between devices with their start and end apart: 17 -> 17, of which waited for: 5 -> 8; matrix products, arithmetic and copies ran while one was open for 0% -> 0% of each run, Pallas kernels for 41% -> 35%
where the time goes in v5:
time: 95 us; the launch traced here: 94.6 us
  Pallas kernels  39.5 us (42%)
  waiting for transfers between devices  26 us (27%)
  starting transfers between devices  21.4 us (23%)
  local copies, waits for them, and re-layouts  5.82 us (6%)
  between operations  0.99 us (1%)
    pallas_call x14, Pallas kernels, call(): pl.pallas_call(body, name=name, grid_spec=pltpu.PrefetchScalarGridSpec(nu...  39.5 us
    ppermute x6, waiting for transfers between devices, ring(): return lax.ppermute(value, 'mp', [(i, (i + step) % n) for i in range(n)])  17.4 us
    ppermute x6, starting transfers between devices, ring(): return lax.ppermute(value, 'mp', [(i, (i + step) % n) for i in range(n)])  10.5 us
    ppermute x7, starting transfers between devices, send(): return lax.ppermute(mixed[s, flip], ('cfg', 'mp'), pairs)  10.2 us
    ppermute x7, waiting for transfers between devices, send(): return lax.ppermute(mixed[s, flip], ('cfg', 'mp'), pairs)  7.19 us
    unnamed x48, local copies, waits for them, and re-layouts  5.73 us
  transfers between devices with their start and end apart: 17, of which 8 were waited for; matrix products, arithmetic and copies ran while one was open for 0% of the time, Pallas kernels for 35%

profile of v5, /device:TPU:0, one launch (start us, length us, event | category | flops | bytes accessed | tf_op | source)
XLA Modules:
  0.0 94.6 jit_solution(6744823733745691675)
XLA Ops:
  1.5 5.0 %collective-permute-start.2 = (bf16[64,256]{1,0:T(8,128)(2,1)S(1)}, bf16[64,256]{1,0:T(8,128)(2,1)S(1)}, u32[]{:S(2)}, u32[]{:S(2)}) collective-permute-start(bf16[64,256]{1,0:T(8,128)(2,1)S(1)} %bitcast_convert_fusion.refs_0_), channel_id=1, source_target_pairs={{0,3},{1,0},{2,1},{3,2},{4,7},{5,4},{6,5},{7,6},{8,11},{9,8},{10,9... | collective-permute-start | bytes 98312 | tf_op jit(solution)/shard_map/ppermute | solution.py:22
  6.5 1.0 %collective-permute-start = (bf16[64,256]{1,0:T(8,128)(2,1)S(1)}, bf16[64,256]{1,0:T(8,128)(2,1)S(1)}, u32[]{:S(2)}, u32[]{:S(2)}) collective-permute-start(bf16[64,256]{1,0:T(8,128)(2,1)S(1)} %bitcast_convert_fusion.refs_0_), channel_id=1, source_target_pairs={{0,1},{1,2},{2,3},{3,0},{4,5},{5,6},{6,7},{7,4},{8,9},{9,10},{10,1... | collective-permute-start | bytes 98312 | tf_op jit(solution)/shard_map/ppermute | solution.py:22
  7.5 2.5 %collective-permute-start.4 = (bf16[128,3072]{1,0:T(8,128)(2,1)}, bf16[128,3072]{1,0:T(8,128)(2,1)S(1)}, u32[]{:S(2)}, u32[]{:S(2)}) collective-permute-start(bf16[128,3072]{1,0:T(8,128)(2,1)} %bitcast.21), channel_id=1, source_target_pairs={{0,1},{1,2},{2,3},{3,0},{4,5},{5,6},{6,7},{7,4},{8,9},{9,10},{10,1... | collective-permute-start | bytes 2359304 | tf_op jit(solution)/shard_map/ppermute | solution.py:22
  10.1 3.0 %copy-done = bf16[3072,1152]{1,0:T(8,128)(2,1)S(1)} copy-done((bf16[3072,1152]{1,0:T(8,128)(2,1)S(1)}, bf16[3072,1152]{1,0:T(8,128)(2,1)}, u32[]{:S(2)}) %copy-start) | copy-done | bytes 7077912
  13.1 1.0 %copy-done.1 = bf16[64,3072]{1,0:T(8,128)(2,1)S(1)} copy-done((bf16[64,3072]{1,0:T(8,128)(2,1)S(1)}, bf16[64,3072]{1,0:T(8,128)(2,1)}, u32[]{:S(2)}) %copy-start.1) | copy-done | bytes 393240
  14.1 1.0 %copy-done.3 = f32[8,3,3072]{2,0,1:T(8,128)S(1)} copy-done((f32[8,3,3072]{2,0,1:T(8,128)S(1)}, f32[8,3,3072]{2,0,1:T(8,128)}, u32[]{:S(2)}) %copy-start.3) | copy-done | bytes 294936
  15.8 5.4 %fold.1 = (bf16[3,2,192,384]{3,2,1,0:T(8,128)(2,1)S(1)}, f32[3,2,8,384]{3,2,1,0:T(8,128)S(1)}) custom-call(s32[7]{0:T(128)S(1)} %stack.15.ids, s32[4]{0:T(128)S(1)} %copy-done.10, bf16[64,3072]{1,0:T(8,128)(2,1)S(1)} %copy-done.1, f32[3,8,3072]{2,1,0:T(8,128)S(1)} %bitcast.16, bf16[3072,1152]{1,0:T(8,128)(2,1)S(1)} %copy-done), custom_call_target="tpu_custom_call" | custom-call | flops 1925185536 | bytes 7077888 | tf_op jit(solution)/shard_map/fold/pallas_call | solution.py:54
  21.2 6.1 %collective-permute-done.1.refs_2_ = bf16[64,256]{1,0:T(8,128)(2,1)S(1)} collective-permute-done((bf16[64,256]{1,0:T(8,128)(2,1)S(1)}, bf16[64,256]{1,0:T(8,128)(2,1)S(1)}, u32[]{:S(2)}, u32[]{:S(2)}) %collective-permute-start.1) | collective-permute-done | bytes 32800 | tf_op jit(solution)/shard_map/ppermute | solution.py:22
  27.3 3.5 %prep.1.lat_ref = bf16[1024,128]{1,0:T(8,128)(2,1)S(1)} custom-call(bf16[64,256]{1,0:T(8,128)(2,1)S(1)} %bitcast_convert_fusion.refs_0_, bf16[64,256]{1,0:T(8,128)(2,1)S(1)} %collective-permute-done.refs_1_, bf16[64,256]{1,0:T(8,128)(2,1)S(1)} %collective-permute-done.1.refs_2_, bf16[64,256]{1,0:T(8,128)(2,1)S(1)} %collective-permute-done.2.refs_3_, ...), custom_call_target="tpu_custom_call" | custom-call | tf_op jit(solution)/shard_map/prep/pallas_call | solution.py:54
  30.9 7.4 %image_own.1 = (bf16[3,1024,128]{2,1,0:T(8,128)(2,1)S(1)}, f32[3,1024,256]{2,1,0:T(8,128)S(1)}) custom-call(s32[7]{0:T(128)S(1)} %stack.15.ids, s32[4]{0:T(128)S(1)} %copy-done.14, bf16[1024,128]{1,0:T(8,128)(2,1)S(1)} %prep.1.lat_ref, bf16[3,2,192,384]{3,2,1,0:T(8,128)(2,1)S(1)} %get-tuple-element.35.mats_ref, ...), custom_call_target="tpu_custom_call" | custom-call | tf_op jit(solution)/shard_map/image_own/pallas_call | solution.py:54
  38.4 0.9 image_mate.1.acc_ref
  39.3 6.1 %collective-permute-done.3.refs_1_ = bf16[128,3072]{1,0:T(8,128)(2,1)S(1)} collective-permute-done((bf16[128,3072]{1,0:T(8,128)(2,1)S(1)}, bf16[128,3072]{1,0:T(8,128)(2,1)S(1)}, u32[]{:S(2)}, u32[]{:S(2)}) %collective-permute-start.3) | collective-permute-done | bytes 786464 | tf_op jit(solution)/shard_map/ppermute | solution.py:22
  45.4 1.9 %collective-permute-start.6 = (bf16[128,3072]{1,0:T(8,128)(2,1)S(1)}, bf16[128,3072]{1,0:T(8,128)(2,1)S(1)}, u32[]{:S(2)}, u32[]{:S(2)}) collective-permute-start(bf16[128,3072]{1,0:T(8,128)(2,1)S(1)} %collective-permute-done.3.refs_1_), channel_id=1, source_target_pairs={{0,3},{1,0},{2,1},{3,2},{4,7},{5,4},{6,5},{7,6},{8,11},{9,8},{10,9... | collective-permute-start | bytes 2359304 | tf_op jit(solution)/shard_map/ppermute | solution.py:22
  47.3 3.0 %text_kv_near.1.own1 = bf16[3,256,256]{2,1,0:T(8,128)(2,1)S(1)} custom-call(s32[7]{0:T(128)S(1)} %stack.15.ids, s32[4]{0:T(128)S(1)} %copy-done.11, bf16[128,3072]{1,0:T(8,128)(2,1)S(1)} %collective-permute-done.4.refs_0_, bf16[128,3072]{1,0:T(8,128)(2,1)S(1)} %collective-permute-done.3.refs_1_, f32[8,2,3072]{2,1,0:T(2,128)S(1)} %copy-done.5, ...), custom_call_target="tpu_custom_call" | custom-call | tf_op jit(solution)/shard_map/text_kv_near/pallas_call | solution.py:54
  50.4 1.9 %text_kv_own.1.own0 = bf16[3,128,256]{2,1,0:T(8,128)(2,1)S(1)} custom-call(s32[7]{0:T(128)S(1)} %stack.15.ids, s32[4]{0:T(128)S(1)} %copy-done.11, bf16[128,3072]{1,0:T(8,128)(2,1)S(1)} %bitcast.23, f32[8,2,3072]{2,1,0:T(2,128)S(1)} %copy-done.5, bf16[3072,768]{1,0:T(8,128)(2,1)S(1)} %bitcast.13, f32[1,128]{1,0:T(1,128)S(1)} %bitcast.29), custom_call_target="tpu_custom_call" | custom-call | flops 603979776 | bytes 4718592 | tf_op jit(solution)/shard_map/text_kv_own/pallas_call | solution.py:54
  52.9 1.6 %out_weights.1 = (bf16[1536,3072]{1,0:T(8,128)(2,1)S(1)}, f32[128,3072]{1,0:T(8,128)S(1)}) custom-call(s32[7]{0:T(128)S(1)} %stack.15.ids, bf16[1536,3072]{1,0:T(8,128)(2,1)S(1)} %bitcast.15, f32[64,256]{1,0:T(8,128)S(1)} %bitcast.24, bf16[64,3072]{1,0:T(8,128)(2,1)S(1)} %copy-done.2), custom_call_target="tpu_custom_call" | custom-call | tf_op jit(solution)/shard_map/out_weights/pallas_call | solution.py:54
  54.6 3.9 %text_attention_near.1.acc_ref = f32[3,1024,256]{2,1,0:T(8,128)S(1)} custom-call(s32[7]{0:T(128)S(1)} %stack.15.ids, s32[4]{0:T(128)S(1)} %copy-done.15, s32[2,4]{1,0:T(2,128)S(1)} %copy-done.12, bf16[3,1024,128]{2,1,0:T(8,128)(2,1)S(1)} %get-tuple-element.37.q_ref, f32[3,1024,256]{2,1,0:T(8,128)S(1)} %image_mate.1.acc_ref, ...), custom_call_target="tpu_custom_call" | custom-call | tf_op jit(solution)/shard_map/text_attention_near/pallas_call | solution.py:54
  58.5 5.2 %collective-permute-done.6.refs_0_ = bf16[128,3072]{1,0:T(8,128)(2,1)S(1)} collective-permute-done((bf16[128,3072]{1,0:T(8,128)(2,1)S(1)}, bf16[128,3072]{1,0:T(8,128)(2,1)S(1)}, u32[]{:S(2)}, u32[]{:S(2)}) %collective-permute-start.6) | collective-permute-done | bytes 786464 | tf_op jit(solution)/shard_map/ppermute | solution.py:22
  63.7 1.9 %text_kv_far.1.own_ref = bf16[3,128,256]{2,1,0:T(8,128)(2,1)S(1)} custom-call(s32[7]{0:T(128)S(1)} %stack.15.ids, s32[4]{0:T(128)S(1)} %copy-done.11, bf16[128,3072]{1,0:T(8,128)(2,1)S(1)} %collective-permute-done.6.refs_0_, f32[8,2,3072]{2,1,0:T(2,128)S(1)} %copy-done.5, bf16[3072,768]{1,0:T(8,128)(2,1)S(1)} %bitcast.13, f32[1,128]{1,0:T(1,128)S(1)} %bitcast.30), custom_call_target="tpu_custom_call" | custom-call | tf_op jit(solution)/shard_map/text_kv_far/pallas_call | solution.py:54
  65.7 1.4 %collective-permute-done.9.mate_ref = bf16[3,128,256]{2,1,0:T(8,128)(2,1)S(1)} collective-permute-done((bf16[3,128,256]{2,1,0:T(8,128)(2,1)S(1)}, bf16[3,128,256]{2,1,0:T(8,128)(2,1)S(1)}, u32[]{:S(2)}, u32[]{:S(2)}) %collective-permute-start.9) | collective-permute-done | bytes 196640 | tf_op jit(solution)/shard_map/ppermute | solution.py:27
  67.2 1.1 %text_attention_far.1 = (bf16[128,384]{1,0:T(8,128)(2,1)S(1)}, bf16[128,384]{1,0:T(8,128)(2,1)S(1)}) custom-call(s32[7]{0:T(128)S(1)} %stack.15.ids, s32[4]{0:T(128)S(1)} %copy-done.15, s32[2,4]{1,0:T(2,128)S(1)} %copy-done.12, bf16[3,1024,128]{2,1,0:T(8,128)(2,1)S(1)} %get-tuple-element.37.q_ref, f32[3,1024,256]{2,1,0:T(8,128)S(1)} %text_attention_near.1.acc_ref, ...), custom_call_target="tpu_custom_call" | custom-call | tf_op jit(solution)/shard_map/text_attention_far/pallas_call | solution.py:54
  68.2 2.8 %collective-permute-start.11 = (bf16[128,384]{1,0:T(8,128)(2,1)S(1)}, bf16[128,384]{1,0:T(8,128)(2,1)S(1)}, u32[]{:S(2)}, u32[]{:S(2)}) collective-permute-start(bf16[128,384]{1,0:T(8,128)(2,1)S(1)} %get-tuple-element.48), channel_id=1, source_target_pairs={{0,3},{1,0},{2,1},{3,2},{16,19},{17,16},{18,17},{19,18},{4,7},{5,4... | collective-permute-start | bytes 294920 | tf_op jit(solution)/shard_map/ppermute | solution.py:424
  71.0 1.0 %collective-permute-start.12 = (bf16[128,384]{1,0:T(8,128)(2,1)S(1)}, bf16[128,384]{1,0:T(8,128)(2,1)S(1)}, u32[]{:S(2)}, u32[]{:S(2)}) collective-permute-start(bf16[128,384]{1,0:T(8,128)(2,1)S(1)} %get-tuple-element.49), channel_id=1, source_target_pairs={{0,19},{1,16},{2,17},{3,18},{16,3},{17,0},{18,1},{19,2},{4,23},{5,... | collective-permute-start | bytes 294920 | tf_op jit(solution)/shard_map/ppermute | solution.py:424
  72.0 1.5 %text_attention_rest.1 = (bf16[128,384]{1,0:T(8,128)(2,1)S(1)}, bf16[128,384]{1,0:T(8,128)(2,1)S(1)}, bf16[128,384]{1,0:T(8,128)(2,1)S(1)}, bf16[128,384]{1,0:T(...) custom-call(s32[7]{0:T(128)S(1)} %stack.15.ids, s32[4]{0:T(128)S(1)} %copy-done.15, ...), custom_call_target="tpu_custom_call" | custom-call | tf_op jit(solution)/shard_map/text_attention_rest/pallas_call | solution.py:54
  74.1 2.0 %collective-permute-start.13 = (bf16[128,384]{1,0:T(8,128)(2,1)S(1)}, bf16[128,384]{1,0:T(8,128)(2,1)S(1)}, u32[]{:S(2)}, u32[]{:S(2)}) collective-permute-start(bf16[128,384]{1,0:T(8,128)(2,1)S(1)} %get-tuple-element.50), channel_id=1, source_target_pairs={{0,1},{1,2},{2,3},{3,0},{16,17},{17,18},{18,19},{19,16},{4,5},{5,6... | collective-permute-start | bytes 294920 | tf_op jit(solution)/shard_map/ppermute | solution.py:424
  76.0 1.0 %collective-permute-start.14 = (bf16[128,384]{1,0:T(8,128)(2,1)S(1)}, bf16[128,384]{1,0:T(8,128)(2,1)S(1)}, u32[]{:S(2)}, u32[]{:S(2)}) collective-permute-start(bf16[128,384]{1,0:T(8,128)(2,1)S(1)} %get-tuple-element.51), channel_id=1, source_target_pairs={{0,17},{1,18},{2,19},{3,16},{16,1},{17,2},{18,3},{19,0},{4,21},{5,... | collective-permute-start | bytes 294920 | tf_op jit(solution)/shard_map/ppermute | solution.py:424
  77.0 2.4 %collective-permute-start.16 = (bf16[128,384]{1,0:T(8,128)(2,1)S(1)}, bf16[128,384]{1,0:T(8,128)(2,1)S(1)}, u32[]{:S(2)}, u32[]{:S(2)}) collective-permute-start(bf16[128,384]{1,0:T(8,128)(2,1)S(1)} %get-tuple-element.54), channel_id=1, source_target_pairs={{0,2},{1,3},{2,0},{3,1},{16,18},{17,19},{18,16},{19,17},{4,6},{5,7... | collective-permute-start | bytes 294920 | tf_op jit(solution)/shard_map/ppermute | solution.py:424
  80.7 3.9 %collective-permute-done.14.refs_5_ = bf16[128,384]{1,0:T(8,128)(2,1)S(1)} collective-permute-done((bf16[128,384]{1,0:T(8,128)(2,1)S(1)}, bf16[128,384]{1,0:T(8,128)(2,1)S(1)}, u32[]{:S(2)}, u32[]{:S(2)}) %collective-permute-start.14) | collective-permute-done | bytes 98336 | tf_op jit(solution)/shard_map/ppermute | solution.py:424
  84.6 2.2 %out_early.1.refs_0_ = f32[256,3072]{1,0:T(8,128)S(1)} custom-call(bf16[128,384]{1,0:T(8,128)(2,1)S(1)} %get-tuple-element.46.refs_0_, bf16[128,384]{1,0:T(8,128)(2,1)S(1)} %collective-permute-done.10.refs_1_, bf16[128,384]{1,0:T(8,128)(2,1)S(1)} %collective-permute-done.11.refs_2_, bf16[128,384]{1,0:T(8,128)(2,1)S(1)} %collective-permute-done.12.refs_3_, ...), custom_call_target="tpu_custom_call" | custom-call | tf_op jit(solution)/shard_map/out_early/pallas_call | solution.py:54
  86.8 2.2 %collective-permute-done.16.refs_1_ = bf16[128,384]{1,0:T(8,128)(2,1)S(1)} collective-permute-done((bf16[128,384]{1,0:T(8,128)(2,1)S(1)}, bf16[128,384]{1,0:T(8,128)(2,1)S(1)}, u32[]{:S(2)}, u32[]{:S(2)}) %collective-permute-start.16) | collective-permute-done | bytes 98336 | tf_op jit(solution)/shard_map/ppermute | solution.py:424
  89.0 2.2 %out_own.1.refs_3_ = f32[64,128]{1,0:T(8,128)S(1)} custom-call(s32[7]{0:T(128)S(1)} %stack.15.ids, s32[4]{0:T(128)S(1)} %copy-done.11, f32[256,3072]{1,0:T(8,128)S(1)} %out_early.1.refs_0_, bf16[128,384]{1,0:T(8,128)(2,1)S(1)} %collective-permute-done.16.refs_1_, bf16[1536,3072]{1,0:T(8,128)(2,1)S(1)} %get-tuple-element.52.refs_6_.refs_2_, ...), custom_call_target="tpu_custom_call" | custom-call | tf_op jit(solution)/shard_map/out_own/pallas_call | solution.py:54
  91.6 2.9 %out_late.1 = (f32[1,64,128]{2,1,0:T(8,128)}, f32[1,64,128]{2,1,0:T(8,128)}) custom-call(s32[7]{0:T(128)S(1)} %stack.15.ids, s32[4]{0:T(128)S(1)} %copy-done.11, s32[4]{0:T(128)S(1)} %copy-done.14, f32[4]{0:T(128)S(1)} %copy-done.16, f32[8]{0:T(128)S(1)} %copy-done.17, f32[256,3072]{1,0:T(8,128)S(1)} %out_early.1.refs_0_, ...), custom_call_target="tpu_custom_call" | custom-call | tf_op jit(solution)/shard_map/out_late/pallas_call | solution.py:54
  (68 shorter events, 4.6 us)
Async XLA Ops:
  1.5 19.7 %collective-permute-start.2 = (bf16[64,256]{1,0:T(8,128)(2,1)S(1)}, bf16[64,256]{1,0:T(8,128)(2,1)S(1)}, u32[]{:S(2)}, u32[]{:S(2)}) collective-permute-start(bf16[64,256]{1,0:T(8,128)(2,1)S(1)} %bitcast_convert_fusion.refs_0_), channel_id=1, source_target_pairs={{0,3},{1,0},{2,1},{3,2},{4,7},{5,4},{6,5},{7,6},{8,11},{9,8},{10,9... | collective-permute-start | bytes 98312 | tf_op jit(solution)/shard_map/ppermute | solution.py:22
  6.5 20.8 %collective-permute-start.1 = (bf16[64,256]{1,0:T(8,128)(2,1)S(1)}, bf16[64,256]{1,0:T(8,128)(2,1)S(1)}, u32[]{:S(2)}, u32[]{:S(2)}) collective-permute-start(bf16[64,256]{1,0:T(8,128)(2,1)S(1)} %bitcast_convert_fusion.refs_0_), channel_id=1, source_target_pairs={{0,2},{1,3},{2,0},{3,1},{4,6},{5,7},{6,4},{7,5},{8,10},{9,11},{10,... | collective-permute-start | bytes 98312 | tf_op jit(solution)/shard_map/ppermute | solution.py:22
  6.5 20.8 %collective-permute-start = (bf16[64,256]{1,0:T(8,128)(2,1)S(1)}, bf16[64,256]{1,0:T(8,128)(2,1)S(1)}, u32[]{:S(2)}, u32[]{:S(2)}) collective-permute-start(bf16[64,256]{1,0:T(8,128)(2,1)S(1)} %bitcast_convert_fusion.refs_0_), channel_id=1, source_target_pairs={{0,1},{1,2},{2,3},{3,0},{4,5},{5,6},{6,7},{7,4},{8,9},{9,10},{10,1... | collective-permute-start | bytes 98312 | tf_op jit(solution)/shard_map/ppermute | solution.py:22
  7.5 31.8 %collective-permute-start.4 = (bf16[128,3072]{1,0:T(8,128)(2,1)}, bf16[128,3072]{1,0:T(8,128)(2,1)S(1)}, u32[]{:S(2)}, u32[]{:S(2)}) collective-permute-start(bf16[128,3072]{1,0:T(8,128)(2,1)} %bitcast.21), channel_id=1, source_target_pairs={{0,1},{1,2},{2,3},{3,0},{4,5},{5,6},{6,7},{7,4},{8,9},{9,10},{10,1... | collective-permute-start | bytes 2359304 | tf_op jit(solution)/shard_map/ppermute | solution.py:22
  15.7 11.6 %copy-start.8 = (bf16[1,128,3072]{2,1,0:T(8,128)(2,1)S(1)}, bf16[1,128,3072]{2,1,0:T(8,128)(2,1)}, u32[]{:S(2)}) copy-start(bf16[1,128,3072]{2,1,0:T(8,128)(2,1)} %param.19) | copy-start | bytes 2359300
  15.7 11.6 %copy-start.2 = (bf16[64,3072]{1,0:T(8,128)(2,1)S(1)}, bf16[64,3072]{1,0:T(8,128)(2,1)}, u32[]{:S(2)}) copy-start(bf16[64,3072]{1,0:T(8,128)(2,1)} %win_ref.3) | copy-start | bytes 1179652
  15.7 15.1 %copy-start.13 = (f32[128]{0:T(128)S(1)}, f32[128]{0:T(128)}, u32[]{:S(2)}) copy-start(f32[128]{0:T(128)} %param.24) | copy-start | bytes 1540
  15.7 15.2 %copy-start.14 = (s32[4]{0:T(128)S(1)}, s32[4]{0:T(128)}, u32[]{:S(2)}) copy-start(s32[4]{0:T(128)} %img_len.5) | copy-start | bytes 52
  15.7 15.2 %copy-start.18 = (f32[128]{0:T(128)S(1)}, f32[128]{0:T(128)}, u32[]{:S(2)}) copy-start(f32[128]{0:T(128)} %param.23) | copy-start | bytes 1540
  15.7 22.6 %copy-start.12 = (s32[2,4]{1,0:T(2,128)S(1)}, s32[2,4]{1,0:T(2,128)}, u32[]{:S(2)}) copy-start(s32[2,4]{1,0:T(2,128)} %flags.7) | copy-start | bytes 100
  27.3 18.1 %collective-permute-start.3 = (bf16[128,3072]{1,0:T(8,128)(2,1)S(1)}, bf16[128,3072]{1,0:T(8,128)(2,1)S(1)}, u32[]{:S(2)}, u32[]{:S(2)}) collective-permute-start(bf16[128,3072]{1,0:T(8,128)(2,1)S(1)} %bitcast.22), channel_id=1, source_target_pairs={{0,3},{1,0},{2,1},{3,2},{4,7},{5,4},{6,5},{7,6},{8,11},{9,8},{10,9... | collective-permute-start | bytes 2359304 | tf_op jit(solution)/shard_map/ppermute | solution.py:22
  30.8 7.5 %collective-permute-start.5 = (bf16[1024,128]{1,0:T(8,128)(2,1)S(1)}, bf16[1024,128]{1,0:T(8,128)(2,1)S(1)}, u32[]{:S(2)}, u32[]{:S(2)}) collective-permute-start(bf16[1024,128]{1,0:T(8,128)(2,1)S(1)} %prep.1.lat_ref), channel_id=1, source_target_pairs={{0,4},{4,0},{8,12},{12,8},{1,5},{5,1},{9,13},{13,9},{2,6},{6,2},{1... | collective-permute-start | bytes 786440 | tf_op jit(solution)/shard_map/ppermute | solution.py:27
  30.9 16.4 %slice-start = ((s8[4718592]{0:T(1024)(128)(4,1)}), s8[4194304]{0:T(1024)(128)(4,1)S(1)}, s32[]{:S(2)}) async-start(s8[4718592]{0:T(1024)(128)(4,1)} %bitcast.12), calls=%async_computation | async-start | bytes 8388608
  30.9 16.4 %copy-start.5 = (f32[8,2,3072]{2,1,0:T(2,128)S(1)}, f32[8,2,3072]{2,1,0:T(2,128)}, u32[]{:S(2)}) copy-start(f32[8,2,3072]{2,1,0:T(2,128)} %refs_1_.3) | copy-start | bytes 589828
  30.9 16.4 %copy-start.11 = (s32[4]{0:T(128)S(1)}, s32[4]{0:T(128)}, u32[]{:S(2)}) copy-start(s32[4]{0:T(128)} %tstep.11) | copy-start | bytes 52
  38.4 8.9 %slice-start.1 = ((s8[4718592]{0:T(1024)(128)(4,1)}), s8[524288]{0:T(1024)(128)(4,1)S(1)}, s32[]{:S(2)}) async-start(s8[4718592]{0:T(1024)(128)(4,1)} %bitcast.12), calls=%async_computation.1 | async-start | bytes 1048576
  38.4 14.5 %slice-start.2 = ((s8[9437184]{0:T(1024)(128)(4,1)}), s8[4194304]{0:T(1024)(128)(4,1)S(1)}, s32[]{:S(2)}) async-start(s8[9437184]{0:T(1024)(128)(4,1)} %bitcast.14), calls=%async_computation.2 | async-start | bytes 8388608
  38.4 14.5 %slice-start.3 = ((s8[9437184]{0:T(1024)(128)(4,1)}), s8[4194304]{0:T(1024)(128)(4,1)S(1)}, s32[]{:S(2)}) async-start(s8[9437184]{0:T(1024)(128)(4,1)} %bitcast.14), calls=%async_computation.3 | async-start | bytes 8388608
  39.3 13.6 %slice-start.4 = ((s8[9437184]{0:T(1024)(128)(4,1)}), s8[1048576]{0:T(1024)(128)(4,1)S(1)}, s32[]{:S(2)}) async-start(s8[9437184]{0:T(1024)(128)(4,1)} %bitcast.14), calls=%async_computation.4 | async-start | bytes 2097152
  45.4 18.3 %collective-permute-start.6 = (bf16[128,3072]{1,0:T(8,128)(2,1)S(1)}, bf16[128,3072]{1,0:T(8,128)(2,1)S(1)}, u32[]{:S(2)}, u32[]{:S(2)}) collective-permute-start(bf16[128,3072]{1,0:T(8,128)(2,1)S(1)} %collective-permute-done.3.refs_1_), channel_id=1, source_target_pairs={{0,3},{1,0},{2,1},{3,2},{4,7},{5,4},{6,5},{7,6},{8,11},{9,8},{10,9... | collective-permute-start | bytes 2359304 | tf_op jit(solution)/shard_map/ppermute | solution.py:22
  50.3 4.3 %collective-permute-start.8 = (bf16[3,256,256]{2,1,0:T(8,128)(2,1)S(1)}, bf16[3,256,256]{2,1,0:T(8,128)(2,1)S(1)}, u32[]{:S(2)}, u32[]{:S(2)}) collective-permute-start(bf16[3,256,256]{2,1,0:T(8,128)(2,1)S(1)} %text_kv_near.1.own1), channel_id=1, source_target_pairs={{0,4},{4,0},{8,12},{12,8},{1,5},{5,1},{9,13},{13,9},{2,6},{6,2},{1... | collective-permute-start | bytes 1179656 | tf_op jit(solution)/shard_map/ppermute | solution.py:27
  52.4 2.2 %collective-permute-start.7 = (bf16[3,128,256]{2,1,0:T(8,128)(2,1)S(1)}, bf16[3,128,256]{2,1,0:T(8,128)(2,1)S(1)}, u32[]{:S(2)}, u32[]{:S(2)}) collective-permute-start(bf16[3,128,256]{2,1,0:T(8,128)(2,1)S(1)} %text_kv_own.1.own0), channel_id=1, source_target_pairs={{0,4},{4,0},{8,12},{12,8},{1,5},{5,1},{9,13},{13,9},{2,6},{6,2},{1... | collective-permute-start | bytes 589832 | tf_op jit(solution)/shard_map/ppermute | solution.py:27
  65.7 1.5 %collective-permute-start.9 = (bf16[3,128,256]{2,1,0:T(8,128)(2,1)S(1)}, bf16[3,128,256]{2,1,0:T(8,128)(2,1)S(1)}, u32[]{:S(2)}, u32[]{:S(2)}) collective-permute-start(bf16[3,128,256]{2,1,0:T(8,128)(2,1)S(1)} %text_kv_far.1.own_ref), channel_id=1, source_target_pairs={{0,4},{4,0},{8,12},{12,8},{1,5},{5,1},{9,13},{13,9},{2,6},{6,2},{1... | collective-permute-start | bytes 589832 | tf_op jit(solution)/shard_map/ppermute | solution.py:27
  68.2 8.7 %collective-permute-start.11 = (bf16[128,384]{1,0:T(8,128)(2,1)S(1)}, bf16[128,384]{1,0:T(8,128)(2,1)S(1)}, u32[]{:S(2)}, u32[]{:S(2)}) collective-permute-start(bf16[128,384]{1,0:T(8,128)(2,1)S(1)} %get-tuple-element.48), channel_id=1, source_target_pairs={{0,3},{1,0},{2,1},{3,2},{16,19},{17,16},{18,17},{19,18},{4,7},{5,4... | collective-permute-start | bytes 294920 | tf_op jit(solution)/shard_map/ppermute | solution.py:424
  71.0 8.4 %collective-permute-start.12 = (bf16[128,384]{1,0:T(8,128)(2,1)S(1)}, bf16[128,384]{1,0:T(8,128)(2,1)S(1)}, u32[]{:S(2)}, u32[]{:S(2)}) collective-permute-start(bf16[128,384]{1,0:T(8,128)(2,1)S(1)} %get-tuple-element.49), channel_id=1, source_target_pairs={{0,19},{1,16},{2,17},{3,18},{16,3},{17,0},{18,1},{19,2},{4,23},{5,... | collective-permute-start | bytes 294920 | tf_op jit(solution)/shard_map/ppermute | solution.py:424
  73.5 6.4 %collective-permute-start.10 = (bf16[128,384]{1,0:T(8,128)(2,1)S(1)}, bf16[128,384]{1,0:T(8,128)(2,1)S(1)}, u32[]{:S(2)}, u32[]{:S(2)}) collective-permute-start(bf16[128,384]{1,0:T(8,128)(2,1)S(1)} %get-tuple-element.47), channel_id=1, source_target_pairs={{0,16},{1,17},{2,18},{3,19},{16,0},{17,1},{18,2},{19,3},{4,20},{5,... | collective-permute-start | bytes 294920 | tf_op jit(solution)/shard_map/ppermute | solution.py:424
  74.1 6.6 %collective-permute-start.13 = (bf16[128,384]{1,0:T(8,128)(2,1)S(1)}, bf16[128,384]{1,0:T(8,128)(2,1)S(1)}, u32[]{:S(2)}, u32[]{:S(2)}) collective-permute-start(bf16[128,384]{1,0:T(8,128)(2,1)S(1)} %get-tuple-element.50), channel_id=1, source_target_pairs={{0,1},{1,2},{2,3},{3,0},{16,17},{17,18},{18,19},{19,16},{4,5},{5,6... | collective-permute-start | bytes 294920 | tf_op jit(solution)/shard_map/ppermute | solution.py:424
  76.0 8.6 %collective-permute-start.14 = (bf16[128,384]{1,0:T(8,128)(2,1)S(1)}, bf16[128,384]{1,0:T(8,128)(2,1)S(1)}, u32[]{:S(2)}, u32[]{:S(2)}) collective-permute-start(bf16[128,384]{1,0:T(8,128)(2,1)S(1)} %get-tuple-element.51), channel_id=1, source_target_pairs={{0,17},{1,18},{2,19},{3,16},{16,1},{17,2},{18,3},{19,0},{4,21},{5,... | collective-permute-start | bytes 294920 | tf_op jit(solution)/shard_map/ppermute | solution.py:424
  77.0 12.0 %collective-permute-start.16 = (bf16[128,384]{1,0:T(8,128)(2,1)S(1)}, bf16[128,384]{1,0:T(8,128)(2,1)S(1)}, u32[]{:S(2)}, u32[]{:S(2)}) collective-permute-start(bf16[128,384]{1,0:T(8,128)(2,1)S(1)} %get-tuple-element.54), channel_id=1, source_target_pairs={{0,2},{1,3},{2,0},{3,1},{16,18},{17,19},{18,16},{19,17},{4,6},{5,7... | collective-permute-start | bytes 294920 | tf_op jit(solution)/shard_map/ppermute | solution.py:424
  79.4 12.2 %collective-permute-start.15 = (bf16[128,384]{1,0:T(8,128)(2,1)S(1)}, bf16[128,384]{1,0:T(8,128)(2,1)S(1)}, u32[]{:S(2)}, u32[]{:S(2)}) collective-permute-start(bf16[128,384]{1,0:T(8,128)(2,1)S(1)} %get-tuple-element.53), channel_id=1, source_target_pairs={{0,18},{1,19},{2,16},{3,17},{16,2},{17,3},{18,0},{19,1},{4,22},{5,... | collective-permute-start | bytes 294920 | tf_op jit(solution)/shard_map/ppermute | solution.py:424
  84.6 4.4 %copy-start.6 = (bf16[3072,64]{0,1:T(8,128)(2,1)S(1)}, bf16[3072,64]{0,1:T(8,128)(2,1)}, u32[]{:S(2)}) copy-start(bf16[3072,64]{0,1:T(8,128)(2,1)} %param.26) | copy-start | bytes 1179652
  84.6 4.4 %copy-start.7 = (f32[8,2,3072]{2,1,0:T(2,128)S(1)}, f32[8,2,3072]{2,1,0:T(2,128)}, u32[]{:S(2)}) copy-start(f32[8,2,3072]{2,1,0:T(2,128)} %refs_7_.1) | copy-start | bytes 589828
  (9 other events, 19.6 us)
